TPU v7x, 32 devices: a whole 2x2x4 slice. The times are simulated.
32 devices in a mesh: dp: 4 (over y, core), seq: 8 (over z, x).
Axes of the slice: x: 2, y: 2, z: 4, core: 2. Of those that a mesh axis runs over, the one named last changes fastest.
Arguments:
- tokens: bfloat16 [8, 1536, 1536], P('dp', 'seq'), may hold values from -6 to 6
- cotangent: bfloat16 [8, 1536, 1536], P('dp', 'seq'), may hold values from -6 to 6
- norm_gains: float32 [2, 1536], P(None, ('dp', 'seq')), may hold values from 0.5 to 1.5
- in_proj: float32 [1536, 4608], P(('dp', 'seq')), may hold values from -0.15625 to 0.15625
- conv_taps: float32 [3, 1536], P(None, ('dp', 'seq')), may hold values from -3 to 3
- out_proj: float32 [1536, 1536], P(('dp', 'seq')), may hold values from -0.15625 to 0.15625
- gate_up: float32 [2, 1536, 6912], P(None, ('dp', 'seq')), may hold values from -0.15625 to 0.15625
- down_proj: float32 [6912, 1536], P(('dp', 'seq')), may hold values from -0.078125 to 0.078125
- first_gains: float32 [2, 1536], P(None, ('dp', 'seq')), may hold values from -64 to 64
- first_in: float32 [1536, 4608], P(('dp', 'seq')), may hold values from -64 to 64
- first_conv: float32 [3, 1536], P(None, ('dp', 'seq')), may hold values from -64 to 64
- first_out: float32 [1536, 1536], P(('dp', 'seq')), may hold values from -64 to 64
- first_gate_up: float32 [2, 1536, 6912], P(None, ('dp', 'seq')), may hold values from -20 to 20
- first_down: float32 [6912, 1536], P(('dp', 'seq')), may hold values from -40 to 40
- second_gains: float32 [2, 1536], P(None, ('dp', 'seq')), may hold values from 651.264 to 2580.48
- second_in: float32 [1536, 4608], P(('dp', 'seq')), may hold values from 417.792 to 1658.88
- second_conv: float32 [3, 1536], P(None, ('dp', 'seq')), may hold values from 651.264 to 2580.48
- second_out: float32 [1536, 1536], P(('dp', 'seq')), may hold values from 528.384 to 2088.96
- second_gate_up: float32 [2, 1536, 6912], P(None, ('dp', 'seq')), may hold values from 57.7536 to 233.472
- second_down: float32 [6912, 1536], P(('dp', 'seq')), may hold values from 159.744 to 651.264
Outputs:
- block_out: bfloat16 [8, 1536, 1536], P('dp', 'seq')
- token_grad: float32 [8, 1536, 1536], P('dp', 'seq')
- grad_gains: float32 [2, 1536], P(None, ('dp', 'seq'))
- grad_in: float32 [1536, 4608], P(('dp', 'seq'))
- grad_conv: float32 [3, 1536], P(None, ('dp', 'seq'))
- grad_out: float32 [1536, 1536], P(('dp', 'seq'))
- grad_gate_up: float32 [2, 1536, 6912], P(None, ('dp', 'seq'))
- grad_down: float32 [6912, 1536], P(('dp', 'seq'))
- moment_gains: float32 [2, 1536], P(None, ('dp', 'seq'))
- moment_in: float32 [1536, 4608], P(('dp', 'seq'))
- moment_conv: float32 [3, 1536], P(None, ('dp', 'seq'))
- moment_out: float32 [1536, 1536], P(('dp', 'seq'))
- moment_gate_up: float32 [2, 1536, 6912], P(None, ('dp', 'seq'))
- moment_down: float32 [6912, 1536], P(('dp', 'seq'))
- updated_gains: float32 [2, 1536], P(None, ('dp', 'seq'))
- updated_in: float32 [1536, 4608], P(('dp', 'seq'))
- updated_conv: float32 [3, 1536], P(None, ('dp', 'seq'))
- updated_out: float32 [1536, 1536], P(('dp', 'seq'))
- updated_gate_up: float32 [2, 1536, 6912], P(None, ('dp', 'seq'))
- updated_down: float32 [6912, 1536], P(('dp', 'seq'))
All inputs are finite; a program needn't handle non-finite values.
Results may differ from a plain program's by a relative error of at most 0.012.
The roundings to bfloat16 on the way count: a program that leaves them out, or rounds other values in their place, can miss the bound.
Values may be sent and summed in bfloat16 or wider, within the bound.
A program may use at most 512 MiB of HBM per device.

v0:
```python
import jax
import jax.numpy as jnp
from jax import lax
from jax.sharding import PartitionSpec as P

STEP = 10


def passed_along(value, axis, by):
    peers = lax.axis_size(axis)
    pairs = [(i, i + by) for i in range(peers) if 0 <= i + by < peers]
    return lax.ppermute(value, axis, pairs)


def rms_parts(values):
    scale = lax.rsqrt(jnp.mean(values * values, axis=-1, keepdims=True) + 1e-05)
    return (values * scale, scale)


def rms_back(grad_hat, normal, scale):
    return scale * (grad_hat - normal * jnp.mean(grad_hat * normal, axis=-1, keepdims=True))


def times_t(left, right):
    return lax.dot_general(
        left, right, (((1,), (1,)), ((), ())), preferred_element_type=jnp.float32
    )


def t_times(left, right):
    return lax.dot_general(
        left, right, (((0,), (0,)), ((), ())), preferred_element_type=jnp.float32
    )


def adamw(weight, first_mom, second_mom, gradient, rate, decay):
    bias_one = 1.0 - 0.9**STEP
    bias_two = 1.0 - 0.95**STEP
    first_new = 0.9 * first_mom + 0.1 * gradient
    second_new = 0.95 * second_mom + 0.05 * gradient * gradient
    direction = first_new / bias_one / (jnp.sqrt(second_new / bias_two) + 1e-08)
    return (second_new, weight - rate * (direction + decay * weight))


def on_device(
    tokens,
    cotangent,
    norm_gains,
    in_proj,
    conv_taps,
    out_proj,
    gate_up,
    down_proj,
    first_gains,
    first_in,
    first_conv,
    first_out,
    first_gate_up,
    first_down,
    second_gains,
    second_in,
    second_conv,
    second_out,
    second_gate_up,
    second_down,
):
    bf16 = jnp.bfloat16
    f32 = jnp.float32
    seq_count, piece, width = tokens.shape
    row_count = seq_count * piece
    gathered = (
        lax.all_gather(norm_gains.astype(bf16), ("dp", "seq"), axis=1, tiled=True),
        lax.all_gather(in_proj.astype(bf16), ("dp", "seq"), axis=0, tiled=True),
        lax.all_gather(conv_taps.astype(bf16), ("dp", "seq"), axis=1, tiled=True),
        lax.all_gather(out_proj.astype(bf16), ("dp", "seq"), axis=0, tiled=True),
        lax.all_gather(gate_up.astype(bf16), ("dp", "seq"), axis=1, tiled=True),
        lax.all_gather(down_proj.astype(bf16), ("dp", "seq"), axis=0, tiled=True),
    )
    gains_full, in_full, taps_full, out_full, gu_full, down_full = gathered
    gain_one = gains_full[0].astype(f32)
    gain_two = gains_full[1].astype(f32)
    taps = taps_full.astype(f32)
    hidden = tokens.astype(f32).reshape(row_count, width)
    hat_one, scale_one = rms_parts(hidden)
    normed = (hat_one * gain_one).astype(bf16)
    projected = jnp.dot(normed, in_full, preferred_element_type=f32)
    b_part = projected[:, :width]
    c_part = projected[:, width : 2 * width]
    x_part = projected[:, 2 * width :]
    mixed_in = (b_part * x_part).reshape(seq_count, piece, width)
    arrived = passed_along(mixed_in[:, piece - 2 :, :], "seq", 1)
    extended = jnp.concatenate([arrived, mixed_in], axis=1)
    conv_out = (
        taps[0] * extended[:, :piece]
        + taps[1] * extended[:, 1 : piece + 1]
        + taps[2] * extended[:, 2:]
    )
    conv_out = conv_out.reshape(row_count, width)
    gated = (c_part * conv_out).astype(bf16)
    middle = hidden + jnp.dot(gated, out_full, preferred_element_type=f32)
    hat_two, scale_two = rms_parts(middle)
    normed_two = (hat_two * gain_two).astype(bf16)
    gate_val = jnp.dot(normed_two, gu_full[0], preferred_element_type=f32)
    up_val = jnp.dot(normed_two, gu_full[1], preferred_element_type=f32)
    sigma = jax.nn.sigmoid(gate_val)
    silu_val = gate_val * sigma
    active = (silu_val * up_val).astype(bf16)
    block_out = (middle + jnp.dot(active, down_full, preferred_element_type=f32)).astype(bf16)
    regathered = (
        lax.all_gather(norm_gains.astype(bf16), ("dp", "seq"), axis=1, tiled=True),
        lax.all_gather(in_proj.astype(bf16), ("dp", "seq"), axis=0, tiled=True),
        lax.all_gather(conv_taps.astype(bf16), ("dp", "seq"), axis=1, tiled=True),
        lax.all_gather(out_proj.astype(bf16), ("dp", "seq"), axis=0, tiled=True),
        lax.all_gather(gate_up.astype(bf16), ("dp", "seq"), axis=1, tiled=True),
        lax.all_gather(down_proj.astype(bf16), ("dp", "seq"), axis=0, tiled=True),
    )
    gains_back, in_back, taps_back, out_back, gu_back, down_back = regathered
    back_one = gains_back[0].astype(f32)
    back_two = gains_back[1].astype(f32)
    back_taps = taps_back.astype(f32)
    cot_low = cotangent.reshape(row_count, width)
    cot_full = cot_low.astype(f32)
    grad_down = t_times(active, cot_low)
    grad_act = times_t(cot_low, down_back)
    dgate = (grad_act * up_val * sigma * (1.0 + gate_val * (1.0 - sigma))).astype(bf16)
    dup = (grad_act * silu_val).astype(bf16)
    grad_gu = jnp.stack([t_times(normed_two, dgate), t_times(normed_two, dup)])
    dnorm_two = times_t(dgate, gu_back[0]) + times_t(dup, gu_back[1])
    gain_grad_two = jnp.sum(dnorm_two * hat_two, axis=0)
    dmiddle = cot_full + rms_back(dnorm_two * back_two, hat_two, scale_two)
    ffn_owned = (
        lax.psum_scatter(grad_gu, ("dp", "seq"), scatter_dimension=1, tiled=True),
        lax.psum_scatter(grad_down, ("dp", "seq"), scatter_dimension=0, tiled=True),
    )
    dmix = dmiddle.astype(bf16)
    grad_out = t_times(gated, dmix)
    dgated = times_t(dmix, out_back)
    dc_part = dgated * conv_out
    dconv = (dgated * c_part).reshape(seq_count, piece, width)
    grad_taps = jnp.stack(
        [
            jnp.sum(dconv * extended[:, :piece], axis=(0, 1)),
            jnp.sum(dconv * extended[:, 1 : piece + 1], axis=(0, 1)),
            jnp.sum(dconv * extended[:, 2:], axis=(0, 1)),
        ]
    )
    grad_ext = (
        back_taps[0] * jnp.pad(dconv, ((0, 0), (0, 2), (0, 0)))
        + back_taps[1] * jnp.pad(dconv, ((0, 0), (1, 1), (0, 0)))
        + back_taps[2] * jnp.pad(dconv, ((0, 0), (2, 0), (0, 0)))
    )
    returned = passed_along(grad_ext[:, :2, :], "seq", -1)
    grad_mixed = grad_ext[:, 2:, :] + jnp.pad(returned, ((0, 0), (piece - 2, 0), (0, 0)))
    grad_mixed = grad_mixed.reshape(row_count, width)
    dproj = jnp.concatenate([grad_mixed * x_part, dc_part, grad_mixed * b_part], axis=-1).astype(
        bf16
    )
    grad_in = t_times(normed, dproj)
    dnorm_one = times_t(dproj, in_back)
    gain_grad_one = jnp.sum(dnorm_one * hat_one, axis=0)
    token_grad = dmiddle + rms_back(dnorm_one * back_one, hat_one, scale_one)
    grad_gains = jnp.stack([gain_grad_one, gain_grad_two])
    mixer_owned = (
        lax.psum_scatter(grad_gains, ("dp", "seq"), scatter_dimension=1, tiled=True),
        lax.psum_scatter(grad_in, ("dp", "seq"), scatter_dimension=0, tiled=True),
        lax.psum_scatter(grad_taps, ("dp", "seq"), scatter_dimension=1, tiled=True),
        lax.psum_scatter(grad_out, ("dp", "seq"), scatter_dimension=0, tiled=True),
    )
    g_gains, g_in, g_conv, g_out = mixer_owned
    g_gu, g_down = ffn_owned
    m_gains, u_gains = adamw(norm_gains, first_gains, second_gains, g_gains, 0.4, 0.0)
    m_in, u_in = adamw(in_proj, first_in, second_in, g_in, 0.02, 0.1)
    m_conv, u_conv = adamw(conv_taps, first_conv, second_conv, g_conv, 0.2, 0.1)
    m_out, u_out = adamw(out_proj, first_out, second_out, g_out, 0.02, 0.1)
    m_gu, u_gu = adamw(gate_up, first_gate_up, second_gate_up, g_gu, 0.02, 0.1)
    m_down, u_down = adamw(down_proj, first_down, second_down, g_down, 0.01, 0.1)
    return (
        block_out.reshape(seq_count, piece, width),
        token_grad.reshape(seq_count, piece, width),
        g_gains,
        g_in,
        g_conv,
        g_out,
        g_gu,
        g_down,
        m_gains,
        m_in,
        m_conv,
        m_out,
        m_gu,
        m_down,
        u_gains,
        u_in,
        u_conv,
        u_out,
        u_gu,
        u_down,
    )


def solution(mesh):
    in_specs = (
        P("dp", "seq", None),
        P("dp", "seq", None),
        P(None, ("dp", "seq")),
        P(("dp", "seq"), None),
        P(None, ("dp", "seq")),
        P(("dp", "seq"), None),
        P(None, ("dp", "seq"), None),
        P(("dp", "seq"), None),
        P(None, ("dp", "seq")),
        P(("dp", "seq"), None),
        P(None, ("dp", "seq")),
        P(("dp", "seq"), None),
        P(None, ("dp", "seq"), None),
        P(("dp", "seq"), None),
        P(None, ("dp", "seq")),
        P(("dp", "seq"), None),
        P(None, ("dp", "seq")),
        P(("dp", "seq"), None),
        P(None, ("dp", "seq"), None),
        P(("dp", "seq"), None),
    )
    out_specs = (
        P("dp", "seq", None),
        P("dp", "seq", None),
        P(None, ("dp", "seq")),
        P(("dp", "seq"), None),
        P(None, ("dp", "seq")),
        P(("dp", "seq"), None),
        P(None, ("dp", "seq"), None),
        P(("dp", "seq"), None),
        P(None, ("dp", "seq")),
        P(("dp", "seq"), None),
        P(None, ("dp", "seq")),
        P(("dp", "seq"), None),
        P(None, ("dp", "seq"), None),
        P(("dp", "seq"), None),
        P(None, ("dp", "seq")),
        P(("dp", "seq"), None),
        P(None, ("dp", "seq")),
        P(("dp", "seq"), None),
        P(None, ("dp", "seq"), None),
        P(("dp", "seq"), None),
    )
    return jax.shard_map(
        on_device, mesh=mesh, in_specs=in_specs, out_specs=out_specs, check_vma=False
    )
```

profile of v0, /device:TPU:1, one launch (start us, length us, event | category | flops | bytes accessed | tf_op | source)
XLA Modules:
  0.0 2366.7 jit_solution(16570074619396498716)
XLA Ops:
  15.1 61.6 %all-gather = bf16[32,48,2]{1,2,0:T(2,128)(2,1)S(1)} all-gather(bf16[1,48,2]{1,2,0:T(2,128)(2,1)S(1)} %convert_bitcast_fusion.1), channel_id=1, replica_groups=mesh['dp'=4,'seq'=8] {'dp','seq'}, dimensions={0}, use_global_device_ids=true | all-gather | bytes 6336 | tf_op jit(solution)/shard_map/all_gather | solution.py:72
  77.3 63.0 %all-gather.1 = bf16[32,48,3]{1,2,0:T(4,128)(2,1)S(1)} all-gather(bf16[1,48,3]{1,2,0:T(4,128)(2,1)S(1)} %convert_bitcast_fusion), channel_id=1, replica_groups=mesh['dp'=4,'seq'=8] {'dp','seq'}, dimensions={0}, use_global_device_ids=true | all-gather | bytes 9504 | tf_op jit(solution)/shard_map/all_gather | solution.py:74
  143.6 9.0 fusion.34
  161.1 22.0 all-gather.9.cloned.1.call-done
  189.6 233.8 %all-gather.11.cloned.1.call-done = bf16[2,1536,6912]{2,1,0:T(8,128)(2,1)} async-done(((bf16[2,48,6912]{2,1,0:T(8,128)(2,1)}), bf16[2,1536,6912]{2,1,0:T(8,128)(2,1)}) %all-gather.11.cloned.1.call-update) | async-done | bytes 42467344 | tf_op jit(solution)/shard_map/all_gather | solution.py:76
  423.4 15.7 fusion.1
  439.1 15.3 fusion.3
  454.4 106.5 %all-gather.13.cloned.1.call-done = bf16[6912,1536]{1,0:T(8,128)(2,1)} async-done(((bf16[216,1536]{1,0:T(8,128)(2,1)}), bf16[6912,1536]{1,0:T(8,128)(2,1)}) %all-gather.13.cloned.1.call-update) | async-done | bytes 21233680 | tf_op jit(solution)/shard_map/all_gather | solution.py:77
  560.8 25.4 %multiply_convert_fusion = (bf16[384,6912]{1,0:T(8,128)(2,1)}, bf16[384,6912]{1,0:T(8,128)(2,1)}, bf16[384,6912]{1,0:T(8,128)(2,1)}) fusion(f32[384,6912]{1,0:T(8,128)} %fusion.1, f32[384,6912]{1,0:T(8,128)} %fusion.3, bf16[384,1536]{1,0:T(8,128)(2,1)} %bitcast.93, bf16[6912,1536]{1,0:T(8,128)(2,1)} %all-gather.13.cloned.1.call-done), kind=kOutput, calls=%fused_computation.9 | convolution fusion | flops 8193540096 | bytes 59572224 | tf_op jit(solution)/shard_map/dot_general | solution.py:25
  586.3 15.2 fusion
  601.4 17.0 multiply_reduce_fusion.3
  622.3 7.1 multiply_reduce_fusion
  641.4 14.1 multiply_reduce_fusion.4
  665.5 13.7 fusion.13
  680.5 20.7 fusion.35
  702.4 20.3 convolution_bitcast_fusion
  722.7 20.3 convolution_bitcast_fusion.1
  743.0 56.0 %pad_maximum_fusion = f32[2,1536,6912]{2,1,0:T(8,128)} fusion(f32[1,1536,6912]{2,1,0:T(8,128)} %convolution_bitcast_fusion, f32[1,1536,6912]{2,1,0:T(8,128)} %convolution_bitcast_fusion.1), kind=kLoop, calls=%fused_computation | loop fusion | flops 21233664 | bytes 169869312 | tf_op jit(solution)/shard_map/stack | solution.py:127
  799.1 15.7 fusion.6
  830.1 138.8 %reduce-scatter.13.cloned.1.call-done = f32[48,1536]{1,0:T(8,128)} async-done(((f32[1536,1536]{1,0:T(8,128)}), f32[48,1536]{1,0:T(8,128)}) %reduce-scatter.13.cloned.1.call-update) | async-done | bytes 294928 | tf_op jit(solution)/shard_map/reduce_scatter | solution.py:167
  971.2 270.3 %reduce-scatter.11.cloned.1.call-done = f32[48,4608]{1,0:T(8,128)} async-done(((f32[1536,4608]{1,0:T(8,128)}), f32[48,4608]{1,0:T(8,128)}) %reduce-scatter.11.cloned.1.call-update) | async-done | bytes 884752 | tf_op jit(solution)/shard_map/reduce_scatter | solution.py:165
  1244.8 382.4 %reduce-scatter.17.cloned.1.call-done = f32[216,1536]{1,0:T(8,128)} async-done(((f32[6912,1536]{1,0:T(8,128)}), f32[216,1536]{1,0:T(8,128)}) %reduce-scatter.17.cloned.1.call-update) | async-done | bytes 1327120 | tf_op jit(solution)/shard_map/reduce_scatter | solution.py:133
  1632.2 719.5 %reduce-scatter.15.cloned.1.call-done = f32[2,48,6912]{2,1,0:T(8,128)} async-done(((f32[2,1536,6912]{2,1,0:T(8,128)}), f32[2,48,6912]{2,1,0:T(8,128)}) %reduce-scatter.15.cloned.1.call-update) | async-done | bytes 2654224 | tf_op jit(solution)/shard_map/reduce_scatter | solution.py:132
  2351.7 7.7 multiply_subtract_fusion
  (162 shorter events, 80.5 us)
Async XLA Ops:
  7.2 135.4 %all-gather.7.cloned.1.call-start = ((), (), s32[]{:S(2)}) async-start(), calls=%async_computation.6 | async-start | bytes 14598144 | tf_op jit(solution)/shard_map/all_gather | solution.py:73
  9.2 173.8 %all-gather.9.cloned.1.call-start = ((), (), s32[]{:S(2)}) async-start(), calls=%async_computation.7 | async-start | bytes 4866048 | tf_op jit(solution)/shard_map/all_gather | solution.py:75
  11.0 412.4 %all-gather.11.cloned.1.call-start = ((), (), s32[]{:S(2)}) async-start(), calls=%async_computation.8 | async-start | bytes 43794432 | tf_op jit(solution)/shard_map/all_gather | solution.py:76
  14.1 62.8 %copy-start.8 = (bf16[2,192,1536]{2,1,0:T(8,128)(2,1)S(1)}, bf16[2,192,1536]{2,1,0:T(8,128)(2,1)}, u32[]{:S(2)}) copy-start(bf16[2,192,1536]{2,1,0:T(8,128)(2,1)} %param.20) | copy-start | bytes 3538948
  14.1 63.2 %copy-start.38 = (f32[3,48]{1,0:T(4,128)S(1)}, f32[3,48]{1,0:T(4,128)}, u32[]{:S(2)}) copy-start(f32[3,48]{1,0:T(4,128)} %param.24) | copy-start | bytes 1732
  14.1 546.8 %all-gather.13.cloned.1.call-start = ((), (), s32[]{:S(2)}) async-start(), calls=%async_computation.9 | async-start | bytes 21897216 | tf_op jit(solution)/shard_map/all_gather | solution.py:77
  15.1 799.8 %reduce-scatter.21.cloned.1.call-start = ((), (), s32[]{:S(2)}) async-start(), calls=%async_computation.15 | async-start | bytes 811008
  77.3 65.3 %copy-start.34 = (f32[384]{0:T(512)}, f32[384]{0:T(512)S(1)}, u32[]{:S(2)}) copy-start(f32[384]{0:T(512)S(1)} %rsqrt.20) | copy-start | bytes 4612
  153.0 4.5 collective-permute-start
  189.6 249.5 %copy-start.6 = (bf16[384,1536]{1,0:T(8,128)(2,1)}, bf16[384,1536]{1,0:T(8,128)(2,1)S(1)}, u32[]{:S(2)}) copy-start(bf16[384,1536]{1,0:T(8,128)(2,1)S(1)} %multiply_convert_fusion.3) | copy-start | bytes 3538948
  630.1 4.6 collective-permute-start.1
  634.0 194.0 %reduce-scatter.19.cloned.1.call-start = ((), (), s32[]{:S(2)}) async-start(), calls=%async_computation.14 | async-start | bytes 811008
  658.2 310.7 %reduce-scatter.13.cloned.1.call-start = ((), (), s32[]{:S(2)}) async-start(), calls=%async_computation.11 | async-start | bytes 9732096 | tf_op jit(solution)/shard_map/reduce_scatter | solution.py:167
  663.5 578.0 %reduce-scatter.11.cloned.1.call-start = ((), (), s32[]{:S(2)}) async-start(), calls=%async_computation.10 | async-start | bytes 29196288 | tf_op jit(solution)/shard_map/reduce_scatter | solution.py:165
  679.2 948.0 %reduce-scatter.17.cloned.1.call-start = ((), (), s32[]{:S(2)}) async-start(), calls=%async_computation.13 | async-start | bytes 43794432 | tf_op jit(solution)/shard_map/reduce_scatter | solution.py:133
  701.2 1650.5 %reduce-scatter.15.cloned.1.call-start = ((), (), s32[]{:S(2)}) async-start(), calls=%async_computation.12 | async-start | bytes 87588864 | tf_op jit(solution)/shard_map/reduce_scatter | solution.py:132
  799.0 19.2 copy-start.2
  799.1 19.2 copy-start.10
  799.1 19.2 copy-start.31
  799.1 19.2 copy-start.36
  822.0 419.5 %copy-start.22 = (f32[48,4608]{1,0:T(8,128)S(1)}, f32[48,4608]{1,0:T(8,128)}, u32[]{:S(2)}) copy-start(f32[48,4608]{1,0:T(8,128)} %param.23) | copy-start | bytes 2654212
  822.0 419.5 %copy-start.23 = (f32[48,4608]{1,0:T(8,128)S(1)}, f32[48,4608]{1,0:T(8,128)}, u32[]{:S(2)}) copy-start(f32[48,4608]{1,0:T(8,128)} %param.29) | copy-start | bytes 2654212
  828.9 416.0 %copy-start.40 = (f32[2,48]{1,0:T(2,128)}, f32[2,48]{1,0:T(2,128)S(1)}, u32[]{:S(2)}) copy-start(f32[2,48]{1,0:T(2,128)S(1)} %copy.47) | copy-start | bytes 1156
  1244.8 1106.9 %copy-start.11 = (f32[2,48,6912]{2,1,0:T(8,128)S(1)}, f32[2,48,6912]{2,1,0:T(8,128)}, u32[]{:S(2)}) copy-start(f32[2,48,6912]{2,1,0:T(8,128)} %param.26) | copy-start | bytes 7962628
  (31 other events, 137.8 us)
Sparse Core Ops, SparseCore 0:
  11.6 106.0 all-gather.6
  121.3 61.7 all-gather.8
  186.7 236.5 all-gather.10
  426.8 134.0 all-gather.12
  634.1 93.6 reduce-scatter.20
  733.4 94.5 reduce-scatter.18
  834.5 134.3 reduce-scatter.12
  977.1 264.3 reduce-scatter.10
  1249.6 377.5 reduce-scatter.16
  1634.1 717.5 reduce-scatter.14
where the time goes:
time: 2370 us
  waiting for transfers between devices  1880 us (79%)
  matrix products  219 us (9%)
  blocking collectives  125 us (5%)
  other arithmetic  105 us (4%)
    reduce_scatter x1, waiting for transfers between devices, on_device(): lax.psum_scatter(grad_gu, ('dp', 'seq'), scatter_dimension=1, tiled=True)  719 us
    reduce_scatter x1, waiting for transfers between devices, on_device(): lax.psum_scatter(grad_down, ('dp', 'seq'), scatter_dimension=0, tiled=True)  382 us
    reduce_scatter x1, waiting for transfers between devices, on_device(): lax.psum_scatter(grad_in, ('dp', 'seq'), scatter_dimension=0, tiled=True)  270 us
    all_gather x1, waiting for transfers between devices, on_device(): lax.all_gather(gate_up.astype(bf16), ('dp', 'seq'), axis=1, tiled=True)  234 us
    reduce_scatter x1, waiting for transfers between devices, on_device(): lax.psum_scatter(grad_out, ('dp', 'seq'), scatter_dimension=0, tiled=True)  139 us
    all_gather x1, waiting for transfers between devices, on_device(): lax.all_gather(down_proj.astype(bf16), ('dp', 'seq'), axis=0, tiled=True)  106 us
    dot_general x5, matrix products, t_times(): lax.dot_general(left, right, (((0,), (0,)), ((), ())), preferred_element_...  80.1 us
    dot_general x5, matrix products, times_t(): lax.dot_general(left, right, (((1,), (1,)), ((), ())), preferred_element_...  78.8 us
  transfers between devices with their start and end apart: 12, of which 10 were waited for; matrix products, arithmetic and copies ran while one was open for 11% of the time, Pallas kernels for 0%

commit v1 on v0

v1 whole, which is shorter than its diff:
```python
import functools

import jax
import jax.numpy as jnp
from jax import lax
from jax.experimental import pallas as pl
from jax.experimental.pallas import tpu as pltpu
from jax.sharding import Mesh
from jax.sharding import PartitionSpec as P

STEP = 10
MESH = pl.DeviceIdType.MESH
BF16 = jnp.bfloat16
F32 = jnp.float32
FLIPS = [(dy, dc, dx) for dy in (0, 1) for dc in (0, 1) for dx in (0, 1)][1:]
ANY = pl.BlockSpec(memory_space=pl.ANY)
VMEM = pl.BlockSpec(memory_space=pltpu.VMEM)


def place():
    return tuple(lax.axis_index(a) for a in ("y", "core", "z", "x"))


def flip(value, by):
    return 1 - value if by else value


def remote(src, dst, send, recv, device):
    return pltpu.make_async_remote_copy(
        src_ref=src,
        dst_ref=dst,
        send_sem=send,
        recv_sem=recv,
        device_id=device,
        device_id_type=MESH,
    )


def meet(peers):
    barrier = pltpu.get_barrier_semaphore()
    for peer in peers:
        pl.semaphore_signal(barrier, inc=1, device_id=peer, device_id_type=MESH)
    pl.semaphore_wait(barrier, len(peers))


class Gather:
    def __init__(self, own, full, send, recv):
        self.own, self.full, self.send, self.recv = own, full, send, recv
        self.started = []

    def go(self, src, slot, sem, device):
        seq, x = slot
        copy = remote(src, self.full.at[seq, x], self.send.at[sem], self.recv.at[sem], device)
        copy.start()
        self.started.append(copy)

    def first(self):
        y, c, _, x = place()
        for i, j in ((0, 1), (1, 0)):
            self.go(self.own.at[i], ((y * 2 + c) * 2 + i, x), i, {"x": 1 - x})
            self.go(self.own.at[j], ((y * 2 + c) * 2 + j, x), 2 + j, {"y": 1 - y})
        for i in (0, 1):
            self.go(self.own.at[i], ((y * 2 + c) * 2 + i, x), 6 + i, {"core": 1 - c})

    def arrived(self, sem):
        pltpu.make_async_copy(self.own.at[0], self.own.at[0], self.recv.at[sem]).wait()

    def rest(self):
        y, c, _, x = place()
        from_x = [((y * 2 + c) * 2 + i, 1 - x) for i in (0, 1)]
        from_y = [(((1 - y) * 2 + c) * 2 + i, x) for i in (0, 1)]
        from_d = [(((1 - y) * 2 + c) * 2 + i, 1 - x) for i in (0, 1)]

        def pass_on(slot, sem, device):
            self.go(self.full.at[slot[0], slot[1]], slot, sem, device)

        self.arrived(0)
        pass_on(from_x[0], 4, {"y": 1 - y})
        pass_on(from_x[0], 8, {"core": 1 - c})
        self.arrived(3)
        pass_on(from_y[1], 5, {"x": 1 - x})
        pass_on(from_y[1], 11, {"core": 1 - c})
        self.arrived(1)
        pass_on(from_x[1], 9, {"core": 1 - c})
        self.arrived(2)
        pass_on(from_y[0], 10, {"core": 1 - c})
        self.arrived(4)
        pass_on(from_d[0], 12, {"core": 1 - c})
        self.arrived(5)
        pass_on(from_d[1], 13, {"core": 1 - c})
        for sem in range(6, 14):
            self.arrived(sem)
        for copy in self.started:
            copy.wait_send()


def neighbours():
    y, c, _, x = place()
    return [{"x": 1 - x}, {"y": 1 - y}, {"core": 1 - c}]


def gather_kernel(own, full, send, recv, local):
    y, c, _, x = place()
    meet(neighbours())
    gather = Gather(own, full, send, recv)
    gather.first()
    copies = []
    for i in (0, 1):
        copy = pltpu.make_async_copy(own.at[i], full.at[(y * 2 + c) * 2 + i, x], local.at[i])
        copy.start()
        copies.append(copy)
    gather.rest()
    for copy in copies:
        copy.wait()


def plane_gather(own, collective_id):
    seqs, piece, width = own.shape
    size = 8 * seqs * piece * width * 2
    return pl.pallas_call(
        gather_kernel,
        out_shape=jax.ShapeDtypeStruct((4 * seqs, 2, piece, width), own.dtype),
        in_specs=[ANY],
        out_specs=ANY,
        scratch_shapes=[
            pltpu.SemaphoreType.DMA((14,)),
            pltpu.SemaphoreType.DMA((14,)),
            pltpu.SemaphoreType.DMA((2,)),
        ],
        cost_estimate=pl.CostEstimate(flops=0, bytes_accessed=10 * size, transcendentals=0),
        compiler_params=pltpu.CompilerParams(collective_id=collective_id, has_side_effects=True),
    )(own)


def swap_kernel(count, *refs):
    srcs, dsts, (send, recv, local) = refs[:count], refs[count : 2 * count], refs[2 * count :]
    y, c, _, x = place()
    meet([{"y": flip(y, dy), "core": flip(c, dc), "x": flip(x, dx)} for dy, dc, dx in FLIPS])
    me = (y * 2 + c) * 2 + x
    copies = []
    for k, (src, dst) in enumerate(zip(srcs, dsts)):
        for f, (dy, dc, dx) in enumerate(FLIPS):
            peer = {"y": flip(y, dy), "core": flip(c, dc), "x": flip(x, dx)}
            to = (peer["y"] * 2 + peer["core"]) * 2 + peer["x"]
            copy = remote(src.at[to], dst.at[me], send.at[k, f], recv.at[k, f], peer)
            copy.start()
            copies.append(copy)
        copy = pltpu.make_async_copy(src.at[me], dst.at[me], local.at[k])
        copy.start()
        copies.append(copy)
    for copy in copies:
        copy.wait()


def plane_swap(arrays, collective_id):
    count = len(arrays)
    size = sum(a.size * a.dtype.itemsize for a in arrays)
    return pl.pallas_call(
        functools.partial(swap_kernel, count),
        out_shape=[jax.ShapeDtypeStruct(a.shape, a.dtype) for a in arrays],
        in_specs=[ANY] * count,
        out_specs=[ANY] * count,
        scratch_shapes=[
            pltpu.SemaphoreType.DMA((count, 7)),
            pltpu.SemaphoreType.DMA((count, 7)),
            pltpu.SemaphoreType.DMA((count,)),
        ],
        cost_estimate=pl.CostEstimate(flops=0, bytes_accessed=20 * size, transcendentals=0),
        compiler_params=pltpu.CompilerParams(collective_id=collective_id, has_side_effects=True),
    )(*arrays)


def share_kernel(planes, own, full, line, send, recv, send_z, recv_z, local):
    y, c, z, x = place()
    peers = [{"y": flip(y, dy), "core": flip(c, dc), "x": flip(x, dx)} for dy, dc, dx in FLIPS]
    line_peers = [{"z": lax.rem(z + d, planes)} for d in range(1, planes)]
    meet(peers + line_peers)
    me = (y * 2 + c) * 2 + x
    copies = []
    for d, peer in enumerate(line_peers):
        copy = remote(own, line.at[z], send_z.at[d], recv_z.at[d], peer)
        copy.start()
        copies.append(copy)
    mine = pltpu.make_async_copy(own, line.at[z], local.at[0])
    mine.start()
    for copy in copies:
        copy.wait()
    mine.wait()
    copies = []
    for f, peer in enumerate(peers):
        copy = remote(line, full.at[me], send.at[f], recv.at[f], peer)
        copy.start()
        copies.append(copy)
    mine = pltpu.make_async_copy(line, full.at[me], local.at[1])
    mine.start()
    for copy in copies:
        copy.wait()
    mine.wait()


def share(own, planes, collective_id):
    return pl.pallas_call(
        functools.partial(share_kernel, planes),
        out_shape=jax.ShapeDtypeStruct((8, planes) + own.shape, own.dtype),
        in_specs=[VMEM],
        out_specs=VMEM,
        scratch_shapes=[
            pltpu.VMEM((planes,) + own.shape, own.dtype),
            pltpu.SemaphoreType.DMA((7,)),
            pltpu.SemaphoreType.DMA((7,)),
            pltpu.SemaphoreType.DMA((planes - 1,)),
            pltpu.SemaphoreType.DMA((planes - 1,)),
            pltpu.SemaphoreType.DMA((2,)),
        ],
        compiler_params=pltpu.CompilerParams(collective_id=collective_id, has_side_effects=True),
    )(own)


def scatter_kernel(part, out, held, diag, from_x, from_y, send, recv):
    y, c, _, x = place()
    meet(neighbours())
    copies = []

    def go(src, dst, sem, device):
        copy = remote(src, dst, send.at[sem], recv.at[sem], device)
        copy.start()
        copies.append(copy)
        return copy

    def slot(dy, core, dx, i):
        return ((flip(y, dy) * 2 + core) * 2 + i, flip(x, dx))

    halves = {}
    for n, (dy, dx, i) in enumerate(
        ((1, 1, 0), (1, 1, 1), (0, 1, 1), (1, 0, 0), (0, 1, 0), (1, 0, 1), (0, 0, 0), (0, 0, 1))
    ):
        seq, xx = slot(dy, 1 - c, dx, i)
        halves[dy, dx, i] = go(part.at[seq, xx], held.at[dy, dx, i], n, {"core": 1 - c})

    def add(dy, dx, i, more=None):
        halves[dy, dx, i].wait_recv()
        seq, xx = slot(dy, c, dx, i)
        total = part[seq, xx].astype(F32) + held[dy, dx, i].astype(F32)
        if more is not None:
            total = total + more.astype(F32)
        return total

    def add_keep(dy, dx, i, more=None):
        held[dy, dx, i] = add(dy, dx, i, more).astype(BF16)

    add_keep(1, 1, 0)
    diag_y = go(held.at[1, 1, 0], diag.at[0], 8, {"y": 1 - y})
    add_keep(1, 1, 1)
    diag_x = go(held.at[1, 1, 1], diag.at[1], 9, {"x": 1 - x})
    add_keep(0, 1, 1)
    x_one = go(held.at[0, 1, 1], from_x.at[1], 10, {"x": 1 - x})
    add_keep(1, 0, 0)
    y_zero = go(held.at[1, 0, 0], from_y.at[0], 11, {"y": 1 - y})
    diag_y.wait_recv()
    add_keep(0, 1, 0, diag[0])
    x_zero = go(held.at[0, 1, 0], from_x.at[0], 12, {"x": 1 - x})
    diag_x.wait_recv()
    add_keep(1, 0, 1, diag[1])
    y_one = go(held.at[1, 0, 1], from_y.at[1], 13, {"y": 1 - y})
    for i, (one, two) in enumerate(((x_zero, y_zero), (x_one, y_one))):
        out[i] = add(0, 0, i)
        one.wait_recv()
        two.wait_recv()
        out[i] += from_x[i].astype(F32) + from_y[i].astype(F32)
    for copy in copies:
        copy.wait_send()


def plane_scatter(part, collective_id):
    _, _, piece, width = part.shape
    return pl.pallas_call(
        scatter_kernel,
        out_shape=jax.ShapeDtypeStruct((2, piece, width), F32),
        in_specs=[VMEM],
        out_specs=VMEM,
        scratch_shapes=[
            pltpu.VMEM((2, 2, 2, piece, width), BF16),
            pltpu.VMEM((2, piece, width), BF16),
            pltpu.VMEM((2, piece, width), BF16),
            pltpu.VMEM((2, piece, width), BF16),
            pltpu.SemaphoreType.DMA((14,)),
            pltpu.SemaphoreType.DMA((14,)),
        ],
        cost_estimate=pl.CostEstimate(
            flops=0, bytes_accessed=10 * part.size * 2, transcendentals=0
        ),
        compiler_params=pltpu.CompilerParams(
            collective_id=collective_id, has_side_effects=True, vmem_limit_bytes=40 * 2**20
        ),
    )(part)


def rms_parts(values):
    scale = lax.rsqrt(jnp.mean(values * values, axis=-1, keepdims=True) + 1e-05)
    return (values * scale, scale)


def rms_back(grad_hat, normal, scale):
    return scale * (grad_hat - normal * jnp.mean(grad_hat * normal, axis=-1, keepdims=True))


def times(left, right):
    return jnp.dot(left, right, preferred_element_type=F32)


def times_t(left, right):
    return lax.dot_general(left, right, (((1,), (1,)), ((), ())), preferred_element_type=F32)


def t_times(left, right):
    return lax.dot_general(left, right, (((0,), (0,)), ((), ())), preferred_element_type=F32)


def adamw(weight, first_mom, second_mom, gradient, rate, decay):
    bias_one = 1.0 - 0.9**STEP
    bias_two = 1.0 - 0.95**STEP
    first_new = 0.9 * first_mom + 0.1 * gradient
    second_new = 0.95 * second_mom + 0.05 * gradient * gradient
    direction = first_new / bias_one / (jnp.sqrt(second_new / bias_two) + 1e-08)
    return (second_new, weight - rate * (direction + decay * weight))


def on_device(
    tokens,
    cotangent,
    norm_gains,
    in_proj,
    conv_taps,
    out_proj,
    gate_up,
    down_proj,
    first_gains,
    first_in,
    first_conv,
    first_out,
    first_gate_up,
    first_down,
    second_gains,
    second_in,
    second_conv,
    second_out,
    second_gate_up,
    second_down,
):
    planes = lax.axis_size("z")
    seqs, piece, width = tokens.shape
    rows = seqs * piece
    all_rows = 8 * rows
    own_d = in_proj.shape[0]
    own_f = down_proj.shape[0]
    ff = gate_up.shape[2]
    part_d = width // 8
    part_f = ff // 8

    in_send = in_proj.astype(BF16).reshape(own_d, 3, 4, planes, 2, own_d)
    in_send = in_send.transpose(2, 4, 0, 1, 3, 5).reshape(8, own_d, 3 * part_d)
    gu_send = gate_up.astype(BF16).reshape(2, own_d, 4, planes, 2, own_f)
    gu_send = gu_send.transpose(2, 4, 0, 1, 3, 5).reshape(8, 2, own_d, part_f)
    small = jnp.concatenate([norm_gains, conv_taps], axis=0)
    small_all = share(small, planes, 0)
    in_mine, gu_mine = plane_swap([in_send, gu_send], 1)

    def along_z(value):
        return lax.all_gather(value, "z", axis=0, tiled=False)

    out_t = along_z(out_proj.astype(BF16)).reshape(part_d, width)
    in_t = along_z(in_mine).reshape(planes, 4, 2, own_d, 3 * part_d)
    in_t = in_t.transpose(1, 0, 2, 3, 4).reshape(width, 3 * part_d)
    gu_t = along_z(gu_mine).reshape(planes, 4, 2, 2, own_d, part_f)
    gu_t = gu_t.transpose(3, 1, 0, 2, 4, 5).reshape(2, width, part_f)
    down_t = along_z(down_proj.astype(BF16)).reshape(part_f, width)

    low = small_all.astype(BF16).astype(F32)
    gains = low[:, :, :2].reshape(4, 2, planes, 2, own_d).transpose(3, 0, 2, 1, 4)
    gains = gains.reshape(2, width)
    y, c, z, x = place()
    taps = lax.dynamic_index_in_dim(low[:, :, 2:], (y * 2 + c) * 2 + x, 0, keepdims=False)
    taps = taps.transpose(1, 0, 2).reshape(3, part_d)

    hidden = tokens.astype(F32).reshape(rows, width)
    hat_one, scale_one = rms_parts(hidden)
    normed = (hat_one * gains[0]).astype(BF16).reshape(seqs, piece, width)
    normed_all = plane_gather(normed, 2).reshape(all_rows, width)
    cot_all = plane_gather(cotangent, 3).reshape(all_rows, width)

    projected = times(normed_all, in_t)
    b_part = projected[:, :part_d]
    c_part = projected[:, part_d : 2 * part_d]
    x_part = projected[:, 2 * part_d :]
    count, length = 4 * seqs, 2 * piece
    mixed_in = (b_part * x_part).reshape(count, length, part_d)
    line = [(i, i + 1) for i in range(planes - 1)]
    arrived = lax.ppermute(mixed_in[:, length - 2 :, :], "z", line)
    extended = jnp.concatenate([arrived, mixed_in], axis=1)
    conv_out = (
        taps[0] * extended[:, :length]
        + taps[1] * extended[:, 1 : length + 1]
        + taps[2] * extended[:, 2:]
    )
    conv_out = conv_out.reshape(all_rows, part_d)
    gated = (c_part * conv_out).astype(BF16)

    def blocks(value):
        return value.astype(BF16).reshape(count, 2, piece, width)

    mixer = plane_scatter(blocks(times(gated, out_t)), 4).reshape(rows, width)
    middle = hidden + mixer
    hat_two, scale_two = rms_parts(middle)
    normed_two = (hat_two * gains[1]).astype(BF16).reshape(seqs, piece, width)
    normed_two_all = plane_gather(normed_two, 5).reshape(all_rows, width)
    gate_val = times(normed_two_all, gu_t[0])
    up_val = times(normed_two_all, gu_t[1])
    sigma = jax.nn.sigmoid(gate_val)
    silu_val = gate_val * sigma
    active = (silu_val * up_val).astype(BF16)

    grad_down = t_times(active, cot_all)
    grad_act = times_t(cot_all, down_t)
    dgate = (grad_act * up_val * sigma * (1.0 + gate_val * (1.0 - sigma))).astype(BF16)
    dup = (grad_act * silu_val).astype(BF16)
    grad_gu = jnp.stack([t_times(normed_two_all, dgate), t_times(normed_two_all, dup)])

    def sum_z(value):
        return lax.psum_scatter(value, "z", scatter_dimension=0, tiled=False)

    g_down = sum_z(grad_down.astype(BF16).reshape(planes, own_f, width)).astype(F32)
    grad_gu = grad_gu.astype(BF16).reshape(2, 4, planes, 2, own_d, part_f)
    grad_gu = grad_gu.transpose(2, 1, 3, 0, 4, 5).reshape(planes, 8, 2, own_d, part_f)
    gu_back = sum_z(grad_gu)

    dnorm_two = plane_scatter(blocks(times_t(dgate, gu_t[0]) + times_t(dup, gu_t[1])), 6)
    dnorm_two = dnorm_two.reshape(rows, width)
    gain_grad_two = jnp.sum(dnorm_two * hat_two, axis=0)
    cot_full = cotangent.astype(F32).reshape(rows, width)
    dmiddle = cot_full + rms_back(dnorm_two * gains[1], hat_two, scale_two)
    dmix = dmiddle.astype(BF16).reshape(seqs, piece, width)
    dmix_all = plane_gather(dmix, 7).reshape(all_rows, width)
    branch = plane_scatter(blocks(times(active, down_t)), 8).reshape(rows, width)
    block_out = (middle + branch).astype(BF16)

    grad_out = t_times(gated, dmix_all)
    dgated = times_t(dmix_all, out_t)
    dc_part = dgated * conv_out
    dconv = (dgated * c_part).reshape(count, length, part_d)
    grad_taps = jnp.stack(
        [
            jnp.sum(dconv * extended[:, :length], axis=(0, 1)),
            jnp.sum(dconv * extended[:, 1 : length + 1], axis=(0, 1)),
            jnp.sum(dconv * extended[:, 2:], axis=(0, 1)),
        ]
    )
    grad_ext = (
        taps[0] * jnp.pad(dconv, ((0, 0), (0, 2), (0, 0)))
        + taps[1] * jnp.pad(dconv, ((0, 0), (1, 1), (0, 0)))
        + taps[2] * jnp.pad(dconv, ((0, 0), (2, 0), (0, 0)))
    )
    returned = lax.ppermute(grad_ext[:, :2, :], "z", [(i + 1, i) for i in range(planes - 1)])
    grad_mixed = grad_ext[:, 2:, :] + jnp.pad(returned, ((0, 0), (length - 2, 0), (0, 0)))
    grad_mixed = grad_mixed.reshape(all_rows, part_d)
    dproj = jnp.concatenate([grad_mixed * x_part, dc_part, grad_mixed * b_part], axis=-1)
    dproj = dproj.astype(BF16)
    grad_in = t_times(normed_all, dproj)
    g_out = sum_z(grad_out.astype(BF16).reshape(planes, own_d, width)).astype(F32)
    grad_in = grad_in.astype(BF16).reshape(4, planes, 2, own_d, 3 * part_d)
    grad_in = grad_in.transpose(1, 0, 2, 3, 4).reshape(planes, 8, own_d, 3 * part_d)
    in_back = sum_z(grad_in)
    g_conv = sum_z(grad_taps.reshape(3, planes, own_d).transpose(1, 0, 2))

    dnorm_one = plane_scatter(blocks(times_t(dproj, in_t)), 9).reshape(rows, width)
    gain_grad_one = jnp.sum(dnorm_one * hat_one, axis=0)
    token_grad = dmiddle + rms_back(dnorm_one * gains[0], hat_one, scale_one)
    grad_gains = jnp.stack([gain_grad_one, gain_grad_two])
    g_gains = lax.psum_scatter(
        grad_gains, ("y", "core", "z", "x"), scatter_dimension=1, tiled=True
    )

    in_got, gu_got = plane_swap([in_back, gu_back], 10)
    g_in = in_got.reshape(4, 2, own_d, 3, planes, own_d).transpose(2, 3, 0, 4, 1, 5)
    g_in = g_in.reshape(own_d, 3 * width).astype(F32)
    g_gu = gu_got.reshape(4, 2, 2, own_d, planes, own_f).transpose(2, 3, 0, 4, 1, 5)
    g_gu = g_gu.reshape(2, own_d, ff).astype(F32)

    m_gains, u_gains = adamw(norm_gains, first_gains, second_gains, g_gains, 0.4, 0.0)
    m_in, u_in = adamw(in_proj, first_in, second_in, g_in, 0.02, 0.1)
    m_conv, u_conv = adamw(conv_taps, first_conv, second_conv, g_conv, 0.2, 0.1)
    m_out, u_out = adamw(out_proj, first_out, second_out, g_out, 0.02, 0.1)
    m_gu, u_gu = adamw(gate_up, first_gate_up, second_gate_up, g_gu, 0.02, 0.1)
    m_down, u_down = adamw(down_proj, first_down, second_down, g_down, 0.01, 0.1)
    return (
        block_out.reshape(seqs, piece, width),
        token_grad.reshape(seqs, piece, width),
        g_gains,
        g_in,
        g_conv,
        g_out,
        g_gu,
        g_down,
        m_gains,
        m_in,
        m_conv,
        m_out,
        m_gu,
        m_down,
        u_gains,
        u_in,
        u_conv,
        u_out,
        u_gu,
        u_down,
    )


def solution(mesh):
    lines = mesh.shape["seq"] // 2
    fine = Mesh(mesh.devices.reshape(2, 2, lines, 2), ("y", "core", "z", "x"))
    dp, seq = ("y", "core"), ("z", "x")
    every = dp + seq
    tokens = P(dp, seq, None)
    weights = (
        P(None, every),
        P(every, None),
        P(None, every),
        P(every, None),
        P(None, every, None),
        P(every, None),
    )
    return jax.shard_map(
        on_device,
        mesh=fine,
        in_specs=(tokens, tokens) + weights * 3,
        out_specs=(tokens, tokens) + weights * 3,
        check_vma=False,
    )
```

time: 2370 us -> 969 us (0.41)
  waiting for transfers between devices: 1880 us -> 141 us
  Pallas kernels: 0 us -> 418 us
  blocking collectives: 125 us -> 33.4 us
  local copies, waits for them, and re-layouts: 15.5 us -> 103 us
  other arithmetic: 105 us -> 60.1 us
  matrix products: 219 us -> 183 us
    reduce_scatter x4, waiting for transfers between devices: 1510 us -> 138 us  [sum_z(): return lax.psum_scatter(value, 'z', scatter_dimension=0, tiled=False)]
    pallas_call x0 -> x11, Pallas kernels: none -> 418 us  [the longest x4 179 us: plane_gather(): pl.pallas_call(gather_kernel, out_shape=jax.ShapeDtypeStruct((4 * seqs, 2...]
    all_gather x4 -> x3, waiting for transfers between devices: 362 us -> 0.02 us  [along_z(): return lax.all_gather(value, 'z', axis=0, tiled=False)]
    all_gather x2 -> x1, blocking collectives: 125 us -> 22.9 us  [along_z(): return lax.all_gather(value, 'z', axis=0, tiled=False)]
    another operation x3 -> x1, other arithmetic: 60.7 us -> 3.26 us  [the longest x1 56 us: on_device(): grad_gu = jnp.stack([t_times(normed_two, dgate), t_times(normed_two, dup)])]
    convert_element_type x1 -> x7, local copies, waits for them, and re-layouts: 0.71 us -> 25.8 us  [the longest x3 13.5 us: on_device(): g_gu = g_gu.reshape(2, own_d, ff).astype(F32)]
  transfers between devices with their start and end apart: 12 -> 10, of which waited for: 10 -> 3; matrix products, arithmetic and copies ran while one was open for 11% -> 19% of each run, Pallas kernels for 0% -> 24%
where the time goes in v1:
time: 969 us; the launch traced here: 959 us
  Pallas kernels  418 us (43%)
  matrix products  183 us (19%)
  waiting for transfers between devices  141 us (15%)
  local copies, waits for them, and re-layouts  103 us (11%)
  other arithmetic  60.1 us (6%)
  blocking collectives  33.4 us (3%)
  between operations  15.3 us (2%)
    pallas_call x4, Pallas kernels, plane_gather(): pl.pallas_call(gather_kernel, out_shape=jax.ShapeDtypeStruct((4 * seqs, 2...  179 us
    pallas_call x4, Pallas kernels, plane_scatter(): pl.pallas_call(scatter_kernel, out_shape=jax.ShapeDtypeStruct((2, piece,...  177 us
    reduce_scatter x4, waiting for transfers between devices, sum_z(): return lax.psum_scatter(value, 'z', scatter_dimension=0, tiled=False)  138 us
    dot_general x5, matrix products, times_t(): lax.dot_general(left, right, (((1,), (1,)), ((), ())), preferred_element_...  75.3 us
    dot_general x5, matrix products, t_times(): lax.dot_general(left, right, (((0,), (0,)), ((), ())), preferred_element_...  58.1 us
    pallas_call x2, Pallas kernels, plane_swap(): pl.pallas_call(functools.partial(swap_kernel, count), out_shape=[jax.Shap...  49.9 us
    dot_general x5, matrix products, times(): return jnp.dot(left, right, preferred_element_type=F32)  49.2 us
    unnamed x132, local copies, waits for them, and re-layouts  25.4 us
  transfers between devices with their start and end apart: 10, of which 3 were waited for; matrix products, arithmetic and copies ran while one was open for 19% of the time, Pallas kernels for 24%

profile of v1, /device:TPU:1, one launch (start us, length us, event | category | flops | bytes accessed | tf_op | source)
XLA Modules:
  0.0 959.5 jit_solution(13651775310903537951)
XLA Ops:
  19.8 25.4 %shard_map.349 = (bf16[8,48,576]{2,1,0:T(8,128)(2,1)}, bf16[8,2,48,864]{3,2,1,0:T(8,128)(2,1)}) custom-call(bf16[8,48,576]{2,1,0:T(8,128)(2,1)} %reshape.341.refs_0_, bf16[8,2,48,864]{3,2,1,0:T(8,128)(2,1)} %reshape.343.refs_1_), custom_call_target="tpu_custom_call" | custom-call | bytes 35389440 | tf_op jit(solution)/shard_map/pallas_call | solution.py:158
  63.4 45.2 %shard_map.348 = bf16[8,2,192,1536]{3,2,1,0:T(8,128)(2,1)} custom-call(bf16[2,192,1536]{2,1,0:T(8,128)(2,1)} %fusion.11.own), custom_call_target="tpu_custom_call" | custom-call | bytes 94371840 | tf_op jit(solution)/shard_map/pallas_call | solution.py:120
  108.6 22.9 %all-gather.1 = bf16[192,1536]{1,0:T(8,128)(2,1)} all-gather(bf16[48,1536]{1,0:T(8,128)(2,1)S(1)} %convert_element_type.127), channel_id=3, replica_groups=mesh['y'=2,'core'=2,'z'=4,'x'=2] {'z'}, dimensions={0}, use_global_device_ids=true | all-gather | bytes 737280 | tf_op jit(solution)/shard_map/all_gather | solution.py:369
  158.7 45.3 %shard_map.353 = bf16[8,2,192,1536]{3,2,1,0:T(8,128)(2,1)} custom-call(bf16[2,192,1536]{2,1,0:T(8,128)(2,1)} %own.1), custom_call_target="tpu_custom_call" | custom-call | bytes 94371840 | tf_op jit(solution)/shard_map/pallas_call | solution.py:120
  216.5 44.0 %shard_map.350 = f32[2,192,1536]{2,1,0:T(8,128)S(1)} custom-call(bf16[8,2,192,1536]{3,2,1,0:T(8,128)(2,1)S(1)} %bitcast.128), custom_call_target="tpu_custom_call" | custom-call | bytes 94371840 | tf_op jit(solution)/shard_map/pallas_call | solution.py:276
  262.5 44.3 %shard_map.351 = bf16[8,2,192,1536]{3,2,1,0:T(8,128)(2,1)} custom-call(bf16[2,192,1536]{2,1,0:T(8,128)(2,1)} %multiply_convert_fusion.6.own), custom_call_target="tpu_custom_call" | custom-call | bytes 94371840 | tf_op jit(solution)/shard_map/pallas_call | solution.py:120
  313.5 12.9 %fusion.40 = f32[3072,864]{0,1:T(8,128)} fusion(bf16[3072,1536]{1,0:T(8,128)(2,1)S(1)} %bitcast.137, bf16[1536,864]{1,0:T(8,128)(2,1)} %bitcast.168), kind=kOutput, calls=%fused_computation.100 | convolution fusion | flops 8153726976 | bytes 22708224 | tf_op jit(solution)/shard_map/dot_general | solution.py:308
  326.5 11.6 %fusion.39 = f32[3072,864]{0,1:T(8,128)} fusion(bf16[3072,1536]{1,0:T(8,128)(2,1)S(1)} %bitcast.138, bf16[1536,864]{1,0:T(8,128)(2,1)S(1)} %bitcast.171), kind=kOutput, calls=%fused_computation.99 | convolution fusion | flops 8153726976 | bytes 22708224 | tf_op jit(solution)/shard_map/dot_general | solution.py:308
  338.0 23.3 %multiply_convert_fusion = (bf16[3072,864]{0,1:T(8,128)(2,1)}, bf16[3072,864]{0,1:T(8,128)(2,1)}, bf16[3072,864]{0,1:T(8,128)(2,1)}) fusion(f32[3072,864]{0,1:T(8,128)} %fusion.39, f32[3072,864]{0,1:T(8,128)} %fusion.40, bf16[3072,1536]{1,0:T(8,128)(2,1)} %bitcast.152, bf16[864,1536]{1,0:T(8,128)(2,1)} %all-gather.12.cloned.1.call-done), kind=kOutput, calls=%fused_computation.4 | convolution fusion | flops 8193540096 | bytes 49250304 | tf_op jit(solution)/shard_map/dot_general | solution.py:312
  361.3 16.8 %fusion.41 = f32[3072,1536]{1,0:T(8,128)} fusion(bf16[3072,864]{0,1:T(8,128)(2,1)} %get-tuple-element.57, bf16[1536,864]{1,0:T(8,128)(2,1)} %bitcast.170), kind=kOutput, calls=%fused_computation.101 | convolution fusion | flops 8153726976 | bytes 26836992 | tf_op jit(solution)/shard_map/dot_general | solution.py:312
  378.1 17.2 %add_convert_fusion = bf16[3072,1536]{1,0:T(8,128)(2,1)} fusion(f32[3072,1536]{1,0:T(8,128)} %fusion.41, bf16[3072,864]{0,1:T(8,128)(2,1)} %get-tuple-element.56, bf16[1536,864]{1,0:T(8,128)(2,1)S(1)} %bitcast.169), kind=kOutput, calls=%fused_computation | convolution fusion | flops 8163164160 | bytes 36274176 | tf_op jit(solution)/shard_map/dot_general | solution.py:312
  399.0 43.9 %shard_map.354 = f32[2,192,1536]{2,1,0:T(8,128)S(1)} custom-call(bf16[8,2,192,1536]{3,2,1,0:T(8,128)(2,1)S(1)} %bitcast.129), custom_call_target="tpu_custom_call" | custom-call | bytes 94371840 | tf_op jit(solution)/shard_map/pallas_call | solution.py:276
  446.8 44.3 %shard_map.355 = bf16[8,2,192,1536]{3,2,1,0:T(8,128)(2,1)} custom-call(bf16[2,192,1536]{2,1,0:T(8,128)(2,1)} %fusion.25.own), custom_call_target="tpu_custom_call" | custom-call | bytes 94371840 | tf_op jit(solution)/shard_map/pallas_call | solution.py:120
  529.3 44.9 %shard_map.356 = f32[2,192,1536]{2,1,0:T(8,128)S(1)} custom-call(bf16[8,2,192,1536]{3,2,1,0:T(8,128)(2,1)S(1)} %bitcast.131), custom_call_target="tpu_custom_call" | custom-call | bytes 94371840 | tf_op jit(solution)/shard_map/pallas_call | solution.py:276
  586.1 13.6 %convolution_convert_fusion.3 = bf16[864,1536]{1,0:T(8,128)(2,1)} fusion(bf16[3072,864]{0,1:T(8,128)(2,1)} %get-tuple-element.58, bf16[3072,1536]{1,0:T(8,128)(2,1)} %bitcast.153), kind=kOutput, calls=%fused_computation.24 | convolution fusion | flops 8155054080 | bytes 17399808 | tf_op jit(solution)/shard_map/dot_general | solution.py:316
  599.8 12.9 %copy.71 = bf16[1536,3072]{1,0:T(8,128)(2,1)} copy(bf16[1536,3072]{0,1:T(8,128)(2,1)} %bitcast.134) | data formatting | bytes 18874368 | tf_op jit(solution)/shard_map/dot_general | solution.py:316
  612.8 11.7 %convolution_convert_fusion.4 = bf16[1536,576]{0,1:T(8,128)(2,1)} fusion(bf16[3072,1536]{1,0:T(8,128)(2,1)} %bitcast.151, bf16[3072,192]{0,1:T(8,128)(2,1)} %copy-done.33, bf16[3072,192]{0,1:T(8,128)(2,1)S(1)} %copy-done.30, bf16[3072,192]{0,1:T(8,128)(2,1)S(1)} %copy-done.32), kind=kOutput, calls=%fused_computation.29 | convolution fusion | flops 5447319552 | bytes 14745600 | tf_op jit(solution)/shard_map/dot_general | solution.py:316
  628.8 14.0 %convert_bitcast_fusion = bf16[1,4,4,2,48,864]{5,4,3,2,1,0:T(8,128)(2,1)S(1)} fusion(bf16[4,4,2,48,3072]{4,3,2,1,0:T(8,128)(2,1)} %bitcast.154, bf16[3072,864]{0,1:T(8,128)(2,1)} %get-tuple-element.56), kind=kOutput, calls=%fused_computation.30 | convolution fusion | flops 8155054080 | bytes 17399808 | tf_op jit(solution)/shard_map/dot_general | solution.py:316
  642.9 12.2 %convert_bitcast_fusion.1 = bf16[1,4,4,2,48,864]{5,4,3,2,1,0:T(8,128)(2,1)S(1)} fusion(bf16[4,4,2,48,3072]{4,3,2,1,0:T(8,128)(2,1)S(1)} %bitcast.157, bf16[3072,864]{0,1:T(8,128)(2,1)} %get-tuple-element.57), kind=kOutput, calls=%fused_computation.31 | convolution fusion | flops 8155054080 | bytes 17399808 | tf_op jit(solution)/shard_map/dot_general | solution.py:316
  670.3 13.2 %convolution_convert_fusion = bf16[3072,1536]{1,0:T(8,128)(2,1)S(1)} fusion(bf16[3072,864]{0,1:T(8,128)(2,1)} %get-tuple-element.58, bf16[864,1536]{1,0:T(8,128)(2,1)} %all-gather.12.cloned.1.call-done), kind=kOutput, calls=%fused_computation.1 | convolution fusion | flops 8158445568 | bytes 17399808 | tf_op jit(solution)/shard_map/dot_general | solution.py:308
  683.6 44.5 %shard_map.352 = f32[2,192,1536]{2,1,0:T(8,128)S(1)} custom-call(bf16[8,2,192,1536]{3,2,1,0:T(8,128)(2,1)S(1)} %bitcast.130), custom_call_target="tpu_custom_call" | custom-call | bytes 94371840 | tf_op jit(solution)/shard_map/pallas_call | solution.py:276
  757.3 37.9 %reduce-scatter.8.cloned.1.call-done = bf16[1,8,48,576]{3,2,1,0:T(8,128)(2,1)} async-done(((bf16[4,8,48,576]{3,2,1,0:T(8,128)(2,1)}), bf16[1,8,48,576]{3,2,1,0:T(8,128)(2,1)}) %reduce-scatter.8.cloned.1.call-update) | async-done | bytes 442384 | tf_op jit(solution)/shard_map/reduce_scatter | solution.py:429
  795.2 99.8 %reduce-scatter.10.cloned.1.call-done = bf16[1,8,2,48,864]{4,3,2,1,0:T(8,128)(2,1)} async-done(((bf16[4,8,2,48,864]{4,3,2,1,0:T(8,128)(2,1)}), bf16[1,8,2,48,864]{4,3,2,1,0:T(8,128)(2,1)}) %reduce-scatter.10.cloned.1.call-update) | async-done | bytes 1327120 | tf_op jit(solution)/shard_map/reduce_scatter | solution.py:429
  894.9 24.5 %shard_map.357 = (bf16[8,48,576]{2,1,0:T(8,128)(2,1)}, bf16[8,2,48,864]{3,2,1,0:T(8,128)(2,1)}) custom-call(bf16[8,48,576]{2,1,0:T(8,128)(2,1)} %bitcast.178, bf16[8,2,48,864]{3,2,1,0:T(8,128)(2,1)} %bitcast.176), custom_call_target="tpu_custom_call" | custom-call | bytes 35389440 | tf_op jit(solution)/shard_map/pallas_call | solution.py:158
  (240 shorter events, 217.7 us)
Async XLA Ops:
  7.2 124.3 %all-gather.8.cloned.1.call-start = ((), (), s32[]{:S(2)}) async-start(), calls=%async_computation.9 | async-start | bytes 2457600 | tf_op jit(solution)/shard_map/all_gather | solution.py:369
  45.3 261.5 %all-gather.10.cloned.1.call-start = ((), (), s32[]{:S(2)}) async-start(), calls=%async_computation.10 | async-start | bytes 6881280 | tf_op jit(solution)/shard_map/all_gather | solution.py:369
  46.0 292.0 %all-gather.12.cloned.1.call-start = ((), (), s32[]{:S(2)}) async-start(), calls=%async_computation.11 | async-start | bytes 3317760 | tf_op jit(solution)/shard_map/all_gather | solution.py:369
  47.0 701.6 %reduce-scatter.16.cloned.1.call-start = ((), (), s32[]{:S(2)}) async-start(), calls=%async_computation.12 | async-start | bytes 811008
  63.4 45.2 %copy-start.34 = (f32[48,1536]{1,0:T(8,128)S(1)}, f32[48,1536]{1,0:T(8,128)}, u32[]{:S(2)}) copy-start(f32[48,1536]{1,0:T(8,128)} %param.25) | copy-start | bytes 884740
  147.3 58.6 %copy-start.9 = (f32[24,8,8,384]{3,2,1,0:T(8,128)}, f32[24,8,8,384]{3,2,1,0:T(8,128)S(1)}, u32[]{:S(2)}) copy-start(f32[24,8,8,384]{3,2,1,0:T(8,128)S(1)} %copy.80) | copy-start | bytes 7077892
  150.8 53.2 %collective-permute-start = (f32[8,2,192]{2,0,1:T(8,128)}, f32[8,2,192]{2,0,1:T(8,128)}, u32[]{:S(2)}, u32[]{:S(2)}) collective-permute-start(f32[8,2,192]{2,0,1:T(8,128)} %copy.79), channel_id=1, source_target_pairs={{0,2},{2,4},{4,6},{1,3},{3,5},{5,7},{8,10},{10,12},{12,14},{9,11},... | collective-permute-start | bytes 36872 | tf_op jit(solution)/shard_map/ppermute | solution.py:398
  158.7 285.0 %copy-start.38 = (f32[1536]{0:T(1024)}, f32[1536]{0:T(1024)S(1)}, u32[]{:S(2)}) copy-start(f32[1536]{0:T(1024)S(1)} %mul.457) | copy-start | bytes 18436
  260.9 182.7 %copy-start.5 = (f32[2,192,1536]{2,1,0:T(8,128)}, f32[2,192,1536]{2,1,0:T(8,128)S(1)}, u32[]{:S(2)}) copy-start(f32[2,192,1536]{2,1,0:T(8,128)S(1)} %get-tuple-element.55) | copy-start | bytes 7077892
  261.0 182.7 %copy-start.42 = (f32[2,192]{1,0:T(2,128)}, f32[2,192]{1,0:T(2,128)S(1)}, u32[]{:S(2)}) copy-start(f32[2,192]{1,0:T(2,128)S(1)} %add_rsqrt_fusion) | copy-start | bytes 4612
  446.8 44.3 %copy-start.22 = (bf16[192,1536]{1,0:T(8,128)(2,1)S(1)}, bf16[192,1536]{1,0:T(8,128)(2,1)}, u32[]{:S(2)}) copy-start(bf16[192,1536]{1,0:T(8,128)(2,1)} %all-gather.1) | copy-start | bytes 1769476
  508.5 4.5 collective-permute-start.1
  529.3 46.4 %copy-start.7 = (bf16[2,192,1536]{2,1,0:T(8,128)(2,1)S(1)}, bf16[2,192,1536]{2,1,0:T(8,128)(2,1)}, u32[]{:S(2)}) copy-start(bf16[2,192,1536]{2,1,0:T(8,128)(2,1)} %param.20) | copy-start | bytes 3538948
  529.3 46.3 %copy-start.41 = (f32[1536]{0:T(1024)S(1)}, f32[1536]{0:T(1024)}, u32[]{:S(2)}) copy-start(f32[1536]{0:T(1024)} %copy-done.40) | copy-start | bytes 18436
  529.3 46.3 %copy-start.44 = (f32[2,192]{1,0:T(2,128)S(1)}, f32[2,192]{1,0:T(2,128)}, u32[]{:S(2)}) copy-start(f32[2,192]{1,0:T(2,128)} %copy-done.43) | copy-start | bytes 4612
  579.5 171.4 %reduce-scatter.12.cloned.1.call-start = ((), (), s32[]{:S(2)}) async-start(), calls=%async_computation.7 | async-start | bytes 737280 | tf_op jit(solution)/shard_map/reduce_scatter | solution.py:429
  586.1 167.0 %reduce-scatter.14.cloned.1.call-start = ((), (), s32[]{:S(2)}) async-start(), calls=%async_computation.8 | async-start | bytes 3317760 | tf_op jit(solution)/shard_map/reduce_scatter | solution.py:429
  599.8 195.4 %reduce-scatter.8.cloned.1.call-start = ((), (), s32[]{:S(2)}) async-start(), calls=%async_computation.5 | async-start | bytes 2457600 | tf_op jit(solution)/shard_map/reduce_scatter | solution.py:429
  628.8 266.2 %reduce-scatter.10.cloned.1.call-start = ((), (), s32[]{:S(2)}) async-start(), calls=%async_computation.6 | async-start | bytes 6881280 | tf_op jit(solution)/shard_map/reduce_scatter | solution.py:429
  683.5 46.1 %copy-start.48 = (f32[1,4,48]{2,0,1:T(1,128)S(1)}, f32[1,4,48]{2,0,1:T(1,128)}, u32[]{:S(2)}) copy-start(f32[1,4,48]{2,0,1:T(1,128)} %stack.30) | copy-start | bytes 2308
  683.5 46.1 %copy-start.49 = (f32[1,4,48]{2,0,1:T(1,128)S(1)}, f32[1,4,48]{2,0,1:T(1,128)}, u32[]{:S(2)}) copy-start(f32[1,4,48]{2,0,1:T(1,128)} %stack.31) | copy-start | bytes 2308
  683.5 46.1 %copy-start.50 = (f32[1,4,48]{2,0,1:T(1,128)S(1)}, f32[1,4,48]{2,0,1:T(1,128)}, u32[]{:S(2)}) copy-start(f32[1,4,48]{2,0,1:T(1,128)} %stack.32) | copy-start | bytes 2308
  683.6 59.8 %copy-start.1 = (f32[2,192,1536]{2,1,0:T(8,128)S(1)}, f32[2,192,1536]{2,1,0:T(8,128)}, u32[]{:S(2)}) copy-start(f32[2,192,1536]{2,1,0:T(8,128)} %copy-done) | copy-start | bytes 7077892
  683.6 59.8 %copy-start.39 = (f32[1536]{0:T(1024)S(1)}, f32[1536]{0:T(1024)}, u32[]{:S(2)}) copy-start(f32[1536]{0:T(1024)} %copy-done.38) | copy-start | bytes 18436
  (48 other events, 318.8 us)
Sparse Core Ops, SparseCore 0:
  45.4 44.2 all-gather.7
  91.3 110.7 all-gather.9
  204.3 53.6 all-gather.11
  579.6 92.4 reduce-scatter.15
  674.8 20.6 reduce-scatter.11
  698.2 53.4 reduce-scatter.13
  754.0 41.1 reduce-scatter.7
  797.5 97.4 reduce-scatter.9

commit v2 on v1

v2 whole, which is shorter than its diff:
```python
import functools

import jax
import jax.numpy as jnp
from jax import lax
from jax.experimental import pallas as pl
from jax.experimental.pallas import tpu as pltpu
from jax.sharding import Mesh
from jax.sharding import PartitionSpec as P

STEP = 10
MESH = pl.DeviceIdType.MESH
BF16 = jnp.bfloat16
F32 = jnp.float32
FLIPS = [(dy, dc, dx) for dy in (0, 1) for dc in (0, 1) for dx in (0, 1)][1:]
ANY = pl.BlockSpec(memory_space=pl.ANY)
VMEM = pl.BlockSpec(memory_space=pltpu.VMEM)


def place():
    return tuple(lax.axis_index(a) for a in ("y", "core", "z", "x"))


def flip(value, by):
    return 1 - value if by else value


def remote(src, dst, send, recv, device):
    return pltpu.make_async_remote_copy(
        src_ref=src,
        dst_ref=dst,
        send_sem=send,
        recv_sem=recv,
        device_id=device,
        device_id_type=MESH,
    )


def meet(peers):
    barrier = pltpu.get_barrier_semaphore()
    for peer in peers:
        pl.semaphore_signal(barrier, inc=1, device_id=peer, device_id_type=MESH)
    pl.semaphore_wait(barrier, len(peers))


class Gather:
    def __init__(self, own, full, send, recv, base=0):
        self.own, self.full, self.send, self.recv, self.base = own, full, send, recv, base
        self.started = []

    def go(self, src, slot, sem, device):
        sem = self.base + sem
        copy = remote(
            src, self.full.at[slot[0], slot[1]], self.send.at[sem], self.recv.at[sem], device
        )
        copy.start()
        self.started.append(copy)

    def first(self):
        y, c, _, x = place()
        me = (y * 2 + x) * 2 + c
        for i, j in ((0, 1), (1, 0)):
            self.go(self.own.at[i], (me, i), i, {"x": 1 - x})
            self.go(self.own.at[j], (me, j), 2 + j, {"y": 1 - y})
        for i in (0, 1):
            self.go(self.own.at[i], (me, i), 6 + i, {"core": 1 - c})

    def arrived(self, *sems):
        for sem in sems:
            done = self.recv.at[self.base + sem]
            pltpu.make_async_copy(self.own.at[0], self.own.at[0], done).wait()

    def pass_on(self, dy, dx, i, sem, device):
        y, c, _, x = place()
        slot = ((flip(y, dy) * 2 + flip(x, dx)) * 2 + c, i)
        self.go(self.full.at[slot[0], slot[1]], slot, sem, device)

    def forward(self):
        y, c, _, x = place()
        self.arrived(0)
        self.pass_on(0, 1, 0, 4, {"y": 1 - y})
        self.pass_on(0, 1, 0, 8, {"core": 1 - c})
        self.arrived(3)
        self.pass_on(1, 0, 1, 5, {"x": 1 - x})
        self.pass_on(1, 0, 1, 11, {"core": 1 - c})

    def second(self):
        _, c, _, _ = place()
        self.arrived(1)
        self.pass_on(0, 1, 1, 9, {"core": 1 - c})
        self.arrived(2)
        self.pass_on(1, 0, 0, 10, {"core": 1 - c})

    def last(self):
        _, c, _, _ = place()
        self.arrived(4)
        self.pass_on(1, 1, 0, 12, {"core": 1 - c})
        self.arrived(5)
        self.pass_on(1, 1, 1, 13, {"core": 1 - c})

    def sent(self):
        for copy in self.started:
            copy.wait_send()


def neighbours():
    y, c, _, x = place()
    return [{"x": 1 - x}, {"y": 1 - y}, {"core": 1 - c}]


def others():
    y, c, _, x = place()
    return [{"y": flip(y, dy), "core": flip(c, dc), "x": flip(x, dx)} for dy, dc, dx in FLIPS]


def swap(src, dst, send, recv, local):
    y, c, _, x = place()
    me = (y * 2 + c) * 2 + x
    copies = []
    for f, peer in enumerate(others()):
        to = (peer["y"] * 2 + peer["core"]) * 2 + peer["x"]
        copies.append(remote(src.at[to], dst.at[me], send.at[f], recv.at[f], peer))
    copies.append(pltpu.make_async_copy(src.at[me], dst.at[me], local))
    for copy in copies:
        copy.start()
    return copies


def along_line(planes, own, full, send, recv, local):
    z = lax.axis_index("z")
    copies = [
        remote(own, full.at[z], send.at[d], recv.at[d], peer)
        for d, peer in enumerate(line_peers(planes))
    ]
    copies.append(pltpu.make_async_copy(own, full.at[z], local))
    for copy in copies:
        copy.start()
    return copies


def line_peers(planes):
    return [{"z": lax.rem(lax.axis_index("z") + d, planes)} for d in range(1, planes)]


def gather_kernel(own, full, send, recv, local):
    y, c, _, x = place()
    meet(neighbours())
    gather = Gather(own, full, send, recv)
    gather.first()
    mine = pltpu.make_async_copy(own, full.at[(y * 2 + x) * 2 + c], local)
    mine.start()
    gather.forward()
    gather.second()
    gather.last()
    gather.arrived(*range(6, 14))
    gather.sent()
    mine.wait()


def early_kernel(
    planes,
    own,
    block,
    out,
    full,
    got,
    outs,
    send,
    recv,
    send_s,
    recv_s,
    send_z,
    recv_z,
    local,
):
    y, c, _, x = place()
    meet(others() + line_peers(planes))
    copies = along_line(planes, out, outs, send_z, recv_z, local.at[0])
    gather = Gather(own, full, send, recv)
    gather.first()
    mine = pltpu.make_async_copy(own, full.at[(y * 2 + x) * 2 + c], local.at[1])
    mine.start()
    copies += [mine] + swap(block, got, send_s, recv_s, local.at[2])
    gather.forward()
    gather.second()
    gather.last()
    gather.arrived(*range(6, 14))
    gather.sent()
    for copy in copies:
        copy.wait()


def params(collective_id, vmem=0):
    more = {"vmem_limit_bytes": vmem * 2**20} if vmem else {}
    return pltpu.CompilerParams(collective_id=collective_id, has_side_effects=True, **more)


def cost(micros):
    return pl.CostEstimate(flops=int(micros * 1e9), bytes_accessed=0, transcendentals=0)


def sems(*shape):
    return pltpu.SemaphoreType.DMA(shape)


def plane_gather(own, collective_id):
    return pl.pallas_call(
        gather_kernel,
        out_shape=jax.ShapeDtypeStruct((8,) + own.shape, own.dtype),
        in_specs=[ANY],
        out_specs=ANY,
        scratch_shapes=[sems(14), sems(14), pltpu.SemaphoreType.DMA],
        cost_estimate=cost(45),
        compiler_params=params(collective_id),
    )(own)


def early(planes, own, block, out, collective_id):
    return pl.pallas_call(
        functools.partial(early_kernel, planes),
        out_shape=[
            jax.ShapeDtypeStruct((8,) + own.shape, own.dtype),
            jax.ShapeDtypeStruct(block.shape, block.dtype),
            jax.ShapeDtypeStruct((planes,) + out.shape, out.dtype),
        ],
        in_specs=[ANY] * 3,
        out_specs=[ANY] * 3,
        scratch_shapes=[
            sems(14), sems(14), sems(7), sems(7), sems(planes - 1), sems(planes - 1), sems(3)
        ],
        cost_estimate=cost(65),
        compiler_params=params(collective_id),
    )(own, block, out)


def finish_kernel(planes, ins, gus, gains, taps, outs, ins_got, gus_got, sums, out_sum, *scratch):
    parts, terms, got, outs_got, send, recv, send_g, recv_g = scratch[:8]
    send_z, recv_z, send_o, recv_o, local = scratch[8:]
    meet(others() + line_peers(planes))
    small = swap(gains, parts, send_g, recv_g, local.at[0])
    large = scatter_line(planes, outs, outs_got, send_o, recv_o, local.at[3])
    copies = swap(ins, ins_got, send.at[0], recv.at[0], local.at[1])
    copies += swap(gus, gus_got, send.at[1], recv.at[1], local.at[2])
    for copy in small:
        copy.wait()
    terms[:, 0:2, :] = jnp.sum(parts[...], axis=0)
    terms[:, 2:5, :] = taps[...]
    for copy in scatter_line(planes, terms, got, send_z, recv_z, local.at[0]):
        copy.wait()
    sums[...] = jnp.sum(got[...], axis=0)
    for copy in large:
        copy.wait()
    total = outs_got[0].astype(F32)
    for k in range(1, planes):
        total += outs_got[k].astype(F32)
    out_sum[...] = total
    for copy in copies:
        copy.wait()


def scatter_line(planes, terms, got, send, recv, local):
    z = lax.axis_index("z")
    copies = [
        remote(terms.at[peer["z"]], got.at[z], send.at[d], recv.at[d], peer)
        for d, peer in enumerate(line_peers(planes))
    ]
    copies.append(pltpu.make_async_copy(terms.at[z], got.at[z], local))
    for copy in copies:
        copy.start()
    return copies


def finish(planes, ins, gus, gains, taps, outs, collective_id):
    own = gains.shape[-1]
    return pl.pallas_call(
        functools.partial(finish_kernel, planes),
        out_shape=[
            jax.ShapeDtypeStruct(ins.shape, ins.dtype),
            jax.ShapeDtypeStruct(gus.shape, gus.dtype),
            jax.ShapeDtypeStruct((5, own), F32),
            jax.ShapeDtypeStruct(outs.shape[1:], F32),
        ],
        in_specs=[ANY, ANY, VMEM, VMEM, VMEM],
        out_specs=[ANY, ANY, VMEM, VMEM],
        scratch_shapes=[
            pltpu.VMEM(gains.shape, F32),
            pltpu.VMEM((planes, 5, own), F32),
            pltpu.VMEM((planes, 5, own), F32),
            pltpu.VMEM(outs.shape, BF16),
            sems(2, 7),
            sems(2, 7),
            sems(7),
            sems(7),
            sems(planes - 1),
            sems(planes - 1),
            sems(planes - 1),
            sems(planes - 1),
            sems(4),
        ],
        cost_estimate=cost(25),
        compiler_params=params(collective_id),
    )(ins, gus, gains, taps, outs)


def share_kernel(
    planes, own, block, full, got, line, send, recv, send_z, recv_z, local, send_s, recv_s
):
    y, c, _, x = place()
    meet(others() + line_peers(planes))
    me = (y * 2 + c) * 2 + x
    copies = along_line(planes, own, line, send_z, recv_z, local.at[0])
    swapped = swap(block, got, send_s, recv_s, local.at[1])
    for copy in copies:
        copy.wait()
    copies = []
    for f, peer in enumerate(others()):
        copy = remote(line, full.at[me], send.at[f], recv.at[f], peer)
        copy.start()
        copies.append(copy)
    mine = pltpu.make_async_copy(line, full.at[me], local.at[0])
    mine.start()
    for copy in copies + swapped:
        copy.wait()
    mine.wait()


def share(own, block, planes, collective_id):
    return pl.pallas_call(
        functools.partial(share_kernel, planes),
        out_shape=[
            jax.ShapeDtypeStruct((8, planes) + own.shape, own.dtype),
            jax.ShapeDtypeStruct(block.shape, block.dtype),
        ],
        in_specs=[VMEM, ANY],
        out_specs=[VMEM, ANY],
        scratch_shapes=[
            pltpu.VMEM((planes,) + own.shape, own.dtype),
            pltpu.SemaphoreType.DMA((7,)),
            pltpu.SemaphoreType.DMA((7,)),
            pltpu.SemaphoreType.DMA((planes - 1,)),
            pltpu.SemaphoreType.DMA((planes - 1,)),
            pltpu.SemaphoreType.DMA((2,)),
            pltpu.SemaphoreType.DMA((7,)),
            pltpu.SemaphoreType.DMA((7,)),
        ],
        cost_estimate=cost(12),
        compiler_params=params(collective_id),
    )(own, block)


def load_rows(planes, gathered, rows, sem):
    if len(gathered.shape) == 3:
        copy = pltpu.make_async_copy(gathered, rows, sem)
        copy.start()
        return [copy]
    own = gathered.shape[3]
    copies = []
    for z in range(planes):
        for m in range(8):
            start = (((m // 2) * planes + z) * 2 + m % 2) * own
            for j in (0, 1):
                src = gathered.at[z, m, j]
                copies.append(pltpu.make_async_copy(src, rows.at[j, pl.ds(start, own)], sem))
    for copy in copies:
        copy.start()
    return copies


def ffn_kernel(
    planes,
    cot,
    normed,
    gathered,
    down,
    act_out,
    dgate_out,
    dup_out,
    grad_out,
    full,
    near,
    weights,
    gates,
    ups,
    staged,
    total,
    send,
    recv,
    local,
    near_sem,
    out_sem,
):
    y, c, _, x = place()
    piece, width = cot.shape[1:]
    part = down.shape[0]
    chip_rows = 4 * piece
    half = 2 * piece
    chips = [flip(y, dy) * 2 + flip(x, dx) for dy, dx in ((0, 0), (0, 1), (1, 0), (1, 1))]
    loads = load_rows(planes, gathered, weights, local.at[0])
    mine = pltpu.make_async_copy(cot, full.at[(y * 2 + x) * 2 + c], local.at[1])
    mine.start()

    def fetch(k):
        copy = pltpu.make_async_copy(
            normed.at[pl.ds(chips[k] * 2, 2)], near.at[k % 2], near_sem.at[k % 2]
        )
        copy.start()
        return copy

    fetched = {0: fetch(0), 1: fetch(1)}
    meet(neighbours())
    gather = Gather(cot, full, send, recv)
    gather.first()
    for copy in loads:
        copy.wait()

    def gate_up(k, slot):
        fetched[k].wait()

        def body(i, _):
            rows = pl.ds(pl.multiple_of(i * half, half), half)
            left = near[k % 2, i].reshape(half, width)
            gates[slot, rows, :] = times(left, weights[0])
            ups[slot, rows, :] = times(left, weights[1])
            return 0

        lax.fori_loop(0, 2, body, 0)
        if k + 2 < 4:
            fetched[k + 2] = fetch(k + 2)

    written = {}

    def back(k, slot):
        if k >= 2:
            for copy in written[k - 2]:
                copy.wait()
        room = staged.at[k % 2]

        def body(i, _):
            rows = pl.ds(pl.multiple_of(i * half, half), half)
            grad = times_t(full[chips[k] * 2 + i].reshape(half, width), down[...])
            gate, up = gates[slot, rows, :], ups[slot, rows, :]
            sigma = jax.nn.sigmoid(gate)
            silu = gate * sigma
            room[0, i] = (silu * up).astype(BF16).reshape(2, piece, part)
            dgate = grad * up * sigma * (1.0 + gate * (1.0 - sigma))
            room[1, i] = dgate.astype(BF16).reshape(2, piece, part)
            room[2, i] = (grad * silu).astype(BF16).reshape(2, piece, part)
            return 0

        lax.fori_loop(0, 2, body, 0)
        written[k] = []
        for n, out in enumerate((act_out, dgate_out, dup_out)):
            copy = pltpu.make_async_copy(
                room.at[n], out.at[pl.ds(chips[k] * 2, 2)], out_sem.at[k % 2, n]
            )
            copy.start()
            written[k].append(copy)
        active = room[0].reshape(chip_rows, part)
        tile = width // 3

        def sum_up(n, _):
            columns = pl.ds(pl.multiple_of(n * tile, tile), tile)
            right = full[pl.ds(chips[k] * 2, 2), :, :, columns].reshape(chip_rows, tile)
            product = t_times(active, right)
            if k == 0:
                total[:, columns] = product
            elif k < 3:
                total[:, columns] += product
            else:
                product = total[:, columns] + product
                own = part // planes
                for z in range(planes):
                    grad_out[z, :, columns] = product[z * own : (z + 1) * own].astype(BF16)
            return 0

        lax.fori_loop(0, 3, sum_up, 0)

    gate_up(0, 0)
    mine.wait()
    gather.arrived(6, 7)
    back(0, 0)
    gather.forward()
    gate_up(1, 0)
    gate_up(2, 1)
    gather.second()
    gather.arrived(8, 9)
    back(1, 0)
    gate_up(3, 0)
    gather.arrived(10, 11)
    back(2, 1)
    gather.last()
    gather.arrived(12, 13)
    back(3, 0)
    gather.sent()
    for k in (2, 3):
        for copy in written[k]:
            copy.wait()


def ffn(planes, cot, normed, gathered, down, collective_id):
    _, piece, width = cot.shape
    part = down.shape[0]
    wide = jax.ShapeDtypeStruct((8, 2, piece, part), BF16)
    return pl.pallas_call(
        functools.partial(ffn_kernel, planes),
        out_shape=[wide, wide, wide, jax.ShapeDtypeStruct((planes, part // planes, width), BF16)],
        in_specs=[ANY, ANY, ANY, VMEM],
        out_specs=[ANY, ANY, ANY, VMEM],
        scratch_shapes=[
            pltpu.VMEM((8, 2, piece, width), BF16),
            pltpu.VMEM((2, 2, 2, piece, width), BF16),
            pltpu.VMEM((2, width, part), BF16),
            pltpu.VMEM((2, 4 * piece, part), F32),
            pltpu.VMEM((2, 4 * piece, part), F32),
            pltpu.VMEM((2, 3, 2, 2, piece, part), BF16),
            pltpu.VMEM((part, width), F32),
            pltpu.SemaphoreType.DMA((14,)),
            pltpu.SemaphoreType.DMA((14,)),
            pltpu.SemaphoreType.DMA((2,)),
            pltpu.SemaphoreType.DMA((2,)),
            pltpu.SemaphoreType.DMA((2, 3)),
        ],
        cost_estimate=cost(55),
        compiler_params=params(collective_id, 60),
    )(cot, normed, gathered, down)


def scatter_kernel(planes, pairs, transposed, with_grads, *refs):
    refs = list(refs)
    lefts = [refs.pop(0) for _ in range(pairs)]
    if with_grads:
        gathered, normed = refs.pop(0), refs.pop(0)
        out, grads = refs.pop(0), refs.pop(0)
    else:
        rights = [refs.pop(0) for _ in range(pairs)]
        out = refs.pop(0)
    staged, held, ready, keep, diag, from_x, from_y, send, recv = refs[:9]
    if with_grads:
        weights, every, local = refs[9:]
        rights = [weights.at[j] for j in range(pairs)]
        loads = load_rows(planes, gathered, weights, local.at[0])
        whole = pltpu.make_async_copy(normed, every, local.at[1])
        whole.start()
    y, c, _, x = place()
    _, piece, width = out.shape
    rows = 2 * piece
    tile = width // 3
    meet(neighbours())
    if with_grads:
        for copy in loads:
            copy.wait()
    copies = []

    def go(src, dst, sem, device):
        copy = remote(src, dst, send.at[sem], recv.at[sem], device)
        copy.start()
        copies.append(copy)
        return copy

    def product(dy, dx, core, store):
        member = (flip(y, dy) * 2 + flip(x, dx)) * 2 + core

        def body(n, _):
            columns = pl.ds(pl.multiple_of(n * tile, tile), tile)
            value = None
            for left, right in zip(lefts, rights):
                a = left[member].reshape(rows, left.shape[-1])
                if transposed:
                    term = times_t(a, right[columns, :])
                else:
                    term = times(a, right[:, columns])
                value = term if value is None else value + term
            store(columns, value.reshape(2, piece, tile))
            return 0

        lax.fori_loop(0, 3, body, 0)

    order = ((1, 1), (0, 1), (1, 0), (0, 0))
    over = []

    def to_other_core(n):
        dy, dx = order[n]

        def store(columns, value):
            staged[n, :, :, columns] = value.astype(BF16)

        product(dy, dx, 1 - c, store)
        over.append(go(staged.at[n], held.at[n], n, {"core": 1 - c}))

    def own_core(n, store):
        dy, dx = order[n]
        over[n].wait_recv()

        def add(columns, value):
            store(columns, value + held[n, :, :, columns].astype(F32))

        product(dy, dx, c, add)

    def store_diag(columns, value):
        ready[0, :, :, columns] = value.astype(BF16)

    def store_x(columns, value):
        ready[1, 1, :, columns] = value[1].astype(BF16)
        keep[0, :, columns] = value[0]

    def store_y(columns, value):
        ready[2, 0, :, columns] = value[0].astype(BF16)
        keep[1, :, columns] = value[1]

    def store_own(columns, value):
        out[:, :, columns] = value

    to_other_core(0)
    to_other_core(1)
    own_core(0, store_diag)
    diag_y = go(ready.at[0, 0], diag.at[0], 4, {"y": 1 - y})
    diag_x = go(ready.at[0, 1], diag.at[1], 5, {"x": 1 - x})
    to_other_core(2)
    own_core(1, store_x)
    x_one = go(ready.at[1, 1], from_x.at[1], 6, {"x": 1 - x})
    own_core(2, store_y)
    y_zero = go(ready.at[2, 0], from_y.at[0], 7, {"y": 1 - y})
    to_other_core(3)
    own_core(3, store_own)

    quarter = width // 4

    def gradient(j):
        own = grads.shape[-2]

        def body(q, _):
            columns = pl.ds(pl.multiple_of(q * quarter, quarter), quarter)
            left = every[:, :, :, columns].reshape(8 * rows, quarter)
            right = lefts[j][...].reshape(8 * rows, lefts[j].shape[-1])
            value = t_times(left, right).astype(BF16)
            if len(grads.shape) == 3:
                grads[j, columns, :] = value
                return 0
            for z in range(planes):
                for xx in (0, 1):
                    start = (z * 2 + xx) * own
                    grads[z, q * 2 + xx, j] = value[start : start + own]
            return 0

        lax.fori_loop(0, 4, body, 0)

    if with_grads:
        whole.wait()
        gradient(0)
    diag_y.wait_recv()
    ready[1, 0] = (keep[0] + diag[0].astype(F32)).astype(BF16)
    x_zero = go(ready.at[1, 0], from_x.at[0], 8, {"x": 1 - x})
    diag_x.wait_recv()
    ready[2, 1] = (keep[1] + diag[1].astype(F32)).astype(BF16)
    y_one = go(ready.at[2, 1], from_y.at[1], 9, {"y": 1 - y})
    if with_grads:
        gradient(1)
    for i, (one, two) in enumerate(((x_zero, y_zero), (x_one, y_one))):
        one.wait_recv()
        two.wait_recv()
        out[i] += from_x[i].astype(F32) + from_y[i].astype(F32)
    for copy in copies:
        copy.wait_send()


def plane_scatter(lefts, rights, transposed, collective_id, gathered=None, normed=None):
    piece = lefts[0].shape[2]
    with_grads = gathered is not None
    if with_grads:
        planes, part = gathered.shape[0], gathered.shape[-1]
        width = normed.shape[3]
        operands = [*lefts, gathered, normed]
        in_specs = [VMEM] * len(lefts) + [ANY, ANY]
    else:
        planes = 0
        width = rights[0].shape[0 if transposed else 1]
        operands = [*lefts, *rights]
        in_specs = [VMEM] * len(operands)
    out_shape = [jax.ShapeDtypeStruct((2, piece, width), F32)]
    scratch = [
        pltpu.VMEM((4, 2, piece, width), BF16),
        pltpu.VMEM((4, 2, piece, width), BF16),
        pltpu.VMEM((3, 2, piece, width), BF16),
        pltpu.VMEM((2, piece, width), F32),
        pltpu.VMEM((2, piece, width), BF16),
        pltpu.VMEM((2, piece, width), BF16),
        pltpu.VMEM((2, piece, width), BF16),
        pltpu.SemaphoreType.DMA((10,)),
        pltpu.SemaphoreType.DMA((10,)),
    ]
    if with_grads:
        out_shape.append(jax.ShapeDtypeStruct(gathered.shape, BF16))
        scratch += [
            pltpu.VMEM((2, width, part), BF16),
            pltpu.VMEM((8, 2, piece, width), BF16),
            pltpu.SemaphoreType.DMA((2,)),
        ]
    got = pl.pallas_call(
        functools.partial(scatter_kernel, planes, len(lefts), transposed, with_grads),
        out_shape=out_shape,
        in_specs=in_specs,
        out_specs=[VMEM] * len(out_shape),
        scratch_shapes=scratch,
        cost_estimate=cost(55 if with_grads else 48),
        compiler_params=params(collective_id, 60 if with_grads else 44),
    )(*operands)
    return got if with_grads else got[0]


def rms_parts(values):
    scale = lax.rsqrt(jnp.mean(values * values, axis=-1, keepdims=True) + 1e-05)
    return (values * scale, scale)


def rms_back(grad_hat, normal, scale):
    return scale * (grad_hat - normal * jnp.mean(grad_hat * normal, axis=-1, keepdims=True))


def times(left, right):
    return jnp.dot(left, right, preferred_element_type=F32)


def times_t(left, right):
    return lax.dot_general(left, right, (((1,), (1,)), ((), ())), preferred_element_type=F32)


def t_times(left, right):
    return lax.dot_general(left, right, (((0,), (0,)), ((), ())), preferred_element_type=F32)


def adamw(weight, first_mom, second_mom, gradient, rate, decay):
    bias_one = 1.0 - 0.9**STEP
    bias_two = 1.0 - 0.95**STEP
    first_new = 0.9 * first_mom + 0.1 * gradient
    second_new = 0.95 * second_mom + 0.05 * gradient * gradient
    direction = first_new / bias_one / (jnp.sqrt(second_new / bias_two) + 1e-08)
    return (second_new, weight - rate * (direction + decay * weight))


def on_device(
    tokens,
    cotangent,
    norm_gains,
    in_proj,
    conv_taps,
    out_proj,
    gate_up,
    down_proj,
    first_gains,
    first_in,
    first_conv,
    first_out,
    first_gate_up,
    first_down,
    second_gains,
    second_in,
    second_conv,
    second_out,
    second_gate_up,
    second_down,
):
    planes = lax.axis_size("z")
    seqs, piece, width = tokens.shape
    rows = seqs * piece
    all_rows = 8 * rows
    own_d = in_proj.shape[0]
    own_f = down_proj.shape[0]
    ff = gate_up.shape[2]
    part_d = width // 8
    part_f = ff // 8

    in_send = in_proj.astype(BF16).reshape(own_d, 3, 4, planes, 2, own_d)
    in_send = in_send.transpose(2, 4, 0, 1, 3, 5).reshape(8, own_d, 3 * part_d)
    gu_send = gate_up.astype(BF16).reshape(2, own_d, 4, planes, 2, own_f)
    gu_send = gu_send.transpose(2, 4, 0, 1, 3, 5).reshape(8, 2, own_d, part_f)
    small = jnp.concatenate([norm_gains, conv_taps], axis=0)
    small_all, in_mine = share(small, in_send, planes, 0)

    def along_z(value):
        return lax.all_gather(value, "z", axis=0, tiled=False)

    in_t = along_z(in_mine).reshape(planes, 4, 2, own_d, 3 * part_d)
    in_t = in_t.transpose(1, 0, 2, 3, 4).reshape(width, 3 * part_d)
    down_t = along_z(down_proj.astype(BF16)).reshape(part_f, width)

    low = small_all.astype(BF16).astype(F32)
    gains = low[:, :, :2].reshape(4, 2, planes, 2, own_d).transpose(3, 0, 2, 1, 4)
    gains = gains.reshape(2, width)
    y, c, z, x = place()
    taps = lax.dynamic_index_in_dim(low[:, :, 2:], (y * 2 + c) * 2 + x, 0, keepdims=False)
    taps = taps.transpose(1, 0, 2).reshape(3, part_d)

    hidden = tokens.astype(F32).reshape(rows, width)
    hat_one, scale_one = rms_parts(hidden)
    normed = (hat_one * gains[0]).astype(BF16).reshape(seqs, piece, width)
    normed_all, gu_mine, out_t = early(planes, normed, gu_send, out_proj.astype(BF16), 1)
    normed_all = normed_all.reshape(all_rows, width)
    out_t = out_t.reshape(part_d, width)
    gu_t = along_z(gu_mine)
    in_tiles = own_d % 16 == 0
    if not in_tiles:
        gu_t = gu_t.reshape(planes, 4, 2, 2, own_d, part_f).transpose(3, 1, 0, 2, 4, 5)
        gu_t = gu_t.reshape(2, width, part_f)

    projected = times(normed_all, in_t)
    b_part = projected[:, :part_d]
    c_part = projected[:, part_d : 2 * part_d]
    x_part = projected[:, 2 * part_d :]
    lay = (2, 2, 2, seqs, piece, part_d)
    mixed_in = (b_part * x_part).reshape(lay)
    ends = mixed_in[..., piece - 2 :, :]
    before = lax.ppermute(ends[:, 1], "z", [(i, i + 1) for i in range(planes - 1)])
    arrived = jnp.stack([before, ends[:, 0]], axis=1)
    extended = jnp.concatenate([arrived, mixed_in], axis=-2)
    conv_out = (
        taps[0] * extended[..., :piece, :]
        + taps[1] * extended[..., 1 : piece + 1, :]
        + taps[2] * extended[..., 2:, :]
    )
    conv_out = conv_out.reshape(all_rows, part_d)
    gated = (c_part * conv_out).astype(BF16)

    def members(value):
        return value.reshape(8, seqs, piece, value.shape[-1])

    mixer = plane_scatter([members(gated)], [out_t], False, 2).reshape(rows, width)
    middle = hidden + mixer
    hat_two, scale_two = rms_parts(middle)
    normed_two = (hat_two * gains[1]).astype(BF16).reshape(seqs, piece, width)
    normed_two_all = plane_gather(normed_two, 3)
    active, dgate, dup, grad_down = ffn(planes, cotangent, normed_two_all, gu_t, down_t, 4)

    def sum_z(value):
        return lax.psum_scatter(value, "z", scatter_dimension=0, tiled=False)

    g_down = sum_z(grad_down)
    dnorm_two, grad_gu = plane_scatter([dgate, dup], None, True, 5, gu_t, normed_two_all)
    if not in_tiles:
        grad_gu = grad_gu.reshape(2, 4, planes, 2, own_d, part_f).transpose(2, 1, 3, 0, 4, 5)
        grad_gu = grad_gu.reshape(planes, 8, 2, own_d, part_f)
    grad_gu, g_down = lax.optimization_barrier((grad_gu, g_down))
    g_down = g_down.astype(F32)
    gu_back = sum_z(grad_gu)

    dnorm_two = dnorm_two.reshape(rows, width)
    gain_grad_two = jnp.sum(dnorm_two * hat_two, axis=0)
    cot_full = cotangent.astype(F32).reshape(rows, width)
    dmiddle = cot_full + rms_back(dnorm_two * gains[1], hat_two, scale_two)
    dmix = dmiddle.astype(BF16).reshape(seqs, piece, width)
    dmix_all = plane_gather(dmix, 6).reshape(all_rows, width)

    grad_out = t_times(gated, dmix_all)
    dgated = times_t(dmix_all, out_t)
    dc_part = dgated * conv_out
    dconv = (dgated * c_part).reshape(lay)
    grad_taps = jnp.stack(
        [
            jnp.sum(dconv * extended[..., k : piece + k, :], axis=(0, 1, 2, 3, 4))
            for k in range(3)
        ]
    )

    def padded(before, after):
        return jnp.pad(dconv, [(0, 0)] * 4 + [(before, after), (0, 0)])

    grad_ext = taps[0] * padded(0, 2) + taps[1] * padded(1, 1) + taps[2] * padded(2, 0)
    starts = grad_ext[..., :2, :]
    after = lax.ppermute(starts[:, 0], "z", [(i + 1, i) for i in range(planes - 1)])
    returned = jnp.stack([starts[:, 1], after], axis=1)
    returned = jnp.pad(returned, [(0, 0)] * 4 + [(piece - 2, 0), (0, 0)])
    grad_mixed = (grad_ext[..., 2:, :] + returned).reshape(all_rows, part_d)
    dproj = jnp.concatenate([grad_mixed * x_part, dc_part, grad_mixed * b_part], axis=-1)
    dproj = dproj.astype(BF16)
    grad_in = t_times(normed_all, dproj).astype(BF16)
    grad_in = grad_in.reshape(4, planes, 2, own_d, 3 * part_d).transpose(1, 0, 2, 3, 4)
    grad_in = grad_in.reshape(planes, 8, own_d, 3 * part_d)
    grad_out = grad_out.astype(BF16).reshape(planes, own_d, width)
    grad_in, gu_back, dproj = lax.optimization_barrier((grad_in, gu_back, dproj))
    in_back = sum_z(grad_in)
    taps_parts = grad_taps.reshape(3, planes, own_d).transpose(1, 0, 2)

    dnorm_one = plane_scatter([members(dproj)], [in_t], True, 7).reshape(rows, width)
    gain_grad_one = jnp.sum(dnorm_one * hat_one, axis=0)
    token_grad = dmiddle + rms_back(dnorm_one * gains[0], hat_one, scale_one)
    active, token_grad = lax.optimization_barrier((active, token_grad))
    branch = plane_scatter([active], [down_t], False, 8).reshape(rows, width)
    block_out = (middle + branch).astype(BF16)
    grad_gains = jnp.stack([gain_grad_one, gain_grad_two])
    gains_parts = grad_gains.reshape(2, 4, planes, 2, own_d).transpose(1, 3, 2, 0, 4)
    gains_parts = gains_parts.reshape(8, planes, 2, own_d)
    in_got, gu_got, sums, g_out = finish(
        planes, in_back, gu_back, gains_parts, taps_parts, grad_out, 9
    )
    g_gains, g_conv = sums[:2], sums[2:]
    g_in = in_got.reshape(4, 2, own_d, 3, planes, own_d).transpose(2, 3, 0, 4, 1, 5)
    g_in = g_in.reshape(own_d, 3 * width).astype(F32)
    g_gu = gu_got.reshape(4, 2, 2, own_d, planes, own_f).transpose(2, 3, 0, 4, 1, 5)
    g_gu = g_gu.reshape(2, own_d, ff).astype(F32)

    m_gains, u_gains = adamw(norm_gains, first_gains, second_gains, g_gains, 0.4, 0.0)
    m_in, u_in = adamw(in_proj, first_in, second_in, g_in, 0.02, 0.1)
    m_conv, u_conv = adamw(conv_taps, first_conv, second_conv, g_conv, 0.2, 0.1)
    m_out, u_out = adamw(out_proj, first_out, second_out, g_out, 0.02, 0.1)
    m_gu, u_gu = adamw(gate_up, first_gate_up, second_gate_up, g_gu, 0.02, 0.1)
    m_down, u_down = adamw(down_proj, first_down, second_down, g_down, 0.01, 0.1)
    return (
        block_out.reshape(seqs, piece, width),
        token_grad.reshape(seqs, piece, width),
        g_gains,
        g_in,
        g_conv,
        g_out,
        g_gu,
        g_down,
        m_gains,
        m_in,
        m_conv,
        m_out,
        m_gu,
        m_down,
        u_gains,
        u_in,
        u_conv,
        u_out,
        u_gu,
        u_down,
    )


def solution(mesh):
    lines = mesh.shape["seq"] // 2
    fine = Mesh(mesh.devices.reshape(2, 2, lines, 2), ("y", "core", "z", "x"))
    dp, seq = ("y", "core"), ("z", "x")
    every = dp + seq
    tokens = P(dp, seq, None)
    weights = (
        P(None, every),
        P(every, None),
        P(None, every),
        P(every, None),
        P(None, every, None),
        P(every, None),
    )
    return jax.shard_map(
        on_device,
        mesh=fine,
        in_specs=(tokens, tokens) + weights * 3,
        out_specs=(tokens, tokens) + weights * 3,
        check_vma=False,
    )
```

time: 969 us -> 722 us (0.75)
  matrix products: 183 us -> 35.1 us
  waiting for transfers between devices: 141 us -> 0.17 us
  Pallas kernels: 418 us -> 460 us
  blocking collectives: 33.4 us -> 0 us
  other arithmetic: 60.1 us -> 86.1 us
    reduce_scatter x4 -> x3, waiting for transfers between devices: 138 us -> 0.01 us  [sum_z(): return lax.psum_scatter(value, 'z', scatter_dimension=0, tiled=False)]
    dot_general x5 -> x1, matrix products: 75.3 us -> 10 us  [times_t(): lax.dot_general(left, right, (((1,), (1,)), ((), ())), preferred_element_...]
    dot_general x5 -> x2, matrix products: 58.1 us -> 15.7 us  [t_times(): lax.dot_general(left, right, (((0,), (0,)), ((), ())), preferred_element_...]
    pallas_call x11 -> x10, Pallas kernels: 418 us -> 460 us  [the longest x4 208 us: plane_scatter(): pl.pallas_call(functools.partial(scatter_kernel, planes, len(lefts), tran...]
    dot_general x5 -> x1, matrix products: 49.2 us -> 9.37 us  [times(): return jnp.dot(left, right, preferred_element_type=F32)]
    all_gather x1 -> x0, blocking collectives: 22.9 us -> none  [along_z(): return lax.all_gather(value, 'z', axis=0, tiled=False)]
    reshape x2 -> x5, local copies, waits for them, and re-layouts: 5.87 us -> 25.4 us  [the longest x2 12.3 us: on_device(): dconv = (dgated * c_part).reshape(lay)]
    dot_general x1 -> x0, local copies, waits for them, and re-layouts: 12.9 us -> none  [t_times(): lax.dot_general(left, right, (((0,), (0,)), ((), ())), preferred_element_...]
  transfers between devices with their start and end apart: 10 -> 8, of which waited for: 3 -> 0; matrix products, arithmetic and copies ran while one was open for 19% -> 23% of each run, Pallas kernels for 24% -> 43%
where the time goes in v2:
time: 722 us; the launch traced here: 714 us
  Pallas kernels  460 us (64%)
  local copies, waits for them, and re-layouts  112 us (16%)
  other arithmetic  86.1 us (12%)
  matrix products  35.1 us (5%)
  between operations  15.3 us (2%)
    pallas_call x4, Pallas kernels, plane_scatter(): pl.pallas_call(functools.partial(scatter_kernel, planes, len(lefts), tran...  208 us
    pallas_call x2, Pallas kernels, plane_gather(): pl.pallas_call(gather_kernel, out_shape=jax.ShapeDtypeStruct((8,) + own.s...  88.7 us
    pallas_call x1, Pallas kernels, early(): pl.pallas_call(functools.partial(early_kernel, planes), out_shape=[jax.Sh...  59.9 us
    pallas_call x1, Pallas kernels, ffn(): pl.pallas_call(functools.partial(ffn_kernel, planes), out_shape=[wide, wi...  59 us
    pallas_call x1, Pallas kernels, finish(): pl.pallas_call(functools.partial(finish_kernel, planes), out_shape=[jax.S...  29.1 us
    unnamed x127, local copies, waits for them, and re-layouts  17.7 us
    sub x6, other arithmetic, adamw(): return (second_new, weight - rate * (direction + decay * weight))  17.2 us
    dot_general x2, matrix products, t_times(): lax.dot_general(left, right, (((0,), (0,)), ((), ())), preferred_element_...  15.7 us
  transfers between devices with their start and end apart: 8, of which 0 were waited for; matrix products, arithmetic and copies ran while one was open for 23% of the time, Pallas kernels for 43%

profile of v2, /device:TPU:1, one launch (start us, length us, event | category | flops | bytes accessed | tf_op | source)
XLA Modules:
  0.0 714.0 jit_solution(17327219110309157298)
XLA Ops:
  12.1 15.6 %shard_map.347 = (f32[8,4,5,48]{3,2,1,0:T(8,128)}, bf16[8,48,576]{2,1,0:T(8,128)(2,1)}) custom-call(f32[5,48]{1,0:T(8,128)} %pad_maximum_fusion.3.own, bf16[8,48,576]{2,1,0:T(8,128)(2,1)} %reshape.290.block), custom_call_target="tpu_custom_call" | custom-call | flops 12000000000 | tf_op jit(solution)/shard_map/pallas_call | solution.py:328
  32.6 7.1 reshape.292
  47.7 59.9 %shard_map.348 = (bf16[8,2,192,1536]{3,2,1,0:T(8,128)(2,1)}, bf16[8,2,48,864]{3,2,1,0:T(8,128)(2,1)}, bf16[4,48,1536]{2,1,0:T(8,128)(2,1)}) custom-call(bf16[2,192,1536]{2,1,0:T(8,128)(2,1)} %fusion.13.own, bf16[8,2,48,864]{3,2,1,0:T(8,128)(2,1)} %reshape.293.block, bf16[48,1536]{1,0:T(8,128)(2,1)} %convert_element_type.91.out), custom_call_target="tpu_custom_call" | custom-call | flops 65000001536 | tf_op jit(solution)/shard_map/pallas_call | solution.py:219
  109.7 9.4 %fusion.32 = f32[3072,576]{0,1:T(8,128)S(1)} fusion(bf16[3072,1536]{1,0:T(8,128)(2,1)} %bitcast.124, bf16[1536,576]{1,0:T(8,128)(2,1)S(1)} %bitcast.98), kind=kOutput, calls=%fused_computation.86 | convolution fusion | flops 5435817984 | bytes 18284544 | tf_op jit(solution)/shard_map/dot_general | solution.py:720
  139.8 12.0 %multiply_add_fusion.1 = f32[2,2,2,2,192,192]{4,3,2,1,0,5:T(2,128)} fusion(f32[2,2,2,2,192,192]{4,3,2,1,0,5:T(2,128)S(1)} %reshape.297, f32[192]{0:T(256)S(1)} %mul.443, f32[192]{0:T(256)S(1)} %mul.440, f32[192]{0:T(256)S(1)} %mul.436, f32[2,2,2,2,2,192]{4,3,2,1,0,5:T(2,128)} %copy.95), kind=kLoop, calls=%fused_computation.10 | loop fusion | flops 4128768 | bytes 4745472 | tf_op jit(solution)/shard_map/add | solution.py:816
  160.7 45.9 %shard_map.349 = f32[2,192,1536]{2,1,0:T(8,128)S(1)} custom-call(bf16[8,2,192,192]{3,2,1,0:T(8,128)(2,1)S(1)} %bitcast.100, bf16[192,1536]{1,0:T(8,128)(2,1)S(1)} %bitcast.101), custom_call_target="tpu_custom_call" | custom-call | flops 48000000000 | tf_op jit(solution)/shard_map/pallas_call | solution.py:698
  210.1 44.3 %shard_map.350.normed.refs_3_ = bf16[8,2,192,1536]{3,2,1,0:T(8,128)(2,1)} custom-call(bf16[2,192,1536]{2,1,0:T(8,128)(2,1)} %multiply_convert_fusion.3.own), custom_call_target="tpu_custom_call" | custom-call | flops 44999999488 | tf_op jit(solution)/shard_map/pallas_call | solution.py:207
  254.5 59.0 %shard_map.351 = (bf16[8,2,192,864]{3,2,1,0:T(8,128)(2,1)}, bf16[8,2,192,864]{3,2,1,0:T(8,128)(2,1)}, bf16[8,2,192,864]{3,2,1,0:T(8,128)(2,1)}, bf16[4,216,1536]{2,1,0:T(8,128)(2,1)}) custom-call(bf16[2,192,1536]{2,1,0:T(8,128)(2,1)} %cot.1, bf16[8,2,192,1536]{3,2,1,0:T(8,128)(2,1)} %shard_map.350.normed.refs_3_, bf16[4,8,2,48,864]{4,3,2,1,0:T(8,128)(2,1)} %bitcast.120, ...), custom_call_target="tpu_custom_call" | custom-call | flops 54999998464 | tf_op jit(solution)/shard_map/pallas_call | solution.py:504
  313.7 65.1 %shard_map.352 = (f32[2,192,1536]{2,1,0:T(8,128)}, bf16[4,8,2,48,864]{4,3,2,1,0:T(8,128)(2,1)}) custom-call(bf16[8,2,192,864]{3,2,1,0:T(8,128)(2,1)} %get-tuple-element.48.refs_0_, bf16[8,2,192,864]{3,2,1,0:T(8,128)(2,1)} %get-tuple-element.49.refs_1_, bf16[4,8,2,48,864]{4,3,2,1,0:T(8,128)(2,1)} %bitcast.121, bf16[8,2,192,1536]{3,2,1,0:T(8,128)(2,1)} %shard_map.350.normed.refs_3_), custom_call_target="tpu_custom_call" | custom-call | flops 54999998464 | tf_op jit(solution)/shard_map/pallas_call | solution.py:698
  383.6 44.4 %shard_map.353 = bf16[8,2,192,1536]{3,2,1,0:T(8,128)(2,1)} custom-call(bf16[2,192,1536]{2,1,0:T(8,128)(2,1)} %add_convert_fusion.1.own), custom_call_target="tpu_custom_call" | custom-call | flops 44999999488 | tf_op jit(solution)/shard_map/pallas_call | solution.py:207
  428.0 10.0 %multiply_reduce_fusion.2 = (f32[192]{0:T(256)S(1)}, f32[3072,192]{0,1:T(8,128)}, bf16[3072,192]{0,1:T(8,128)(2,1)}) fusion(f32[3072,192]{0,1:T(8,128)S(1)} %copy-done.17, f32[3072,576]{0,1:T(8,128)} %copy-done.16, f32[3072,192]{0,1:T(8,128)} %copy-done.18, bf16[3072,1536]{1,0:T(8,128)(2,1)} %bitcast.104, bf16[192,1536]{1,0:T(8,128)(2,1)S(1)} %bitcast.102), kind=kOutput, calls=%fused_computation.38 | convolution fusion | flops 1814888192 | bytes 20644608 | tf_op jit(solution)/shard_map/dot_general | solution.py:724
  438.0 5.4 reshape.307
  443.4 6.9 copy.97
  450.3 15.4 %multiply_reduce_fusion.1 = (f32[192]{0:T(256)S(1)}, f32[192]{0:T(256)S(1)}) fusion(f32[2,2,2,2,192,192]{4,3,2,1,0,5:T(2,128)} %reshape.307, f32[2,2,2,2,192,192]{4,3,2,1,0,5:T(2,128)S(1)} %copy-done.12, f32[2,2,2,2,2,192]{4,3,2,1,0,5:T(2,128)} %copy.95), kind=kLoop, calls=%fused_computation.9 | loop fusion | flops 3538560 | bytes 4744704 | tf_op jit(solution)/shard_map/reduce_sum | solution.py:858
  472.6 6.5 convolution_convert_fusion.1
  483.3 5.4 copy.100
  498.4 9.1 %convolution_convert_fusion = bf16[1536,576]{0,1:T(8,128)(2,1)} fusion(bf16[3072,1536]{1,0:T(8,128)(2,1)} %bitcast.125, bf16[3072,192]{0,1:T(8,128)(2,1)S(1)} %get-tuple-element.93, bf16[3072,192]{0,1:T(8,128)(2,1)S(1)} %copy-done.23, bf16[3072,192]{0,1:T(8,128)(2,1)S(1)} %get-tuple-element.92), kind=kOutput, calls=%fused_computation.11 | convolution fusion | flops 5447319552 | bytes 14745600 | tf_op jit(solution)/shard_map/dot_general | solution.py:728
  518.5 6.2 copy.103
  526.8 46.7 %shard_map.354 = f32[2,192,1536]{2,1,0:T(8,128)S(1)} custom-call(bf16[8,2,192,576]{3,2,1,0:T(8,128)(2,1)S(1)} %bitcast.97, bf16[1536,576]{1,0:T(8,128)(2,1)S(1)} %bitcast.99), custom_call_target="tpu_custom_call" | custom-call | flops 48000000000 | tf_op jit(solution)/shard_map/pallas_call | solution.py:698
  581.7 5.8 fusion.4
  587.5 50.1 %shard_map.355 = f32[2,192,1536]{2,1,0:T(8,128)S(1)} custom-call(bf16[8,2,192,864]{3,2,1,0:T(8,128)(2,1)} %get-tuple-element.55.refs_0_, bf16[864,1536]{1,0:T(8,128)(2,1)S(1)} %copy-done.7), custom_call_target="tpu_custom_call" | custom-call | flops 48000000000 | tf_op jit(solution)/shard_map/pallas_call | solution.py:698
  638.9 29.1 %shard_map.356 = (bf16[8,48,576]{2,1,0:T(8,128)(2,1)}, bf16[8,2,48,864]{3,2,1,0:T(8,128)(2,1)}, f32[5,48]{1,0:T(8,128)}, f32[48,1536]{1,0:T(8,128)}) custom-call(bf16[8,48,576]{2,1,0:T(8,128)(2,1)} %bitcast.123, bf16[8,2,48,864]{3,2,1,0:T(8,128)(2,1)} %bitcast.122, f32[8,4,2,48]{3,2,1,0:T(2,128)} %bitcast.116, f32[4,3,48]{2,1,0:T(4,128)} %maximum_bitcast_fusion.1.taps, ...), custom_call_target="tpu_custom_call" | custom-call | flops 24999999488 | tf_op jit(solution)/shard_map/pallas_call | solution.py:275
  676.2 5.5 reshape.317
  696.3 7.8 %multiply_subtract_fusion = (f32[2,48,6912]{2,1,0:T(8,128)}, f32[2,48,6912]{2,1,0:T(8,128)}) fusion(f32[2,48,6912]{2,1,0:T(8,128)S(1)} %copy-done.20, f32[2,48,6912]{2,1,0:T(8,128)} %reshape.317, f32[2,48,6912]{2,1,0:T(8,128)} %param.32, f32[2,48,6912]{2,1,0:T(8,128)} %param.38), kind=kLoop, calls=%fused_computation.13 | loop fusion | flops 9953280 | bytes 15925248 | tf_op jit(solution)/shard_map/sub | solution.py:737
  (222 shorter events, 126.1 us)
Async XLA Ops:
  7.2 100.7 %all-gather.7.cloned.1.call-start = ((), (), s32[]{:S(2)}) async-start(), calls=%async_computation.6 | async-start | bytes 2457600 | tf_op jit(solution)/shard_map/all_gather | solution.py:780
  27.8 226.7 %all-gather.11.cloned.1.call-start = ((), (), s32[]{:S(2)}) async-start(), calls=%async_computation.8 | async-start | bytes 3317760 | tf_op jit(solution)/shard_map/all_gather | solution.py:780
  28.7 225.7 %all-gather.9.cloned.1.call-start = ((), (), s32[]{:S(2)}) async-start(), calls=%async_computation.7 | async-start | bytes 6881280 | tf_op jit(solution)/shard_map/all_gather | solution.py:780
  29.3 17.0 %copy-start.43 = (f32[1536]{0:T(1024)}, f32[1536]{0:T(1024)S(1)}, u32[]{:S(2)}) copy-start(f32[1536]{0:T(1024)S(1)} %mul.431) | copy-start | bytes 18436
  29.6 105.6 %copy-start.48 = (f32[2,192]{1,0:T(2,128)}, f32[2,192]{1,0:T(2,128)S(1)}, u32[]{:S(2)}) copy-start(f32[2,192]{1,0:T(2,128)S(1)} %add_rsqrt_fusion.1) | copy-start | bytes 4612
  107.6 275.5 %reduce-scatter.4.cloned.1.call-start = ((), (), s32[]{:S(2)}) async-start(), calls=%async_computation.3 | async-start | bytes 3317760 | tf_op jit(solution)/shard_map/reduce_scatter | solution.py:834
  132.6 5.0 collective-permute-start
  135.9 15.8 %copy-start.50 = (f32[192]{0:T(256)}, f32[192]{0:T(256)S(1)}, u32[]{:S(2)}) copy-start(f32[192]{0:T(256)S(1)} %mul.436) | copy-start | bytes 2308
  136.0 15.7 %copy-start.52 = (f32[192]{0:T(256)}, f32[192]{0:T(256)S(1)}, u32[]{:S(2)}) copy-start(f32[192]{0:T(256)S(1)} %mul.440) | copy-start | bytes 2308
  136.2 72.7 %copy-start.41 = (f32[1536]{0:T(1024)}, f32[1536]{0:T(1024)S(1)}, u32[]{:S(2)}) copy-start(f32[1536]{0:T(1024)S(1)} %mul.450) | copy-start | bytes 18436
  160.7 45.9 %copy-start.14 = (bf16[2,192,1536]{2,1,0:T(8,128)(2,1)S(1)}, bf16[2,192,1536]{2,1,0:T(8,128)(2,1)}, u32[]{:S(2)}) copy-start(bf16[2,192,1536]{2,1,0:T(8,128)(2,1)} %param.20) | copy-start | bytes 3538948
  208.0 46.4 %copy-start.8 = (f32[2,192,1536]{2,1,0:T(8,128)}, f32[2,192,1536]{2,1,0:T(8,128)S(1)}, u32[]{:S(2)}) copy-start(f32[2,192,1536]{2,1,0:T(8,128)S(1)} %get-tuple-element.91) | copy-start | bytes 7077892
  208.0 46.4 %copy-start.46 = (f32[2,192]{1,0:T(2,128)}, f32[2,192]{1,0:T(2,128)S(1)}, u32[]{:S(2)}) copy-start(f32[2,192]{1,0:T(2,128)S(1)} %add_rsqrt_fusion) | copy-start | bytes 4612
  313.6 204.9 %reduce-scatter.6.cloned.1.call-start = ((), (), s32[]{:S(2)}) async-start(), calls=%async_computation.4 | async-start | bytes 6881280 | tf_op jit(solution)/shard_map/reduce_scatter | solution.py:834
  313.6 65.1 %copy-start.9 = (f32[2,192,1536]{2,1,0:T(8,128)S(1)}, f32[2,192,1536]{2,1,0:T(8,128)}, u32[]{:S(2)}) copy-start(f32[2,192,1536]{2,1,0:T(8,128)} %copy-done.8) | copy-start | bytes 7077892
  313.6 65.1 %copy-start.42 = (f32[1536]{0:T(1024)S(1)}, f32[1536]{0:T(1024)}, u32[]{:S(2)}) copy-start(f32[1536]{0:T(1024)} %copy-done.41) | copy-start | bytes 18436
  313.6 65.1 %copy-start.47 = (f32[2,192]{1,0:T(2,128)S(1)}, f32[2,192]{1,0:T(2,128)}, u32[]{:S(2)}) copy-start(f32[2,192]{1,0:T(2,128)} %copy-done.46) | copy-start | bytes 4612
  383.1 44.8 %copy-start.17 = (f32[3072,192]{0,1:T(8,128)S(1)}, f32[3072,192]{0,1:T(8,128)}, u32[]{:S(2)}) copy-start(f32[3072,192]{0,1:T(8,128)} %slice_multiply_fusion) | copy-start | bytes 7077892
  383.1 255.8 %reduce-scatter.8.cloned.1.call-start = ((), (), s32[]{:S(2)}) async-start(), calls=%async_computation.5 | async-start | bytes 2457600 | tf_op jit(solution)/shard_map/reduce_scatter | solution.py:834
  471.2 10.0 %collective-permute-start.1 = (f32[2,2,2,2,192]{4,3,2,1,0:T(2,128)S(1)}, f32[2,2,2,2,192]{4,3,2,1,0:T(2,128)S(1)}, u32[]{:S(2)}, u32[]{:S(2)}) collective-permute-start(f32[2,2,2,2,192]{4,3,2,1,0:T(2,128)S(1)} %get-tuple-element.95), channel_id=1, source_target_pairs={{2,0},{4,2},{6,4},{3,1},{5,3},{7,5},{10,8},{12,10},{14,12},{11,9},... | collective-permute-start | bytes 36872 | tf_op jit(solution)/shard_map/ppermute | solution.py:868
  526.8 48.1 %copy-start.15 = (bf16[2,192,1536]{2,1,0:T(8,128)(2,1)S(1)}, bf16[2,192,1536]{2,1,0:T(8,128)(2,1)}, u32[]{:S(2)}) copy-start(bf16[2,192,1536]{2,1,0:T(8,128)(2,1)} %param.20) | copy-start | bytes 3538948
  526.8 48.1 %copy-start.44 = (f32[1536]{0:T(1024)S(1)}, f32[1536]{0:T(1024)}, u32[]{:S(2)}) copy-start(f32[1536]{0:T(1024)} %copy-done.43) | copy-start | bytes 18436
  526.8 48.1 %copy-start.49 = (f32[2,192]{1,0:T(2,128)S(1)}, f32[2,192]{1,0:T(2,128)}, u32[]{:S(2)}) copy-start(f32[2,192]{1,0:T(2,128)} %copy-done.48) | copy-start | bytes 4612
  587.5 50.1 %copy-start.10 = (f32[2,192,1536]{2,1,0:T(8,128)S(1)}, f32[2,192,1536]{2,1,0:T(8,128)}, u32[]{:S(2)}) copy-start(f32[2,192,1536]{2,1,0:T(8,128)} %copy-done.8) | copy-start | bytes 7077892
  (46 other events, 269.3 us)
Sparse Core Ops, SparseCore 0:
  27.9 54.5 all-gather.6
  84.7 54.0 all-gather.10
  140.3 101.6 all-gather.8
  313.7 52.4 reduce-scatter.3
  383.2 96.6 reduce-scatter.5
  579.2 41.6 reduce-scatter.7

commit v3 on v2

--- a/solution.py
+++ b/solution.py
@@ -140,6 +140,57 @@
 
 def line_peers(planes):
     return [{"z": lax.rem(lax.axis_index("z") + d, planes)} for d in range(1, planes)]
+
+
+class Line:
+    def __init__(self, planes, own, full, send, recv, local):
+        self.planes, self.own, self.full, self.send, self.recv = planes, own, full, send, recv
+        self.mine = pltpu.make_async_copy(own, full.at[lax.axis_index("z")], local)
+
+    def ways(self):
+        z, planes = lax.axis_index("z"), self.planes
+        return (
+            (0, 1, z, planes - 1 - z),
+            (1, planes - 1, planes - 1 - z, z),
+        )
+
+    def pass_on(self, d):
+        z, planes = lax.axis_index("z"), self.planes
+        for way, by, come, left in self.ways():
+            block = lax.rem(z + d * (planes - by) + planes, planes)
+
+            @pl.when(jnp.logical_and(come >= d, left >= 1))
+            def _():
+                src = self.own if d == 0 else self.full.at[block]
+                device = {"z": lax.rem(z + by, planes)}
+                sem = self.send.at[way, d], self.recv.at[way, d]
+                remote(src, self.full.at[block], *sem, device).start()
+
+    def start(self):
+        self.mine.start()
+        self.pass_on(0)
+
+    def arrived(self, d):
+        for way, _, come, _ in self.ways():
+
+            @pl.when(come >= d)
+            def _():
+                pltpu.make_async_copy(self.own, self.own, self.recv.at[way, d - 1]).wait()
+
+    def step(self, d):
+        self.arrived(d)
+        self.pass_on(d)
+
+    def finish(self):
+        self.arrived(self.planes - 1)
+        for d in range(self.planes - 1):
+            for way, _, come, left in self.ways():
+
+                @pl.when(jnp.logical_and(come >= d, left >= 1))
+                def _():
+                    pltpu.make_async_copy(self.own, self.own, self.send.at[way, d]).wait()
+
+        self.mine.wait()
 
 
 def gather_kernel(own, full, send, recv, local):
@@ -157,37 +208,104 @@
     mine.wait()
 
 
+def by_owner(planes):
+    for owner in range(8 * planes):
+        yield owner, owner // (2 * planes) * 2 + owner % 2, owner // 2 % planes
+
+
 def early_kernel(
     planes,
-    own,
-    block,
-    out,
+    small,
+    tokens,
+    in_proj,
+    gate_up,
+    out_proj,
     full,
-    got,
+    gu_got,
+    ins,
     outs,
+    gains,
+    taps,
+    in_block,
+    in_got,
+    gu_block,
+    out_block,
+    line,
+    smalls,
     send,
     recv,
+    send_i,
+    recv_i,
+    send_g,
+    recv_g,
     send_s,
     recv_s,
     send_z,
     recv_z,
+    send_l,
+    recv_l,
     local,
 ):
-    y, c, _, x = place()
+    y, c, z, x = place()
+    me = (y * 2 + c) * 2 + x
+    own = small.shape[1]
     meet(others() + line_peers(planes))
-    copies = along_line(planes, out, outs, send_z, recv_z, local.at[0])
-    gather = Gather(own, full, send, recv)
+    tiny = along_line(planes, small, line, send_z, recv_z, local.at[0])
+    out_block[...] = out_proj[...].astype(BF16)
+    out_line = Line(planes, out_block, outs, send_l.at[1], recv_l.at[1], local.at[4])
+    out_line.start()
+    for k in range(3):
+        for owner, member, zz in by_owner(planes):
+            start, to = (k * 8 * planes + owner) * own, (k * planes + zz) * own
+            block = in_proj[:, start : start + own].astype(BF16)
+            in_block[member, :, to : to + own] = block
+    in_copies = swap(in_block, in_got, send_i, recv_i, local.at[1])
+    gather = Gather(tokens, full, send, recv)
     gather.first()
-    mine = pltpu.make_async_copy(own, full.at[(y * 2 + x) * 2 + c], local.at[1])
+    mine = pltpu.make_async_copy(tokens, full.at[(y * 2 + x) * 2 + c], local.at[2])
     mine.start()
-    copies += [mine] + swap(block, got, send_s, recv_s, local.at[2])
+    for copy in tiny:
+        copy.wait()
+    tiny = []
+    for f, peer in enumerate(others()):
+        tiny.append(remote(line, smalls.at[me], send_s.at[f], recv_s.at[f], peer))
+    tiny.append(pltpu.make_async_copy(line, smalls.at[me], local.at[0]))
+    for copy in tiny:
+        copy.start()
+    for copy in in_copies:
+        copy.wait()
+    ahead = Line(planes, in_got, ins, send_l.at[0], recv_l.at[0], local.at[1])
+    ahead.start()
+    if planes > 2:
+        out_line.step(1)
+    wide = gate_up.shape[2] // (8 * planes)
+    for j in (0, 1):
+        for owner, member, zz in by_owner(planes):
+            block = gate_up[j, :, owner * wide : (owner + 1) * wide].astype(BF16)
+            gu_block[member, j, :, zz * wide : (zz + 1) * wide] = block
+    gu_copies = swap(gu_block, gu_got, send_g, recv_g, local.at[3])
+    for copy in tiny:
+        copy.wait()
+    for owner, member, zz in by_owner(planes):
+        row = smalls[member, zz, 0:2, :].astype(BF16).astype(F32)
+        gains[:, owner * own : (owner + 1) * own] = row
+    for zz in range(planes):
+        row = line[zz, 2:5, :].astype(BF16).astype(F32)
+        taps[:, zz * own : (zz + 1) * own] = row
+    ahead.step(1)
     gather.forward()
+    for d in range(2, planes - 1):
+        out_line.step(d)
+        ahead.step(d)
     gather.second()
     gather.last()
     gather.arrived(*range(6, 14))
     gather.sent()
-    for copy in copies:
+    for copy in gu_copies:
         copy.wait()
+    mine.wait()
+    ahead.finish()
+    out_line.finish()
 
 
 def params(collective_id, vmem=0):
@@ -215,22 +333,46 @@
     )(own)
 
 
-def early(planes, own, block, out, collective_id):
+def early(planes, small, tokens, in_proj, gate_up, out_proj, collective_id):
+    own, width = out_proj.shape
+    in_block = (8, own, in_proj.shape[1] // 8)
+    gu_block = (8, 2, own, gate_up.shape[2] // 8)
     return pl.pallas_call(
         functools.partial(early_kernel, planes),
         out_shape=[
-            jax.ShapeDtypeStruct((8,) + own.shape, own.dtype),
-            jax.ShapeDtypeStruct(block.shape, block.dtype),
-            jax.ShapeDtypeStruct((planes,) + out.shape, out.dtype),
+            jax.ShapeDtypeStruct((8,) + tokens.shape, BF16),
+            jax.ShapeDtypeStruct(gu_block, BF16),
+            jax.ShapeDtypeStruct((planes,) + in_block, BF16),
+            jax.ShapeDtypeStruct((planes, own, width), BF16),
+            jax.ShapeDtypeStruct((2, width), F32),
+            jax.ShapeDtypeStruct((3, planes * own), F32),
         ],
-        in_specs=[ANY] * 3,
-        out_specs=[ANY] * 3,
+        in_specs=[VMEM, ANY, VMEM, VMEM, VMEM],
+        out_specs=[ANY] * 4 + [VMEM] * 2,
         scratch_shapes=[
-            sems(14), sems(14), sems(7), sems(7), sems(planes - 1), sems(planes - 1), sems(3)
+            pltpu.VMEM(in_block, BF16),
+            pltpu.VMEM(in_block, BF16),
+            pltpu.VMEM(gu_block, BF16),
+            pltpu.VMEM((own, width), BF16),
+            pltpu.VMEM((planes,) + small.shape, F32),
+            pltpu.VMEM((8, planes) + small.shape, F32),
+            sems(14),
+            sems(14),
+            sems(7),
+            sems(7),
+            sems(7),
+            sems(7),
+            sems(7),
+            sems(7),
+            sems(planes - 1),
+            sems(planes - 1),
+            sems(2, 2, planes - 1),
+            sems(2, 2, planes - 1),
+            sems(5),
         ],
-        cost_estimate=cost(65),
-        compiler_params=params(collective_id),
-    )(own, block, out)
+        cost_estimate=cost(70),
+        compiler_params=params(collective_id, 40),
+    )(small, tokens, in_proj, gate_up, out_proj)
 
 
 def finish_kernel(planes, ins, gus, gains, taps, outs, ins_got, gus_got, sums, out_sum, *scratch):
@@ -302,52 +444,6 @@
     )(ins, gus, gains, taps, outs)
 
 
-def share_kernel(
-    planes, own, block, full, got, line, send, recv, send_z, recv_z, local, send_s, recv_s
-):
-    y, c, _, x = place()
-    meet(others() + line_peers(planes))
-    me = (y * 2 + c) * 2 + x
-    copies = along_line(planes, own, line, send_z, recv_z, local.at[0])
-    swapped = swap(block, got, send_s, recv_s, local.at[1])
-    for copy in copies:
-        copy.wait()
-    copies = []
-    for f, peer in enumerate(others()):
-        copy = remote(line, full.at[me], send.at[f], recv.at[f], peer)
-        copy.start()
-        copies.append(copy)
-    mine = pltpu.make_async_copy(line, full.at[me], local.at[0])
-    mine.start()
-    for copy in copies + swapped:
-        copy.wait()
-    mine.wait()
-
-
-def share(own, block, planes, collective_id):
-    return pl.pallas_call(
-        functools.partial(share_kernel, planes),
-        out_shape=[
-            jax.ShapeDtypeStruct((8, planes) + own.shape, own.dtype),
-            jax.ShapeDtypeStruct(block.shape, block.dtype),
-        ],
-        in_specs=[VMEM, ANY],
-        out_specs=[VMEM, ANY],
-        scratch_shapes=[
-            pltpu.VMEM((planes,) + own.shape, own.dtype),
-            pltpu.SemaphoreType.DMA((7,)),
-            pltpu.SemaphoreType.DMA((7,)),
-            pltpu.SemaphoreType.DMA((planes - 1,)),
-            pltpu.SemaphoreType.DMA((planes - 1,)),
-            pltpu.SemaphoreType.DMA((2,)),
-            pltpu.SemaphoreType.DMA((7,)),
-            pltpu.SemaphoreType.DMA((7,)),
-        ],
-        cost_estimate=cost(12),
-        compiler_params=params(collective_id),
-    )(own, block)
-
-
 def load_rows(planes, gathered, rows, sem):
     if len(gathered.shape) == 3:
         copy = pltpu.make_async_copy(gathered, rows, sem)
@@ -371,11 +467,15 @@
     cot,
     normed,
     gathered,
-    down,
+    down_most,
+    down_own,
     act_out,
     dgate_out,
     dup_out,
     grad_out,
+    down,
+    down_rest,
+    down_rows,
     full,
     near,
     weights,
@@ -388,16 +488,20 @@
     local,
     near_sem,
     out_sem,
+    send_l,
+    recv_l,
 ):
     y, c, _, x = place()
     piece, width = cot.shape[1:]
     part = down.shape[0]
+    most = down_most.shape[1]
     chip_rows = 4 * piece
     half = 2 * piece
     chips = [flip(y, dy) * 2 + flip(x, dx) for dy, dx in ((0, 0), (0, 1), (1, 0), (1, 1))]
     loads = load_rows(planes, gathered, weights, local.at[0])
     mine = pltpu.make_async_copy(cot, full.at[(y * 2 + x) * 2 + c], local.at[1])
     mine.start()
+    first_part = pltpu.make_async_copy(down_most, down.at[:, pl.ds(0, most)], local.at[2])
 
     def fetch(k):
         copy = pltpu.make_async_copy(
@@ -407,7 +511,10 @@
         return copy
 
     fetched = {0: fetch(0), 1: fetch(1)}
-    meet(neighbours())
+    first_part.start()
+    meet(neighbours() + list(ring()))
+    ahead = Line(planes, down_own, down_rest, send_l, recv_l, local.at[3])
+    ahead.start()
     gather = Gather(cot, full, send, recv)
     gather.first()
     for copy in loads:
@@ -476,18 +583,28 @@
         lax.fori_loop(0, 3, sum_up, 0)
 
     gate_up(0, 0)
+    if planes > 2:
+        ahead.step(1)
+    gate_up(1, 1)
+    for d in range(2, planes - 1):
+        ahead.step(d)
+    gather.forward()
+    gate_up(2, 2)
     mine.wait()
     gather.arrived(6, 7)
+    first_part.wait()
+    ahead.finish()
+    for zz in range(planes):
+        count = part // planes
+        down_rows[zz * count : (zz + 1) * count, :] = down_rest[zz].astype(F32)
+    down[:, most:] = down_rows[...].astype(BF16)
     back(0, 0)
-    gather.forward()
-    gate_up(1, 0)
-    gate_up(2, 1)
     gather.second()
     gather.arrived(8, 9)
-    back(1, 0)
+    back(1, 1)
     gate_up(3, 0)
     gather.arrived(10, 11)
-    back(2, 1)
+    back(2, 2)
     gather.last()
     gather.arrived(12, 13)
     back(3, 0)
@@ -497,58 +614,65 @@
             copy.wait()
 
 
-def ffn(planes, cot, normed, gathered, down, collective_id):
+def ffn(planes, cot, normed, gathered, down_most, down_own, collective_id):
     _, piece, width = cot.shape
-    part = down.shape[0]
+    part, most = down_most.shape
+    rest = width - most
     wide = jax.ShapeDtypeStruct((8, 2, piece, part), BF16)
     return pl.pallas_call(
         functools.partial(ffn_kernel, planes),
-        out_shape=[wide, wide, wide, jax.ShapeDtypeStruct((planes, part // planes, width), BF16)],
-        in_specs=[ANY, ANY, ANY, VMEM],
-        out_specs=[ANY, ANY, ANY, VMEM],
+        out_shape=[
+            wide,
+            wide,
+            wide,
+            jax.ShapeDtypeStruct((planes, part // planes, width), BF16),
+            jax.ShapeDtypeStruct((part, width), BF16),
+        ],
+        in_specs=[ANY] * 5,
+        out_specs=[ANY, ANY, ANY, VMEM, VMEM],
         scratch_shapes=[
+            pltpu.VMEM((planes, part // planes, rest), BF16),
+            pltpu.VMEM((part, rest), F32),
             pltpu.VMEM((8, 2, piece, width), BF16),
             pltpu.VMEM((2, 2, 2, piece, width), BF16),
             pltpu.VMEM((2, width, part), BF16),
-            pltpu.VMEM((2, 4 * piece, part), F32),
-            pltpu.VMEM((2, 4 * piece, part), F32),
+            pltpu.VMEM((3, 4 * piece, part), F32),
+            pltpu.VMEM((3, 4 * piece, part), F32),
             pltpu.VMEM((2, 3, 2, 2, piece, part), BF16),
             pltpu.VMEM((part, width), F32),
-            pltpu.SemaphoreType.DMA((14,)),
-            pltpu.SemaphoreType.DMA((14,)),
-            pltpu.SemaphoreType.DMA((2,)),
-            pltpu.SemaphoreType.DMA((2,)),
-            pltpu.SemaphoreType.DMA((2, 3)),
+            sems(14),
+            sems(14),
+            sems(4),
+            sems(2),
+            sems(2, 3),
+            sems(2, planes - 1),
+            sems(2, planes - 1),
         ],
         cost_estimate=cost(55),
-        compiler_params=params(collective_id, 60),
-    )(cot, normed, gathered, down)
-
-
-def scatter_kernel(planes, pairs, transposed, with_grads, *refs):
-    refs = list(refs)
-    lefts = [refs.pop(0) for _ in range(pairs)]
-    if with_grads:
-        gathered, normed = refs.pop(0), refs.pop(0)
-        out, grads = refs.pop(0), refs.pop(0)
-    else:
-        rights = [refs.pop(0) for _ in range(pairs)]
-        out = refs.pop(0)
-    staged, held, ready, keep, diag, from_x, from_y, send, recv = refs[:9]
-    if with_grads:
-        weights, every, local = refs[9:]
-        rights = [weights.at[j] for j in range(pairs)]
-        loads = load_rows(planes, gathered, weights, local.at[0])
-        whole = pltpu.make_async_copy(normed, every, local.at[1])
-        whole.start()
+        compiler_params=params(collective_id, 62),
+    )(cot, normed, gathered, down_most, down_own)
+
+
+def room(piece, width):
+    return [
+        pltpu.VMEM((4, 2, piece, width), BF16),
+        pltpu.VMEM((4, 2, piece, width), BF16),
+        pltpu.VMEM((3, 2, piece, width), BF16),
+        pltpu.VMEM((2, piece, width), F32),
+        pltpu.VMEM((2, piece, width), BF16),
+        pltpu.VMEM((2, piece, width), BF16),
+        pltpu.VMEM((2, piece, width), BF16),
+        sems(10),
+        sems(10),
+    ]
+
+
+def scatter(lefts, rights, transposed, out, scratch, fills=()):
+    staged, held, ready, keep, diag, from_x, from_y, send, recv = scratch
     y, c, _, x = place()
     _, piece, width = out.shape
     rows = 2 * piece
     tile = width // 3
-    meet(neighbours())
-    if with_grads:
-        for copy in loads:
-            copy.wait()
     copies = []
 
     def go(src, dst, sem, device):
@@ -622,16 +746,108 @@
     y_zero = go(ready.at[2, 0], from_y.at[0], 7, {"y": 1 - y})
     to_other_core(3)
     own_core(3, store_own)
-
+    if fills:
+        fills[0]()
+    diag_y.wait_recv()
+    ready[1, 0] = (keep[0] + diag[0].astype(F32)).astype(BF16)
+    x_zero = go(ready.at[1, 0], from_x.at[0], 8, {"x": 1 - x})
+    diag_x.wait_recv()
+    ready[2, 1] = (keep[1] + diag[1].astype(F32)).astype(BF16)
+    y_one = go(ready.at[2, 1], from_y.at[1], 9, {"y": 1 - y})
+    if fills:
+        fills[1]()
+    for i, (one, two) in enumerate(((x_zero, y_zero), (x_one, y_one))):
+        one.wait_recv()
+        two.wait_recv()
+        out[i] += from_x[i].astype(F32) + from_y[i].astype(F32)
+    for copy in copies:
+        copy.wait_send()
+
+
+def by_rows(piece, work):
+    step = 16
+
+    def body(n, _):
+        rows = pl.ds(pl.multiple_of(n * step, step), step)
+        for i in (0, 1):
+            work(i, rows)
+        return 0
+
+    lax.fori_loop(0, piece // step, body, 0)
+
+
+def norm_back(i, rows, source, gain, grad, base, sums):
+    normal, scale = rms_parts(source)
+    term = grad * normal
+    sums[...] += term[:8] + term[8:]
+    return base + rms_back(grad * gain, normal, scale)
+
+
+def last_kernel(left, right, tokens, dmiddle, gain, token_grad, sums, out, *scratch):
+    meet(neighbours())
+    scatter([left], [right], True, out, scratch)
+    sums[...] = jnp.zeros_like(sums)
+
+    def work(i, rows):
+        source = tokens[i, rows, :].astype(F32)
+        token_grad[i, rows, :] = norm_back(
+            i, rows, source, gain[...], out[i, rows, :], dmiddle[i, rows, :], sums
+        )
+
+    by_rows(tokens.shape[1], work)
+
+
+def last(left, right, tokens, dmiddle, gain, collective_id):
+    piece, width = left.shape[2], right.shape[0]
+    return pl.pallas_call(
+        last_kernel,
+        out_shape=[
+            jax.ShapeDtypeStruct((2, piece, width), F32),
+            jax.ShapeDtypeStruct((8, width), F32),
+        ],
+        in_specs=[VMEM] * 5,
+        out_specs=[VMEM] * 2,
+        scratch_shapes=[pltpu.VMEM((2, piece, width), F32)] + room(piece, width),
+        cost_estimate=cost(50),
+        compiler_params=params(collective_id, 50),
+    )(left, right, tokens, dmiddle, gain)
+
+
+def ffn_back_kernel(
+    planes,
+    dgate,
+    dup,
+    gathered,
+    normed,
+    middle,
+    cot,
+    gain,
+    grads,
+    dmiddle,
+    dmix,
+    sums,
+    out,
+    weights,
+    every,
+    local,
+    *scratch,
+):
+    loads = load_rows(planes, gathered, weights, local.at[0])
+    whole = pltpu.make_async_copy(normed, every, local.at[1])
+    whole.start()
+    meet(neighbours())
+    lefts = (dgate, dup)
+    width, part = weights.shape[1:]
     quarter = width // 4
+    all_rows = 8 * 2 * normed.shape[2]
 
     def gradient(j):
         own = grads.shape[-2]
 
         def body(q, _):
             columns = pl.ds(pl.multiple_of(q * quarter, quarter), quarter)
-            left = every[:, :, :, columns].reshape(8 * rows, quarter)
-            right = lefts[j][...].reshape(8 * rows, lefts[j].shape[-1])
+            left = every[:, :, :, columns].reshape(all_rows, quarter)
+            right = lefts[j][...].reshape(all_rows, part)
             value = t_times(left, right).astype(BF16)
             if len(grads.shape) == 3:
                 grads[j, columns, :] = value
@@ -644,67 +860,572 @@
 
         lax.fori_loop(0, 4, body, 0)
 
-    if with_grads:
+    def first():
         whole.wait()
         gradient(0)
-    diag_y.wait_recv()
-    ready[1, 0] = (keep[0] + diag[0].astype(F32)).astype(BF16)
-    x_zero = go(ready.at[1, 0], from_x.at[0], 8, {"x": 1 - x})
-    diag_x.wait_recv()
-    ready[2, 1] = (keep[1] + diag[1].astype(F32)).astype(BF16)
-    y_one = go(ready.at[2, 1], from_y.at[1], 9, {"y": 1 - y})
-    if with_grads:
-        gradient(1)
-    for i, (one, two) in enumerate(((x_zero, y_zero), (x_one, y_one))):
-        one.wait_recv()
-        two.wait_recv()
-        out[i] += from_x[i].astype(F32) + from_y[i].astype(F32)
-    for copy in copies:
-        copy.wait_send()
-
-
-def plane_scatter(lefts, rights, transposed, collective_id, gathered=None, normed=None):
-    piece = lefts[0].shape[2]
-    with_grads = gathered is not None
-    if with_grads:
-        planes, part = gathered.shape[0], gathered.shape[-1]
-        width = normed.shape[3]
-        operands = [*lefts, gathered, normed]
-        in_specs = [VMEM] * len(lefts) + [ANY, ANY]
-    else:
-        planes = 0
-        width = rights[0].shape[0 if transposed else 1]
-        operands = [*lefts, *rights]
-        in_specs = [VMEM] * len(operands)
-    out_shape = [jax.ShapeDtypeStruct((2, piece, width), F32)]
-    scratch = [
-        pltpu.VMEM((4, 2, piece, width), BF16),
-        pltpu.VMEM((4, 2, piece, width), BF16),
-        pltpu.VMEM((3, 2, piece, width), BF16),
-        pltpu.VMEM((2, piece, width), F32),
-        pltpu.VMEM((2, piece, width), BF16),
-        pltpu.VMEM((2, piece, width), BF16),
-        pltpu.VMEM((2, piece, width), BF16),
-        pltpu.SemaphoreType.DMA((10,)),
-        pltpu.SemaphoreType.DMA((10,)),
-    ]
-    if with_grads:
-        out_shape.append(jax.ShapeDtypeStruct(gathered.shape, BF16))
-        scratch += [
+
+    for copy in loads:
+        copy.wait()
+    rights = [weights.at[0], weights.at[1]]
+    scatter(lefts, rights, True, out, scratch, (first, lambda: gradient(1)))
+    sums[...] = jnp.zeros_like(sums)
+
+    def work(i, rows):
+        value = norm_back(
+            i,
+            rows,
+            middle[i, rows, :],
+            gain[...],
+            out[i, rows, :],
+            cot[i, rows, :].astype(F32),
+            sums,
+        )
+        dmiddle[i, rows, :] = value
+        dmix[i, rows, :] = value.astype(BF16)
+
+    by_rows(middle.shape[1], work)
+
+
+def ffn_back(planes, dgate, dup, gathered, normed, middle, cot, gain, collective_id):
+    piece, part = dgate.shape[2:]
+    width = normed.shape[3]
+    return pl.pallas_call(
+        functools.partial(ffn_back_kernel, planes),
+        out_shape=[
+            jax.ShapeDtypeStruct(gathered.shape, BF16),
+            jax.ShapeDtypeStruct((2, piece, width), F32),
+            jax.ShapeDtypeStruct((2, piece, width), BF16),
+            jax.ShapeDtypeStruct((8, width), F32),
+        ],
+        in_specs=[VMEM, VMEM, ANY, ANY, VMEM, VMEM, VMEM],
+        out_specs=[VMEM] * 4,
+        scratch_shapes=[
+            pltpu.VMEM((2, piece, width), F32),
             pltpu.VMEM((2, width, part), BF16),
             pltpu.VMEM((8, 2, piece, width), BF16),
-            pltpu.SemaphoreType.DMA((2,)),
+            sems(2),
         ]
+        + room(piece, width),
+        cost_estimate=cost(60),
+        compiler_params=params(collective_id, 60),
+    )(dgate, dup, gathered, normed, middle, cot, gain)
+
+
+def ring():
+    z, planes = lax.axis_index("z"), lax.axis_size("z")
+    return {"z": lax.rem(z + 1, planes)}, {"z": lax.rem(z + planes - 1, planes)}
+
+
+def load_in(planes, gathered, rows, sem):
+    if len(gathered.shape) == 2:
+        copies = [pltpu.make_async_copy(gathered, rows, sem)]
+    else:
+        own = gathered.shape[2]
+        copies = []
+        for z in range(planes):
+            for m in range(8):
+                start = (((m // 2) * planes + z) * 2 + m % 2) * own
+                to = rows.at[pl.ds(start, own)]
+                copies.append(pltpu.make_async_copy(gathered.at[z, m], to, sem))
+    for copy in copies:
+        copy.start()
+    return copies
+
+
+def mixer_kernel(
+    planes,
+    tokens_all,
+    gathered,
+    taps,
+    blocks,
+    tokens,
+    gain,
+    out,
+    normed_two,
+    normed_out,
+    proj_out,
+    conv_out,
+    gated_out,
+    weights_out,
+    right,
+    rows_out,
+    own,
+    every,
+    weights,
+    proj,
+    conv,
+    gated,
+    tall,
+    ends,
+    before,
+    local,
+    ends_sem,
+    send,
+    recv,
+    rights,
+    got,
+    send_o,
+    recv_o,
+    send_s,
+    recv_s,
+):
+    y, c, z, x = place()
+    me = (y * 2 + x) * 2 + c
+    _, _, piece, width = every.shape
+    part = conv.shape[-1]
+    loads = load_in(planes, gathered, weights, local.at[0])
+    chips = {}
+    for n, chip in enumerate((1, 3, 0, 2)):
+        rows = pl.ds(chip * 2, 2)
+        chips[chip] = pltpu.make_async_copy(tokens_all.at[rows], every.at[rows], local.at[1 + n])
+        chips[chip].start()
+    after, prior = ring()
+    meet(others() + [after, prior])
+    count = blocks.shape[1]
+    for zz in range(planes):
+        rows_out[zz * count : (zz + 1) * count, :] = blocks[zz].astype(F32)
+    right[...] = rows_out[...].astype(BF16).reshape(right.shape)
+    whole = Gather(right, rights, send_o, recv_o)
+    whole.first()
+    own_right = pltpu.make_async_copy(right, rights.at[me], local.at[11])
+    own_right.start()
+    for copy in loads:
+        copy.wait()
+    saved = [pltpu.make_async_copy(weights, weights_out, local.at[5])]
+
+    def project(member):
+        value = every[member].reshape(2 * piece, width).astype(F32)
+        value = (rms_parts(value)[0] * gain[0:1, :]).astype(BF16)
+        every[member] = value.reshape(2, piece, width)
+        a = every[member].reshape(2 * piece, width)
+        proj[member] = times(a, weights[...]).reshape(2, piece, 3 * part)
+
+    def inner(member, i, rows):
+        return proj[member, i, rows, :part] * proj[member, i, rows, 2 * part :]
+
+    last = slice(piece - 2, piece)
+    for yy in (0, 1):
+        chips[yy * 2 + 1].wait()
+
+        def second(core, _):
+            member = (yy * 2 + 1) * 2 + core
+            project(member)
+            for i in (0, 1):
+                ends[(yy * 2 + core) * 2 + i] = inner(member, i, last)
+            return 0
+
+        lax.fori_loop(0, 2, second, 0)
+    to_next = remote(ends, before, ends_sem.at[0], ends_sem.at[1], after)
+    to_next.start()
+    for yy in (0, 1):
+        chips[yy * 2].wait()
+
+        def first(core, _):
+            project((yy * 2) * 2 + core)
+            return 0
+
+        lax.fori_loop(0, 2, first, 0)
+        if yy == 0:
+            whole.forward()
+    whole.second()
+    saved.append(pltpu.make_async_copy(proj, proj_out, local.at[6]))
+    saved.append(pltpu.make_async_copy(every, normed_out, local.at[10]))
+    for copy in saved:
+        copy.start()
+
+    def convolve(member, i, start):
+        tall[6:8, :] = start
+        now = inner(member, i, slice(0, piece))
+        tall[8 : 8 + piece, :] = now
+        value = taps[0:1] * tall[6 : 6 + piece, :] + taps[1:2] * tall[7 : 7 + piece, :]
+        value += taps[2:3] * now
+        conv[member, i] = value
+        gate = proj[member, i, :, part : 2 * part]
+        gated[member, i] = (gate * value).astype(BF16)
+
+    def right_half(n, _):
+        member = (n // 2) * 4 + 2 + n % 2
+        for i in (0, 1):
+            convolve(member, i, inner(member - 2, i, last))
+        return 0
+
+    lax.fori_loop(0, 4, right_half, 0)
+    whole.last()
+    to_next.wait_recv()
+
+    def left_half(n, _):
+        member = (n // 2) * 4 + n % 2
+        for i in (0, 1):
+            start = before[n * 2 + i]
+            convolve(member, i, jnp.where(z > 0, start, jnp.zeros_like(start)))
+        return 0
+
+    lax.fori_loop(0, 4, left_half, 0)
+    swapped = [pltpu.make_async_copy(gated.at[me], got.at[me], local.at[12])]
+    for f, peer in enumerate(others()):
+        to = (peer["y"] * 2 + peer["x"]) * 2 + peer["core"]
+        swapped.append(remote(gated.at[to], got.at[me], send_s.at[f], recv_s.at[f], peer))
+    for copy in swapped:
+        copy.start()
+    for n, (src, dst) in enumerate(((conv, conv_out), (gated, gated_out))):
+        saved.append(pltpu.make_async_copy(src, dst, local.at[7 + n]))
+        saved[-1].start()
+    whole.arrived(*range(6, 14))
+    whole.sent()
+    own_right.wait()
+    for copy in swapped:
+        copy.wait()
+    third = width // 3
+
+    def mix(n, _):
+        columns = pl.ds(pl.multiple_of(n * third, third), third)
+        total = tokens[:, :, columns].astype(F32).reshape(2 * piece, third)
+        for member in range(8):
+            left = got[member].reshape(2 * piece, part)
+            total += times(left, rights[member, :, :, columns].reshape(part, third))
+        out[:, :, columns] = total.reshape(2, piece, third)
+        return 0
+
+    lax.fori_loop(0, 3, mix, 0)
+
+    def work(i, rows):
+        own[i, rows, :] = (rms_parts(out[i, rows, :])[0] * gain[1:2, :]).astype(BF16)
+
+    by_rows(piece, work)
+    gather = Gather(own, normed_two, send, recv)
+    gather.first()
+    mine = pltpu.make_async_copy(own, normed_two.at[(y * 2 + x) * 2 + c], local.at[9])
+    mine.start()
+    saved.append(mine)
+    gather.forward()
+    gather.second()
+    gather.last()
+    gather.arrived(*range(6, 14))
+    gather.sent()
+    to_next.wait_send()
+    for copy in saved:
+        copy.wait()
+
+
+def mixer_forward(planes, tokens_all, gathered, taps, blocks, tokens, gain, collective_id):
+    _, _, piece, width = tokens_all.shape
+    part = blocks.shape[1] * planes
+    saved = [
+        (tokens_all.shape, BF16),
+        (tokens_all.shape, BF16),
+        ((8, 2, piece, 3 * part), F32),
+        ((8, 2, piece, part), F32),
+        ((8, 2, piece, part), BF16),
+        ((width, 3 * part), BF16),
+    ]
+    return pl.pallas_call(
+        functools.partial(mixer_kernel, planes),
+        out_shape=[jax.ShapeDtypeStruct((2, piece, width), F32)]
+        + [jax.ShapeDtypeStruct(*item) for item in saved]
+        + [jax.ShapeDtypeStruct((2, part // 2, width), BF16)],
+        in_specs=[ANY, ANY] + [VMEM] * 4,
+        out_specs=[VMEM] + [ANY] * 6 + [VMEM],
+        scratch_shapes=[
+            pltpu.VMEM((part, width), F32),
+            pltpu.VMEM((2, piece, width), BF16),
+            pltpu.VMEM((8, 2, piece, width), BF16),
+            pltpu.VMEM((width, 3 * part), BF16),
+            pltpu.VMEM((8, 2, piece, 3 * part), F32),
+            pltpu.VMEM((8, 2, piece, part), F32),
+            pltpu.VMEM((8, 2, piece, part), BF16),
+            pltpu.VMEM((8 + piece, part), F32),
+            pltpu.VMEM((8, 2, part), F32),
+            pltpu.VMEM((8, 2, part), F32),
+            sems(13),
+            sems(2),
+            sems(14),
+            sems(14),
+            pltpu.VMEM((8, 2, part // 2, width), BF16),
+            pltpu.VMEM((8, 2, piece, part), BF16),
+            sems(14),
+            sems(14),
+            sems(7),
+            sems(7),
+        ],
+        cost_estimate=cost(95),
+        compiler_params=params(collective_id, 60),
+    )(tokens_all, gathered, taps, blocks, tokens, gain)
+
+
+def branch_kernel(
+    planes,
+    active,
+    down,
+    own,
+    right,
+    proj_in,
+    conv_in,
+    gated,
+    normed,
+    taps,
+    out,
+    dmix,
+    dproj,
+    grad_in,
+    grad_out,
+    grad_taps,
+    near,
+    proj,
+    conv,
+    tall,
+    starts,
+    beyond,
+    total_out,
+    total_in,
+    near_sem,
+    local,
+    ends_sem,
+    send,
+    recv,
+    *scratch,
+):
+    y, c, z, x = place()
+    _, _, piece, part = conv.shape
+    width = out.shape[2]
+    chips = [flip(y, dy) * 2 + flip(x, dx) for dy, dx in ((0, 0), (0, 1), (1, 0), (1, 1))]
+    half = 2 * piece
+    loads = [
+        pltpu.make_async_copy(proj_in, proj, local.at[0]),
+        pltpu.make_async_copy(conv_in, conv, local.at[1]),
+    ]
+    for copy in loads:
+        copy.start()
+
+    def fetch(source, k):
+        copy = pltpu.make_async_copy(
+            source.at[pl.ds(chips[k] * 2, 2)], near.at[k % 2], near_sem.at[k % 2]
+        )
+        copy.start()
+        return copy
+
+    after, prior = ring()
+    meet(neighbours() + [after, prior])
+    gather = Gather(own, dmix, send, recv)
+    gather.first()
+    mine = pltpu.make_async_copy(own, dmix.at[(y * 2 + x) * 2 + c], local.at[2])
+    mine.start()
+    to_prior = remote(starts.at[0], beyond, ends_sem.at[0], ends_sem.at[1], prior)
+    grad_taps[...] = jnp.zeros_like(grad_taps)
+    third = width // 3
+
+    def gradients(k):
+        chip, other = chips[k], flip(x, k % 2)
+
+        def body(core, _):
+            member = chip * 2 + core
+            grad = times_t(near[k % 2, core].reshape(half, width), right[...])
+            grad = grad.reshape(2, piece, part)
+            for i in (0, 1):
+                dproj[member, i, :, part : 2 * part] = (grad[i] * conv[member, i]).astype(BF16)
+                dconv = grad[i] * proj[member, i, :, part : 2 * part]
+                conv[member, i] = dconv
+                starts[other, (flip(y, k // 2) * 2 + core) * 2 + i] = dconv[:2]
+            return 0
+
+        lax.fori_loop(0, 2, body, 0)
+
+        def sum_up(n, _):
+            columns = pl.ds(pl.multiple_of(n * third, third), third)
+            left = gated[pl.ds(chip * 2, 2)].reshape(2 * half, part)
+            product = t_times(left, near[k % 2, :, :, :, columns].reshape(2 * half, third))
+            if k == 0:
+                total_out[:, columns] = product
+            elif k < 3:
+                total_out[:, columns] += product
+            else:
+                product = total_out[:, columns] + product
+                own_rows = part // planes
+                for zz in range(planes):
+                    block = product[zz * own_rows : (zz + 1) * own_rows]
+                    grad_out[zz, :, columns] = block.astype(BF16)
+            return 0
+
+        lax.fori_loop(0, 3, sum_up, 0)
+
+    def through(member, i, end):
+        tall[0:piece, :] = conv[member, i]
+        tall[piece : piece + 2, :] = end
+        now, one, two = conv[member, i], tall[1 : piece + 1, :], tall[2 : piece + 2, :]
+        b_part, x_part = proj[member, i, :, :part], proj[member, i, :, 2 * part :]
+        dmixed = taps[2:3] * now + taps[1:2] * one + taps[0:1] * two
+        dproj[member, i, :, :part] = (dmixed * x_part).astype(BF16)
+        dproj[member, i, :, 2 * part :] = (dmixed * b_part).astype(BF16)
+        mixed = b_part * x_part
+        for k, shifted in enumerate((two, one, now)):
+            grad_taps[k : k + 1, :] += jnp.sum(mixed * shifted, axis=0, keepdims=True)
+
+    def left_half(n, _):
+        member = (n // 2) * 4 + n % 2
+        for i in (0, 1):
+            through(member, i, conv[member + 2, i, 0:2, :])
+        return 0
+
+    def right_half(n, _):
+        member = (n // 2) * 4 + 2 + n % 2
+        for i in (0, 1):
+            end = beyond[n * 2 + i]
+            through(member, i, jnp.where(z < planes - 1, end, jnp.zeros_like(end)))
+        return 0
+
+    def one():
+        for copy in loads:
+            copy.wait()
+        mine.wait()
+        gather.arrived(6, 7)
+        fetch(dmix, 0).wait()
+        gradients(0)
+        gather.second()
+        gather.arrived(8, 9)
+        fetched = fetch(dmix, 1)
+        gather.arrived(10, 11)
+        following = fetch(dmix, 2)
+        fetched.wait()
+        gradients(1)
+        following.wait()
+        gradients(2)
+        gather.last()
+        gather.arrived(12, 13)
+        fetch(dmix, 3).wait()
+        to_normed.append(fetch(normed, 0))
+        gradients(3)
+        to_normed.append(fetch(normed, 1))
+        to_prior.start()
+        lax.fori_loop(0, 4, left_half, 0)
+
+    quarter = width // 4
+
+    def two():
+        to_prior.wait_recv()
+        lax.fori_loop(0, 4, right_half, 0)
+        for k in range(4):
+            to_normed[k].wait()
+
+            def sum_up(q, _):
+                columns = pl.ds(pl.multiple_of(q * quarter, quarter), quarter)
+                left = near[k % 2, :, :, :, columns].reshape(2 * half, quarter)
+                right_side = dproj[pl.ds(chips[k] * 2, 2)].reshape(2 * half, 3 * part)
+                product = t_times(left, right_side)
+                if k == 0:
+                    total_in[columns, :] = product
+                elif k < 3:
+                    total_in[columns, :] += product
+                else:
+                    product = (total_in[columns, :] + product).astype(BF16)
+                    if len(grad_in.shape) == 2:
+                        grad_in[columns, :] = product
+                        return 0
+                    own_rows = grad_in.shape[2]
+                    for zz in range(planes):
+                        for xx in (0, 1):
+                            start = (zz * 2 + xx) * own_rows
+                            grad_in[zz, q * 2 + xx] = product[start : start + own_rows]
+                return 0
+
+            lax.fori_loop(0, 4, sum_up, 0)
+            if k < 2:
+                to_normed.append(fetch(normed, k + 2))
+
+    to_normed = []
+    gather.forward()
+    scatter([active], [down], False, out, scratch, (one, two))
+    gather.sent()
+    to_prior.wait_send()
+
+
+def branch_forward(
+    planes, active, down, dmix, right, proj, conv, gated, normed, taps, in_shape, collective_id
+):
+    _, piece, width = dmix.shape
+    part = right.shape[0]
+    outs = [
+        ((2, piece, width), F32),
+        (normed.shape, BF16),
+        ((8, 2, piece, 3 * part), BF16),
+        (in_shape, BF16),
+        ((planes, part // planes, width), BF16),
+        ((3, part), F32),
+    ]
     got = pl.pallas_call(
-        functools.partial(scatter_kernel, planes, len(lefts), transposed, with_grads),
-        out_shape=out_shape,
-        in_specs=in_specs,
-        out_specs=[VMEM] * len(out_shape),
-        scratch_shapes=scratch,
-        cost_estimate=cost(55 if with_grads else 48),
-        compiler_params=params(collective_id, 60 if with_grads else 44),
-    )(*operands)
-    return got if with_grads else got[0]
+        functools.partial(branch_kernel, planes),
+        out_shape=[jax.ShapeDtypeStruct(*item) for item in outs],
+        in_specs=[VMEM, VMEM, ANY, VMEM, ANY, ANY, VMEM, ANY, VMEM],
+        out_specs=[VMEM, ANY] + [VMEM] * 4,
+        scratch_shapes=[
+            pltpu.VMEM((2, 2, 2, piece, width), BF16),
+            pltpu.VMEM((8, 2, piece, 3 * part), F32),
+            pltpu.VMEM((8, 2, piece, part), F32),
+            pltpu.VMEM((8 + piece, part), F32),
+            pltpu.VMEM((2, 8, 2, part), F32),
+            pltpu.VMEM((8, 2, part), F32),
+            pltpu.VMEM((part, width), F32),
+            pltpu.VMEM((width, 3 * part), F32),
+            sems(2),
+            sems(3),
+            sems(2),
+            sems(14),
+            sems(14),
+        ]
+        + room(piece, width),
+        cost_estimate=cost(90),
+        compiler_params=params(collective_id, 62),
+    )(active, down, dmix, right, proj, conv, gated, normed, taps)
+    return got[:1] + got[2:]
+
+
+def update_kernel(planes, three, rate, decay, got, weight, first, second, grad, moment, updated):
+    wide = got.shape[-1] // planes
+    parts = 1
+    if three:
+        wide, parts = wide // 3, 3
+    for k in range(parts):
+        for owner in range(8 * planes):
+            pair, z, xx = owner // (2 * planes), owner // 2 % planes, owner % 2
+            start = (k * planes + z) * wide
+            to = (k * 8 * planes + owner) * wide
+            if three:
+                value = got[pair * 2 + xx, :, start : start + wide]
+            else:
+                value = got[pair * 2 + xx, 0, :, start : start + wide]
+            if three:
+                grad[:, to : to + wide] = value.astype(F32)
+            else:
+                grad[0, :, to : to + wide] = value.astype(F32)
+    moment[...], updated[...] = adamw(
+        weight[...], first[...], second[...], grad[...], rate, decay
+    )
+
+
+def update(planes, got, weight, first, second, rate, decay):
+    three = weight.ndim == 2
+    rows = weight.shape[-2]
+    step = 16 if rows % 16 == 0 else rows
+    part = got.shape[-1]
+    columns = weight.shape[-1]
+    if three:
+        grid = (rows // step,)
+        got_spec = pl.BlockSpec((8, step, part), lambda n: (0, n, 0))
+        spec = pl.BlockSpec((step, columns), lambda n: (n, 0))
+    else:
+        grid = (2, rows // step)
+        got_spec = pl.BlockSpec((8, 1, step, part), lambda j, n: (0, j, n, 0))
+        spec = pl.BlockSpec((1, step, columns), lambda j, n: (j, n, 0))
+    size = weight.size * 4
+    return pl.pallas_call(
+        functools.partial(update_kernel, planes, three, rate, decay),
+        out_shape=[jax.ShapeDtypeStruct(weight.shape, F32)] * 3,
+        grid=grid,
+        in_specs=[got_spec, spec, spec, spec],
+        out_specs=[spec] * 3,
+        cost_estimate=pl.CostEstimate(
+            flops=12 * size, bytes_accessed=7 * size, transcendentals=0
+        ),
+        compiler_params=pltpu.CompilerParams(vmem_limit_bytes=32 * 2**20),
+    )(got, weight, first, second)
 
 
 def rms_parts(values):
@@ -769,72 +1490,41 @@
     part_d = width // 8
     part_f = ff // 8
 
-    in_send = in_proj.astype(BF16).reshape(own_d, 3, 4, planes, 2, own_d)
-    in_send = in_send.transpose(2, 4, 0, 1, 3, 5).reshape(8, own_d, 3 * part_d)
-    gu_send = gate_up.astype(BF16).reshape(2, own_d, 4, planes, 2, own_f)
-    gu_send = gu_send.transpose(2, 4, 0, 1, 3, 5).reshape(8, 2, own_d, part_f)
-    small = jnp.concatenate([norm_gains, conv_taps], axis=0)
-    small_all, in_mine = share(small, in_send, planes, 0)
+    in_tiles = own_d % 16 == 0
 
     def along_z(value):
         return lax.all_gather(value, "z", axis=0, tiled=False)
 
-    in_t = along_z(in_mine).reshape(planes, 4, 2, own_d, 3 * part_d)
-    in_t = in_t.transpose(1, 0, 2, 3, 4).reshape(width, 3 * part_d)
-    down_t = along_z(down_proj.astype(BF16)).reshape(part_f, width)
-
-    low = small_all.astype(BF16).astype(F32)
-    gains = low[:, :, :2].reshape(4, 2, planes, 2, own_d).transpose(3, 0, 2, 1, 4)
-    gains = gains.reshape(2, width)
-    y, c, z, x = place()
-    taps = lax.dynamic_index_in_dim(low[:, :, 2:], (y * 2 + c) * 2 + x, 0, keepdims=False)
-    taps = taps.transpose(1, 0, 2).reshape(3, part_d)
-
-    hidden = tokens.astype(F32).reshape(rows, width)
-    hat_one, scale_one = rms_parts(hidden)
-    normed = (hat_one * gains[0]).astype(BF16).reshape(seqs, piece, width)
-    normed_all, gu_mine, out_t = early(planes, normed, gu_send, out_proj.astype(BF16), 1)
-    normed_all = normed_all.reshape(all_rows, width)
-    out_t = out_t.reshape(part_d, width)
+    most = width // 3 * 2
+    down_low = down_proj.astype(BF16)
+    down_most = along_z(down_low[:, :most]).reshape(part_f, most)
+    small = jnp.concatenate([norm_gains, conv_taps], axis=0)
+    tokens_all, gu_mine, in_t, out_blocks, gains, taps = early(
+        planes, small, tokens, in_proj, gate_up, out_proj, 0
+    )
+    if not in_tiles:
+        in_t = in_t.reshape(planes, 4, 2, own_d, 3 * part_d).transpose(1, 0, 2, 3, 4)
+        in_t = in_t.reshape(width, 3 * part_d)
     gu_t = along_z(gu_mine)
-    in_tiles = own_d % 16 == 0
     if not in_tiles:
         gu_t = gu_t.reshape(planes, 4, 2, 2, own_d, part_f).transpose(3, 1, 0, 2, 4, 5)
         gu_t = gu_t.reshape(2, width, part_f)
 
-    projected = times(normed_all, in_t)
-    b_part = projected[:, :part_d]
-    c_part = projected[:, part_d : 2 * part_d]
-    x_part = projected[:, 2 * part_d :]
-    lay = (2, 2, 2, seqs, piece, part_d)
-    mixed_in = (b_part * x_part).reshape(lay)
-    ends = mixed_in[..., piece - 2 :, :]
-    before = lax.ppermute(ends[:, 1], "z", [(i, i + 1) for i in range(planes - 1)])
-    arrived = jnp.stack([before, ends[:, 0]], axis=1)
-    extended = jnp.concatenate([arrived, mixed_in], axis=-2)
-    conv_out = (
-        taps[0] * extended[..., :piece, :]
-        + taps[1] * extended[..., 1 : piece + 1, :]
-        + taps[2] * extended[..., 2:, :]
+    middle, normed_two_all, normed_all, proj, conv, gated, in_whole, out_t = mixer_forward(
+        planes, tokens_all, in_t, taps, out_blocks, tokens, gains, 2
     )
-    conv_out = conv_out.reshape(all_rows, part_d)
-    gated = (c_part * conv_out).astype(BF16)
-
-    def members(value):
-        return value.reshape(8, seqs, piece, value.shape[-1])
-
-    mixer = plane_scatter([members(gated)], [out_t], False, 2).reshape(rows, width)
-    middle = hidden + mixer
-    hat_two, scale_two = rms_parts(middle)
-    normed_two = (hat_two * gains[1]).astype(BF16).reshape(seqs, piece, width)
-    normed_two_all = plane_gather(normed_two, 3)
-    active, dgate, dup, grad_down = ffn(planes, cotangent, normed_two_all, gu_t, down_t, 4)
+    out_t = out_t.reshape(part_d, width)
+    active, dgate, dup, grad_down, down_t = ffn(
+        planes, cotangent, normed_two_all, gu_t, down_most, down_low[:, most:], 4
+    )
 
     def sum_z(value):
         return lax.psum_scatter(value, "z", scatter_dimension=0, tiled=False)
 
     g_down = sum_z(grad_down)
-    dnorm_two, grad_gu = plane_scatter([dgate, dup], None, True, 5, gu_t, normed_two_all)
+    grad_gu, dmiddle, dmix, gain_two = ffn_back(
+        planes, dgate, dup, gu_t, normed_two_all, middle, cotangent, gains[1:], 5
+    )
     if not in_tiles:
         grad_gu = grad_gu.reshape(2, 4, planes, 2, own_d, part_f).transpose(2, 1, 3, 0, 4, 5)
         grad_gu = grad_gu.reshape(planes, 8, 2, own_d, part_f)
@@ -842,70 +1532,47 @@
     g_down = g_down.astype(F32)
     gu_back = sum_z(grad_gu)
 
-    dnorm_two = dnorm_two.reshape(rows, width)
-    gain_grad_two = jnp.sum(dnorm_two * hat_two, axis=0)
-    cot_full = cotangent.astype(F32).reshape(rows, width)
-    dmiddle = cot_full + rms_back(dnorm_two * gains[1], hat_two, scale_two)
-    dmix = dmiddle.astype(BF16).reshape(seqs, piece, width)
-    dmix_all = plane_gather(dmix, 6).reshape(all_rows, width)
-
-    grad_out = t_times(gated, dmix_all)
-    dgated = times_t(dmix_all, out_t)
-    dc_part = dgated * conv_out
-    dconv = (dgated * c_part).reshape(lay)
-    grad_taps = jnp.stack(
-        [
-            jnp.sum(dconv * extended[..., k : piece + k, :], axis=(0, 1, 2, 3, 4))
-            for k in range(3)
-        ]
+    branch, dproj, grad_in, grad_out, grad_taps = branch_forward(
+        planes,
+        active,
+        down_t,
+        dmix,
+        out_t,
+        proj,
+        conv,
+        gated,
+        normed_all,
+        taps,
+        in_t.shape,
+        7,
     )
-
-    def padded(before, after):
-        return jnp.pad(dconv, [(0, 0)] * 4 + [(before, after), (0, 0)])
-
-    grad_ext = taps[0] * padded(0, 2) + taps[1] * padded(1, 1) + taps[2] * padded(2, 0)
-    starts = grad_ext[..., :2, :]
-    after = lax.ppermute(starts[:, 0], "z", [(i + 1, i) for i in range(planes - 1)])
-    returned = jnp.stack([starts[:, 1], after], axis=1)
-    returned = jnp.pad(returned, [(0, 0)] * 4 + [(piece - 2, 0), (0, 0)])
-    grad_mixed = (grad_ext[..., 2:, :] + returned).reshape(all_rows, part_d)
-    dproj = jnp.concatenate([grad_mixed * x_part, dc_part, grad_mixed * b_part], axis=-1)
-    dproj = dproj.astype(BF16)
-    grad_in = t_times(normed_all, dproj).astype(BF16)
-    grad_in = grad_in.reshape(4, planes, 2, own_d, 3 * part_d).transpose(1, 0, 2, 3, 4)
-    grad_in = grad_in.reshape(planes, 8, own_d, 3 * part_d)
-    grad_out = grad_out.astype(BF16).reshape(planes, own_d, width)
+    block_out = (middle + branch).astype(BF16)
+    if not in_tiles:
+        grad_in = grad_in.reshape(4, planes, 2, own_d, 3 * part_d).transpose(1, 0, 2, 3, 4)
+        grad_in = grad_in.reshape(planes, 8, own_d, 3 * part_d)
     grad_in, gu_back, dproj = lax.optimization_barrier((grad_in, gu_back, dproj))
     in_back = sum_z(grad_in)
     taps_parts = grad_taps.reshape(3, planes, own_d).transpose(1, 0, 2)
 
-    dnorm_one = plane_scatter([members(dproj)], [in_t], True, 7).reshape(rows, width)
-    gain_grad_one = jnp.sum(dnorm_one * hat_one, axis=0)
-    token_grad = dmiddle + rms_back(dnorm_one * gains[0], hat_one, scale_one)
-    active, token_grad = lax.optimization_barrier((active, token_grad))
-    branch = plane_scatter([active], [down_t], False, 8).reshape(rows, width)
-    block_out = (middle + branch).astype(BF16)
-    grad_gains = jnp.stack([gain_grad_one, gain_grad_two])
+    token_grad, gain_one = last(dproj, in_whole, tokens, dmiddle, gains[:1], 8)
+    grad_gains = jnp.stack([jnp.sum(gain_one, axis=0), jnp.sum(gain_two, axis=0)])
     gains_parts = grad_gains.reshape(2, 4, planes, 2, own_d).transpose(1, 3, 2, 0, 4)
     gains_parts = gains_parts.reshape(8, planes, 2, own_d)
     in_got, gu_got, sums, g_out = finish(
         planes, in_back, gu_back, gains_parts, taps_parts, grad_out, 9
     )
     g_gains, g_conv = sums[:2], sums[2:]
-    g_in = in_got.reshape(4, 2, own_d, 3, planes, own_d).transpose(2, 3, 0, 4, 1, 5)
-    g_in = g_in.reshape(own_d, 3 * width).astype(F32)
-    g_gu = gu_got.reshape(4, 2, 2, own_d, planes, own_f).transpose(2, 3, 0, 4, 1, 5)
-    g_gu = g_gu.reshape(2, own_d, ff).astype(F32)
-
     m_gains, u_gains = adamw(norm_gains, first_gains, second_gains, g_gains, 0.4, 0.0)
-    m_in, u_in = adamw(in_proj, first_in, second_in, g_in, 0.02, 0.1)
+    g_in, m_in, u_in = update(planes, in_got, in_proj, first_in, second_in, 0.02, 0.1)
     m_conv, u_conv = adamw(conv_taps, first_conv, second_conv, g_conv, 0.2, 0.1)
     m_out, u_out = adamw(out_proj, first_out, second_out, g_out, 0.02, 0.1)
-    m_gu, u_gu = adamw(gate_up, first_gate_up, second_gate_up, g_gu, 0.02, 0.1)
+    g_gu, m_gu, u_gu = update(
+        planes, gu_got, gate_up, first_gate_up, second_gate_up, 0.02, 0.1
+    )
     m_down, u_down = adamw(down_proj, first_down, second_down, g_down, 0.01, 0.1)
     return (
-        block_out.reshape(seqs, piece, width),
-        token_grad.reshape(seqs, piece, width),
+        block_out,
+        token_grad,
         g_gains,
         g_in,
         g_conv,

time: 722 us -> 536 us (0.74)
  local copies, waits for them, and re-layouts: 112 us -> 18.4 us
  other arithmetic: 86.1 us -> 12.9 us
  matrix products: 35.1 us -> 0 us
  Pallas kernels: 460 us -> 479 us
  waiting for transfers between devices: 0.17 us -> 8.05 us
    reshape x13 -> x2, local copies, waits for them, and re-layouts: 43.2 us -> 1.37 us  [on_device(): taps_parts = grad_taps.reshape(3, planes, own_d).transpose(1, 0, 2)]
    dot_general x4 -> x0, matrix products: 35.1 us -> none  [the longest x2 15.7 us: t_times(): lax.dot_general(left, right, (((0,), (0,)), ((), ())), preferred_element_...]
    convert_element_type x8 -> x0, local copies, waits for them, and re-layouts: 26.5 us -> none  [the longest x3 13.7 us: on_device(): g_gu = g_gu.reshape(2, own_d, ff).astype(F32)]
    add x4 -> x0, other arithmetic: 25 us -> none  [the longest x1 12 us: on_device(): taps[0] * extended[..., :piece, :] + taps[1] * extended[..., 1:piece + 1, :]]
    reduce_sum x5 -> x2, other arithmetic: 19.9 us -> 0.04 us  [the longest x1 0.02 us: on_device(): jnp.sum(gain_one, axis=0)]
    pallas_call x1, Pallas kernels: 59.9 us -> 77.6 us  [early(): pl.pallas_call(functools.partial(early_kernel, planes), out_shape=[jax.Sh...]
    convert_element_type x9 -> x1, other arithmetic: 11.9 us -> 1.54 us  [on_device(): down_low = down_proj.astype(BF16)]
    sub x6 -> x4, other arithmetic: 17.2 us -> 7.37 us  [adamw(): return (second_new, weight - rate * (direction + decay * weight))]
  transfers between devices with their start and end apart: 8 -> 5, of which waited for: 0 -> 2; matrix products, arithmetic and copies ran while one was open for 23% -> 2% of each run, Pallas kernels for 43% -> 72%
where the time goes in v3:
time: 536 us; the launch traced here: 533 us
  Pallas kernels  479 us (89%)
  local copies, waits for them, and re-layouts  18.4 us (3%)
  between operations  14.4 us (3%)
  other arithmetic  12.9 us (2%)
  waiting for transfers between devices  8.05 us (2%)
    pallas_call x1, Pallas kernels, mixer_forward(): pl.pallas_call(functools.partial(mixer_kernel, planes), out_shape=[jax.Sh...  94.7 us
    pallas_call x1, Pallas kernels, branch_forward(): pl.pallas_call(functools.partial(branch_kernel, planes), out_shape=[jax.S...  88 us
    pallas_call x1, Pallas kernels, early(): pl.pallas_call(functools.partial(early_kernel, planes), out_shape=[jax.Sh...  77.6 us
    pallas_call x1, Pallas kernels, ffn_back(): pl.pallas_call(functools.partial(ffn_back_kernel, planes), out_shape=[jax...  68.7 us
    pallas_call x1, Pallas kernels, ffn(): pl.pallas_call(functools.partial(ffn_kernel, planes), out_shape=[wide, wi...  59.3 us
    pallas_call x1, Pallas kernels, last(): pl.pallas_call(last_kernel, out_shape=[jax.ShapeDtypeStruct((2, piece, wi...  55 us
    pallas_call x1, Pallas kernels, finish(): pl.pallas_call(functools.partial(finish_kernel, planes), out_shape=[jax.S...  28.1 us
    unnamed x68, local copies, waits for them, and re-layouts  13.2 us
  transfers between devices with their start and end apart: 5, of which 2 were waited for; matrix products, arithmetic and copies ran while one was open for 2% of the time, Pallas kernels for 72%

profile of v3, /device:TPU:1, one launch (start us, length us, event | category | flops | bytes accessed | tf_op | source)
XLA Modules:
  0.0 533.3 jit_solution(13089661245117950071)
XLA Ops:
  7.3 1.5 convert_element_type.9
  10.6 1.2 copy-done.6
  11.8 1.3 copy-done.13
  13.1 77.6 %shard_map.347 = (bf16[8,2,192,1536]{3,2,1,0:T(8,128)(2,1)}, bf16[8,2,48,864]{3,2,1,0:T(8,128)(2,1)S(1)}, bf16[4,8,48,576]{3,2,1,0:T(8,128)(2,1)S(1)}, bf16[4,48...) custom-call(f32[5,48]{1,0:T(8,128)S(1)} %pad_maximum_fusion.small, ...), custom_call_target="tpu_custom_call" | custom-call | flops 70000001024 | tf_op jit(solution)/shard_map/pallas_call | solution.py:340
  91.7 1.3 copy-done.16
  94.6 1.6 slice.25.down_own
  96.9 94.7 %shard_map.348 = (f32[2,192,1536]{2,1,0:T(8,128)}, bf16[8,2,192,1536]{3,2,1,0:T(8,128)(2,1)}, bf16[8,2,192,1536]{3,2,1,0:T(8,128)(2,1)}, f32[8,2,192,576]{3,2,1,...) custom-call(bf16[8,2,192,1536]{3,2,1,0:T(8,128)(2,1)} %get-tuple-ele, ...), custom_call_target="tpu_custom_call" | custom-call | flops 95000002560 | tf_op jit(solution)/shard_map/pallas_call | solution.py:1121
  191.6 5.6 %all-gather.5.cloned.1.call-done = bf16[32,2,48,864]{3,2,1,0:T(8,128)(2,1)} async-done(((bf16[8,2,48,864]{3,2,1,0:T(8,128)(2,1)}), bf16[32,2,48,864]{3,2,1,0:T(8,128)(2,1)}) %all-gather.5.cloned.1.call-update) | async-done | bytes 5308432 | tf_op jit(solution)/shard_map/all_gather | solution.py:1496
  197.2 59.3 %shard_map.349 = (bf16[8,2,192,864]{3,2,1,0:T(8,128)(2,1)}, bf16[8,2,192,864]{3,2,1,0:T(8,128)(2,1)}, bf16[8,2,192,864]{3,2,1,0:T(8,128)(2,1)}, bf16[4,216,1536]{2,1,0:T(8,128)(2,1)}, bf16[864,1536]{1,0:T(8,128)(2,1)}) custom-call(bf16[2,192,1536]{2,1,0:T(8,128)(2,1)} %cot.3, bf16[8,2,192,1536]{3,2,1,0:T(8,128)(2,1)} %get-tuple-element.71.normed, ...), custom_call_target="tpu_custom_call" | custom-call | flops 54999998464 | tf_op jit(solution)/shard_map/pallas_call | solution.py:622
  256.7 68.7 %shard_map.350 = (bf16[4,8,2,48,864]{4,3,2,1,0:T(8,128)(2,1)}, f32[2,192,1536]{2,1,0:T(8,128)}, bf16[2,192,1536]{2,1,0:T(8,128)(2,1)}, f32[8,1536]{1,0:T(8,128)}) custom-call(bf16[8,2,192,864]{3,2,1,0:T(8,128)(2,1)} %get-tuple-element.75.dgate, bf16[8,2,192,864]{3,2,1,0:T(8,128)(2,1)} %get-tuple-element.76.dup, bf16[4,8,2,48,864]{4,3,2,1,0:T(8,128)(2,1)} %bitcast.15, ...), custom_call_target="tpu_custom_call" | custom-call | flops 60000002048 | tf_op jit(solution)/shard_map/pallas_call | solution.py:892
  325.5 88.0 %shard_map.351 = (f32[2,192,1536]{2,1,0:T(8,128)}, bf16[8,2,192,1536]{3,2,1,0:T(8,128)(2,1)}, bf16[8,2,192,576]{3,2,1,0:T(8,128)(2,1)}, bf16[4,8,48,576]{3,2,1,0...) custom-call(bf16[8,2,192,864]{3,2,1,0:T(8,128)(2,1)} %get-tuple-element.73.active, ...), custom_call_target="tpu_custom_call" | custom-call | flops 89999998976 | tf_op jit(solution)/shard_map/pallas_call | solution.py:1353
  415.0 4.0 add_convert_fusion
  419.0 2.3 multiply_subtract_fusion
  421.3 2.3 reduce-scatter.6.cloned.1.call-done
  423.7 55.0 %shard_map.352 = (f32[2,192,1536]{2,1,0:T(8,128)}, f32[8,1536]{1,0:T(8,128)S(1)}) custom-call(bf16[8,2,192,576]{3,2,1,0:T(8,128)(2,1)} %get-tuple-element.89.left, bf16[1536,576]{1,0:T(8,128)(2,1)S(1)} %copy-done.15, bf16[2,192,1536]{2,1,0:T(8,128)(2,1)S(1)} %copy-done.14, f32[2,192,1536]{2,1,0:T(8,128)} %get-tuple-element.91.dmiddle, ...), custom_call_target="tpu_custom_call" | custom-call | flops 49999998976 | tf_op jit(solution)/shard_map/pallas_call | solution.py:802
  479.5 28.1 %shard_map.353 = (bf16[8,48,576]{2,1,0:T(8,128)(2,1)}, bf16[8,2,48,864]{3,2,1,0:T(8,128)(2,1)}, f32[5,48]{1,0:T(8,128)}, f32[48,1536]{1,0:T(8,128)}) custom-call(bf16[8,48,576]{2,1,0:T(8,128)(2,1)} %bitcast.17, bf16[8,2,48,864]{3,2,1,0:T(8,128)(2,1)} %bitcast.16, f32[8,4,2,48]{3,2,1,0:T(2,128)} %bitcast.12, f32[4,3,48]{2,1,0:T(4,128)} %bitcast.13, ...), custom_call_target="tpu_custom_call" | custom-call | flops 24999999488 | tf_op jit(solution)/shard_map/pallas_call | solution.py:417
  507.6 1.4 multiply_subtract_fusion.3
  509.0 1.3 multiply_subtract_fusion.2
  510.3 2.4 multiply_subtract_fusion.1
  512.6 1.2 copy-done.9
  514.8 2.6 shard_map.354
  517.5 1.7 copy-done.3
  519.2 5.2 shard_map.355
  524.4 1.4 copy.48
  (86 shorter events, 9.4 us)
Async XLA Ops:
  7.2 3.4 copy-start.27
  7.2 3.4 copy-start.29
  7.2 3.4 copy-start
  7.2 3.4 copy-start.11
  7.2 184.4 %all-gather.7.cloned.1.call-start = ((), (), s32[]{:S(2)}) async-start(), calls=%async_computation.7 | async-start | bytes 2211840 | tf_op jit(solution)/shard_map/all_gather | solution.py:1496
  10.5 186.7 %all-gather.5.cloned.1.call-start = ((), (), s32[]{:S(2)}) async-start(), calls=%async_computation.6 | async-start | bytes 6881280 | tf_op jit(solution)/shard_map/all_gather | solution.py:1496
  94.4 231.0 %reduce-scatter.4.cloned.1.call-start = ((), (), s32[]{:S(2)}) async-start(), calls=%async_computation.3 | async-start | bytes 3317760 | tf_op jit(solution)/shard_map/reduce_scatter | solution.py:1522
  256.6 167.0 %reduce-scatter.6.cloned.1.call-start = ((), (), s32[]{:S(2)}) async-start(), calls=%async_computation.4 | async-start | bytes 6881280 | tf_op jit(solution)/shard_map/reduce_scatter | solution.py:1522
  325.4 154.1 %reduce-scatter.8.cloned.1.call-start = ((), (), s32[]{:S(2)}) async-start(), calls=%async_computation.5 | async-start | bytes 2457600 | tf_op jit(solution)/shard_map/reduce_scatter | solution.py:1522
  325.4 89.4 %copy-start.26 = (f32[8,1536]{1,0:T(8,128)S(1)}, f32[8,1536]{1,0:T(8,128)}, u32[]{:S(2)}) copy-start(f32[8,1536]{1,0:T(8,128)} %get-tuple-element.96) | copy-start | bytes 147460
  415.0 4.0 copy-start.19
  415.0 4.0 copy-start.22
  415.0 4.0 copy-start.23
  415.0 4.0 copy-start.25
  419.0 4.7 copy-start.15
  479.5 28.1 %copy-start.30 = (f32[2,48]{1,0:T(2,128)S(1)}, f32[2,48]{1,0:T(2,128)}, u32[]{:S(2)}) copy-start(f32[2,48]{1,0:T(2,128)} %param.22) | copy-start | bytes 1156
  479.5 29.5 %copy-start.28 = (f32[3,48]{1,0:T(4,128)S(1)}, f32[3,48]{1,0:T(4,128)}, u32[]{:S(2)}) copy-start(f32[3,48]{1,0:T(4,128)} %param.24) | copy-start | bytes 1732
  479.5 29.5 %copy-start.31 = (f32[3,48]{1,0:T(4,128)S(1)}, f32[3,48]{1,0:T(4,128)}, u32[]{:S(2)}) copy-start(f32[3,48]{1,0:T(4,128)} %param.30) | copy-start | bytes 1732
  479.5 29.5 %copy-start.32 = (f32[3,48]{1,0:T(4,128)S(1)}, f32[3,48]{1,0:T(4,128)}, u32[]{:S(2)}) copy-start(f32[3,48]{1,0:T(4,128)} %param.36) | copy-start | bytes 1732
  479.5 33.1 %copy-start.8 = (f32[48,4608]{1,0:T(8,128)S(1)}, f32[48,4608]{1,0:T(8,128)}, u32[]{:S(2)}) copy-start(f32[48,4608]{1,0:T(8,128)} %first.2) | copy-start | bytes 2654212
  479.5 38.0 %copy-start.2 = (f32[2,48,6912]{2,1,0:T(8,128)S(1)}, f32[2,48,6912]{2,1,0:T(8,128)}, u32[]{:S(2)}) copy-start(f32[2,48,6912]{2,1,0:T(8,128)} %first.3) | copy-start | bytes 7962628
  507.6 5.1 copy-start.7
  510.3 7.2 %copy-start.4 = (bf16[8,2,48,864]{3,2,1,0:T(8,128)(2,1)S(1)}, bf16[8,2,48,864]{3,2,1,0:T(8,128)(2,1)}, u32[]{:S(2)}) copy-start(bf16[8,2,48,864]{3,2,1,0:T(8,128)(2,1)} %get-tuple-element.103.got) | copy-start | bytes 3981316
  519.2 5.2 copy-start.21
  (14 other events, 19.9 us)
Sparse Core Ops, SparseCore 0:
  10.6 54.0 all-gather.6
  94.5 102.6 all-gather.4
  256.7 52.8 reduce-scatter.3
  325.5 98.0 reduce-scatter.5
  425.8 41.7 reduce-scatter.7

commit v4 on v3

--- a/solution.py
+++ b/solution.py
@@ -662,12 +662,12 @@
         pltpu.VMEM((2, piece, width), BF16),
         pltpu.VMEM((2, piece, width), BF16),
         pltpu.VMEM((2, piece, width), BF16),
-        sems(10),
-        sems(10),
+        sems(11),
+        sems(11),
     ]
 
 
-def scatter(lefts, rights, transposed, out, scratch, fills=()):
+def scatter(lefts, rights, transposed, out, scratch, fills=(), loaded=None):
     staged, held, ready, keep, diag, from_x, from_y, send, recv = scratch
     y, c, _, x = place()
     _, piece, width = out.shape
@@ -681,20 +681,20 @@
         copies.append(copy)
         return copy
 
-    def product(dy, dx, core, store):
+    def product(dy, dx, core, store, i=None):
         member = (flip(y, dy) * 2 + flip(x, dx)) * 2 + core
 
         def body(n, _):
             columns = pl.ds(pl.multiple_of(n * tile, tile), tile)
             value = None
             for left, right in zip(lefts, rights):
-                a = left[member].reshape(rows, left.shape[-1])
+                a = left[member].reshape(rows, left.shape[-1]) if i is None else left[member, i]
                 if transposed:
                     term = times_t(a, right[columns, :])
                 else:
                     term = times(a, right[:, columns])
                 value = term if value is None else value + term
-            store(columns, value.reshape(2, piece, tile))
+            store(columns, value.reshape(2, piece, tile) if i is None else value)
             return 0
 
         lax.fori_loop(0, 3, body, 0)
@@ -720,9 +720,6 @@
 
         product(dy, dx, c, add)
 
-    def store_diag(columns, value):
-        ready[0, :, :, columns] = value.astype(BF16)
-
     def store_x(columns, value):
         ready[1, 1, :, columns] = value[1].astype(BF16)
         keep[0, :, columns] = value[0]
@@ -734,19 +731,48 @@
     def store_own(columns, value):
         out[:, :, columns] = value
 
-    to_other_core(0)
+    def diag_half(i):
+        dy, dx = order[0]
+
+        def store(columns, value):
+            staged[0, i, :, columns] = value.astype(BF16)
+
+        product(dy, dx, 1 - c, store, i)
+        return go(staged.at[0, i], held.at[0, i], 0 if i == 0 else 10, {"core": 1 - c})
+
+    def diag_sum(i, copy):
+        dy, dx = order[0]
+
+        def store(columns, value):
+            copy_in = held[0, i, :, columns].astype(F32)
+            ready[0, i, :, columns] = (value + copy_in).astype(BF16)
+
+        copy.wait_recv()
+        product(dy, dx, c, store, i)
+
+    if loaded:
+        loaded(0)
+    halves = [diag_half(0), diag_half(1)]
+    diag_sum(0, halves[0])
+    diag_y = go(ready.at[0, 0], diag.at[0], 4, {"y": 1 - y})
+    diag_sum(1, halves[1])
+    diag_x = go(ready.at[0, 1], diag.at[1], 5, {"x": 1 - x})
+    over.append(None)
+    if loaded:
+        loaded(1)
     to_other_core(1)
-    own_core(0, store_diag)
-    diag_y = go(ready.at[0, 0], diag.at[0], 4, {"y": 1 - y})
-    diag_x = go(ready.at[0, 1], diag.at[1], 5, {"x": 1 - x})
+    if loaded:
+        loaded(2)
     to_other_core(2)
     own_core(1, store_x)
     x_one = go(ready.at[1, 1], from_x.at[1], 6, {"x": 1 - x})
     own_core(2, store_y)
     y_zero = go(ready.at[2, 0], from_y.at[0], 7, {"y": 1 - y})
+    if loaded:
+        loaded(3)
     to_other_core(3)
     own_core(3, store_own)
-    if fills:
+    if fills and fills[0]:
         fills[0]()
     diag_y.wait_recv()
     ready[1, 0] = (keep[0] + diag[0].astype(F32)).astype(BF16)
@@ -765,7 +791,7 @@
 
 
 def by_rows(piece, work):
-    step = 16
+    step = 32
 
     def body(n, _):
         rows = pl.ds(pl.multiple_of(n * step, step), step)
@@ -779,13 +805,53 @@
 def norm_back(i, rows, source, gain, grad, base, sums):
     normal, scale = rms_parts(source)
     term = grad * normal
-    sums[...] += term[:8] + term[8:]
+    sums[...] += (term[:8] + term[8:16]) + (term[16:24] + term[24:])
     return base + rms_back(grad * gain, normal, scale)
 
 
-def last_kernel(left, right, tokens, dmiddle, gain, token_grad, sums, out, *scratch):
-    meet(neighbours())
-    scatter([left], [right], True, out, scratch)
+def load(pairs, sem):
+    copies = [pltpu.make_async_copy(src, dst, sem.at[n]) for n, (src, dst) in enumerate(pairs)]
+    for copy in copies:
+        copy.start()
+    return copies
+
+
+def far_first():
+    y, _, _, x = place()
+    return [flip(y, dy) * 2 + flip(x, dx) for dy, dx in ((1, 1), (0, 1), (1, 0), (0, 0))]
+
+
+def last_kernel(
+    planes,
+    left_in,
+    right_in,
+    tokens_in,
+    dmiddle_in,
+    ins,
+    gain,
+    token_grad,
+    sums,
+    in_sum,
+    out,
+    left,
+    right,
+    tokens,
+    dmiddle,
+    ins_got,
+    sem,
+    send_z,
+    recv_z,
+    *scratch,
+):
+    parts = [(right_in, right)]
+    parts += [(left_in.at[pl.ds(n * 2, 2)], left.at[pl.ds(n * 2, 2)]) for n in far_first()]
+    copies = load(parts + [(tokens_in, tokens), (dmiddle_in, dmiddle)], sem)
+    meet(neighbours() + line_peers(planes))
+    line = scatter_line(planes, ins, ins_got, send_z, recv_z, sem.at[7])
+    copies[0].wait()
+    scatter([left], [right], True, out, scratch, loaded=lambda n: copies[1 + n].wait())
+    copies[5].wait()
+    copies[6].wait()
     sums[...] = jnp.zeros_like(sums)
 
     def work(i, rows):
@@ -795,32 +861,51 @@
         )
 
     by_rows(tokens.shape[1], work)
-
-
-def last(left, right, tokens, dmiddle, gain, collective_id):
+    for copy in line:
+        copy.wait()
+    for member in range(8):
+        total = ins_got[0, member].astype(F32)
+        for k in range(1, planes):
+            total += ins_got[k, member].astype(F32)
+        in_sum[member] = total.astype(BF16)
+
+
+def last(planes, left, right, tokens, dmiddle, ins, gain, collective_id):
     piece, width = left.shape[2], right.shape[0]
     return pl.pallas_call(
-        last_kernel,
+        functools.partial(last_kernel, planes),
         out_shape=[
             jax.ShapeDtypeStruct((2, piece, width), F32),
             jax.ShapeDtypeStruct((8, width), F32),
+            jax.ShapeDtypeStruct(ins.shape[1:], BF16),
         ],
-        in_specs=[VMEM] * 5,
-        out_specs=[VMEM] * 2,
-        scratch_shapes=[pltpu.VMEM((2, piece, width), F32)] + room(piece, width),
+        in_specs=[ANY] * 5 + [VMEM],
+        out_specs=[VMEM] * 3,
+        scratch_shapes=[
+            pltpu.VMEM((2, piece, width), F32),
+            pltpu.VMEM(left.shape, BF16),
+            pltpu.VMEM(right.shape, BF16),
+            pltpu.VMEM(tokens.shape, BF16),
+            pltpu.VMEM(dmiddle.shape, F32),
+            pltpu.VMEM(ins.shape, BF16),
+            sems(8),
+            sems(planes - 1),
+            sems(planes - 1),
+        ]
+        + room(piece, width),
         cost_estimate=cost(50),
         compiler_params=params(collective_id, 50),
-    )(left, right, tokens, dmiddle, gain)
+    )(left, right, tokens, dmiddle, ins, gain)
 
 
 def ffn_back_kernel(
     planes,
-    dgate,
-    dup,
+    dgate_in,
+    dup_in,
     gathered,
     normed,
-    middle,
-    cot,
+    middle_in,
+    cot_in,
     gain,
     grads,
     dmiddle,
@@ -829,14 +914,24 @@
     out,
     weights,
     every,
+    dgate,
+    dup,
+    middle,
+    cot,
     local,
+    sem,
     *scratch,
 ):
     loads = load_rows(planes, gathered, weights, local.at[0])
+    lefts = (dgate, dup)
+    parts = []
+    for n in far_first():
+        rows = pl.ds(n * 2, 2)
+        parts += [(dgate_in.at[rows], dgate.at[rows]), (dup_in.at[rows], dup.at[rows])]
+    copies = load(parts + [(middle_in, middle), (cot_in, cot)], sem)
     whole = pltpu.make_async_copy(normed, every, local.at[1])
     whole.start()
     meet(neighbours())
-    lefts = (dgate, dup)
     width, part = weights.shape[1:]
     quarter = width // 4
     all_rows = 8 * 2 * normed.shape[2]
@@ -860,14 +955,22 @@
 
         lax.fori_loop(0, 4, body, 0)
 
-    def first():
+    def both():
         whole.wait()
         gradient(0)
+        gradient(1)
 
     for copy in loads:
         copy.wait()
     rights = [weights.at[0], weights.at[1]]
-    scatter(lefts, rights, True, out, scratch, (first, lambda: gradient(1)))
+
+    def loaded(n):
+        copies[2 * n].wait()
+        copies[2 * n + 1].wait()
+
+    scatter(lefts, rights, True, out, scratch, (None, both), loaded)
+    copies[8].wait()
+    copies[9].wait()
     sums[...] = jnp.zeros_like(sums)
 
     def work(i, rows):
@@ -897,13 +1000,18 @@
             jax.ShapeDtypeStruct((2, piece, width), BF16),
             jax.ShapeDtypeStruct((8, width), F32),
         ],
-        in_specs=[VMEM, VMEM, ANY, ANY, VMEM, VMEM, VMEM],
+        in_specs=[ANY] * 6 + [VMEM],
         out_specs=[VMEM] * 4,
         scratch_shapes=[
             pltpu.VMEM((2, piece, width), F32),
             pltpu.VMEM((2, width, part), BF16),
             pltpu.VMEM((8, 2, piece, width), BF16),
+            pltpu.VMEM(dgate.shape, BF16),
+            pltpu.VMEM(dup.shape, BF16),
+            pltpu.VMEM(middle.shape, F32),
+            pltpu.VMEM(cot.shape, BF16),
             sems(2),
+            sems(10),
         ]
         + room(piece, width),
         cost_estimate=cost(60),
@@ -1154,13 +1262,13 @@
 
 def branch_kernel(
     planes,
-    active,
-    down,
+    active_in,
+    down_in,
     own,
     right,
     proj_in,
     conv_in,
-    gated,
+    gated_in,
     normed,
     taps,
     out,
@@ -1170,6 +1278,9 @@
     grad_out,
     grad_taps,
     near,
+    active,
+    down,
+    gated,
     proj,
     conv,
     tall,
@@ -1189,12 +1300,6 @@
     width = out.shape[2]
     chips = [flip(y, dy) * 2 + flip(x, dx) for dy, dx in ((0, 0), (0, 1), (1, 0), (1, 1))]
     half = 2 * piece
-    loads = [
-        pltpu.make_async_copy(proj_in, proj, local.at[0]),
-        pltpu.make_async_copy(conv_in, conv, local.at[1]),
-    ]
-    for copy in loads:
-        copy.start()
 
     def fetch(source, k):
         copy = pltpu.make_async_copy(
@@ -1207,8 +1312,10 @@
     meet(neighbours() + [after, prior])
     gather = Gather(own, dmix, send, recv)
     gather.first()
-    mine = pltpu.make_async_copy(own, dmix.at[(y * 2 + x) * 2 + c], local.at[2])
+    mine = pltpu.make_async_copy(own, dmix.at[(y * 2 + x) * 2 + c], local.at[5])
     mine.start()
+    pairs = [(active_in, active), (down_in, down), (proj_in, proj), (conv_in, conv)]
+    loads = load(pairs + [(gated_in, gated)], local)
     to_prior = remote(starts.at[0], beyond, ends_sem.at[0], ends_sem.at[1], prior)
     grad_taps[...] = jnp.zeros_like(grad_taps)
     third = width // 3
@@ -1273,7 +1380,7 @@
         return 0
 
     def one():
-        for copy in loads:
+        for copy in loads[2:]:
             copy.wait()
         mine.wait()
         gather.arrived(6, 7)
@@ -1288,6 +1395,8 @@
         gradients(1)
         following.wait()
         gradients(2)
+
+    def one_more():
         gather.last()
         gather.arrived(12, 13)
         fetch(dmix, 3).wait()
@@ -1300,6 +1409,7 @@
     quarter = width // 4
 
     def two():
+        one_more()
         to_prior.wait_recv()
         lax.fori_loop(0, 4, right_half, 0)
         for k in range(4):
@@ -1332,6 +1442,8 @@
 
     to_normed = []
     gather.forward()
+    loads[0].wait()
+    loads[1].wait()
     scatter([active], [down], False, out, scratch, (one, two))
     gather.sent()
     to_prior.wait_send()
@@ -1353,10 +1465,13 @@
     got = pl.pallas_call(
         functools.partial(branch_kernel, planes),
         out_shape=[jax.ShapeDtypeStruct(*item) for item in outs],
-        in_specs=[VMEM, VMEM, ANY, VMEM, ANY, ANY, VMEM, ANY, VMEM],
+        in_specs=[ANY, ANY, ANY, VMEM, ANY, ANY, ANY, ANY, VMEM],
         out_specs=[VMEM, ANY] + [VMEM] * 4,
         scratch_shapes=[
             pltpu.VMEM((2, 2, 2, piece, width), BF16),
+            pltpu.VMEM(active.shape, BF16),
+            pltpu.VMEM(down.shape, BF16),
+            pltpu.VMEM(gated.shape, BF16),
             pltpu.VMEM((8, 2, piece, 3 * part), F32),
             pltpu.VMEM((8, 2, piece, part), F32),
             pltpu.VMEM((8 + piece, part), F32),
@@ -1365,7 +1480,7 @@
             pltpu.VMEM((part, width), F32),
             pltpu.VMEM((width, 3 * part), F32),
             sems(2),
-            sems(3),
+            sems(6),
             sems(2),
             sems(14),
             sems(14),
@@ -1550,11 +1665,11 @@
     if not in_tiles:
         grad_in = grad_in.reshape(4, planes, 2, own_d, 3 * part_d).transpose(1, 0, 2, 3, 4)
         grad_in = grad_in.reshape(planes, 8, own_d, 3 * part_d)
-    grad_in, gu_back, dproj = lax.optimization_barrier((grad_in, gu_back, dproj))
-    in_back = sum_z(grad_in)
     taps_parts = grad_taps.reshape(3, planes, own_d).transpose(1, 0, 2)
 
-    token_grad, gain_one = last(dproj, in_whole, tokens, dmiddle, gains[:1], 8)
+    token_grad, gain_one, in_back = last(
+        planes, dproj, in_whole, tokens, dmiddle, grad_in, gains[:1], 8
+    )
     grad_gains = jnp.stack([jnp.sum(gain_one, axis=0), jnp.sum(gain_two, axis=0)])
     gains_parts = grad_gains.reshape(2, 4, planes, 2, own_d).transpose(1, 3, 2, 0, 4)
     gains_parts = gains_parts.reshape(8, planes, 2, own_d)

time: 536 us -> 527 us (0.983)
  Pallas kernels: 479 us -> 471 us
    unnamed x68 -> x72, local copies, waits for them, and re-layouts: 13.2 us -> 14.7 us
  transfers between devices with their start and end apart: 5 -> 4, of which waited for: 2 -> 1; matrix products, arithmetic and copies ran while one was open for 2% -> 2% of each run, Pallas kernels for 72% -> 71%
where the time goes in v4:
time: 527 us; the launch traced here: 524 us
  Pallas kernels  471 us (89%)
  local copies, waits for them, and re-layouts  19.3 us (4%)
  between operations  14.3 us (3%)
  other arithmetic  12.8 us (2%)
  waiting for transfers between devices  6.53 us (1%)
    pallas_call x1, Pallas kernels, mixer_forward(): pl.pallas_call(functools.partial(mixer_kernel, planes), out_shape=[jax.Sh...  94.1 us
    pallas_call x1, Pallas kernels, branch_forward(): pl.pallas_call(functools.partial(branch_kernel, planes), out_shape=[jax.S...  85.3 us
    pallas_call x1, Pallas kernels, early(): pl.pallas_call(functools.partial(early_kernel, planes), out_shape=[jax.Sh...  77.6 us
    pallas_call x1, Pallas kernels, ffn_back(): pl.pallas_call(functools.partial(ffn_back_kernel, planes), out_shape=[jax...  66 us
    pallas_call x1, Pallas kernels, ffn(): pl.pallas_call(functools.partial(ffn_kernel, planes), out_shape=[wide, wi...  59.4 us
    pallas_call x1, Pallas kernels, last(): pl.pallas_call(functools.partial(last_kernel, planes), out_shape=[jax.Sha...  51 us
    pallas_call x1, Pallas kernels, finish(): pl.pallas_call(functools.partial(finish_kernel, planes), out_shape=[jax.S...  29.5 us
    unnamed x72, local copies, waits for them, and re-layouts  14.7 us
  transfers between devices with their start and end apart: 4, of which 1 were waited for; matrix products, arithmetic and copies ran while one was open for 2% of the time, Pallas kernels for 71%

profile of v4, /device:TPU:1, one launch (start us, length us, event | category | flops | bytes accessed | tf_op | source)
XLA Modules:
  0.0 523.8 jit_solution(5177165415008296101)
XLA Ops:
  7.3 1.5 convert_element_type.9
  10.6 1.2 copy-done.6
  11.8 1.3 copy-done.13
  13.1 77.6 %shard_map.347 = (bf16[8,2,192,1536]{3,2,1,0:T(8,128)(2,1)}, bf16[8,2,48,864]{3,2,1,0:T(8,128)(2,1)S(1)}, bf16[4,8,48,576]{3,2,1,0:T(8,128)(2,1)S(1)}, bf16[4,48...) custom-call(f32[5,48]{1,0:T(8,128)S(1)} %pad_maximum_fusion.small, ...), custom_call_target="tpu_custom_call" | custom-call | flops 70000001024 | tf_op jit(solution)/shard_map/pallas_call | solution.py:340
  91.7 1.3 copy-done.17
  94.5 1.6 slice.25.down_own
  96.7 94.1 %shard_map.348 = (f32[2,192,1536]{2,1,0:T(8,128)}, bf16[8,2,192,1536]{3,2,1,0:T(8,128)(2,1)}, bf16[8,2,192,1536]{3,2,1,0:T(8,128)(2,1)}, f32[8,2,192,576]{3,2,1,...) custom-call(bf16[8,2,192,1536]{3,2,1,0:T(8,128)(2,1)} %get-tuple-ele, ...), custom_call_target="tpu_custom_call" | custom-call | flops 95000002560 | tf_op jit(solution)/shard_map/pallas_call | solution.py:1229
  190.8 6.4 %all-gather.5.cloned.1.call-done = bf16[32,2,48,864]{3,2,1,0:T(8,128)(2,1)} async-done(((bf16[8,2,48,864]{3,2,1,0:T(8,128)(2,1)}), bf16[32,2,48,864]{3,2,1,0:T(8,128)(2,1)}) %all-gather.5.cloned.1.call-update) | async-done | bytes 5308432 | tf_op jit(solution)/shard_map/all_gather | solution.py:1611
  197.2 59.4 %shard_map.349 = (bf16[8,2,192,864]{3,2,1,0:T(8,128)(2,1)}, bf16[8,2,192,864]{3,2,1,0:T(8,128)(2,1)}, bf16[8,2,192,864]{3,2,1,0:T(8,128)(2,1)}, bf16[4,216,1536]{2,1,0:T(8,128)(2,1)}, bf16[864,1536]{1,0:T(8,128)(2,1)}) custom-call(bf16[2,192,1536]{2,1,0:T(8,128)(2,1)} %cot_in.1, bf16[8,2,192,1536]{3,2,1,0:T(8,128)(2,1)} %get-tuple-element.69.normed, ...), custom_call_target="tpu_custom_call" | custom-call | flops 54999998464 | tf_op jit(solution)/shard_map/pallas_call | solution.py:622
  256.7 66.0 %shard_map.350 = (bf16[4,8,2,48,864]{4,3,2,1,0:T(8,128)(2,1)}, f32[2,192,1536]{2,1,0:T(8,128)}, bf16[2,192,1536]{2,1,0:T(8,128)(2,1)}, f32[8,1536]{1,0:T(8,128)}) custom-call(bf16[8,2,192,864]{3,2,1,0:T(8,128)(2,1)} %get-tuple-element.73.dgate_in, bf16[8,2,192,864]{3,2,1,0:T(8,128)(2,1)} %get-tuple-element.74.dup_in, bf16[4,8,2,48,864]{4,3,2,1,0:T(8,128)(2,1)} %bitcast.14, ...), custom_call_target="tpu_custom_call" | custom-call | flops 60000002048 | tf_op jit(solution)/shard_map/pallas_call | solution.py:995
  322.8 85.3 %shard_map.351 = (f32[2,192,1536]{2,1,0:T(8,128)}, bf16[8,2,192,1536]{3,2,1,0:T(8,128)(2,1)}, bf16[8,2,192,576]{3,2,1,0:T(8,128)(2,1)}, bf16[4,8,48,576]{3,2,1,0...) custom-call(bf16[8,2,192,864]{3,2,1,0:T(8,128)(2,1)} %get-tuple-element.71.active_in, ...), custom_call_target="tpu_custom_call" | custom-call | flops 89999998976 | tf_op jit(solution)/shard_map/pallas_call | solution.py:1465
  408.1 1.5 copy-done.15
  409.7 51.0 %shard_map.352 = (f32[2,192,1536]{2,1,0:T(8,128)}, f32[8,1536]{1,0:T(8,128)S(1)}, bf16[8,48,576]{2,1,0:T(8,128)(2,1)S(1)}) custom-call(bf16[8,2,192,576]{3,2,1,0:T(8,128)(2,1)} %get-tuple-element.82.left_in, bf16[1536,576]{1,0:T(8,128)(2,1)S(1)} %copy-done.15, bf16[2,192,1536]{2,1,0:T(8,128)(2,1)S(1)} %copy-done.14, ...), custom_call_target="tpu_custom_call" | custom-call | flops 49999998976 | tf_op jit(solution)/shard_map/pallas_call | solution.py:875
  462.3 3.8 add_convert_fusion
  466.2 2.3 multiply_subtract_fusion
  468.6 29.5 %shard_map.353 = (bf16[8,48,576]{2,1,0:T(8,128)(2,1)}, bf16[8,2,48,864]{3,2,1,0:T(8,128)(2,1)}, f32[5,48]{1,0:T(8,128)}, f32[48,1536]{1,0:T(8,128)}) custom-call(bf16[8,48,576]{2,1,0:T(8,128)(2,1)} %copy-done.16, bf16[8,2,48,864]{3,2,1,0:T(8,128)(2,1)} %bitcast.15, f32[8,4,2,48]{3,2,1,0:T(2,128)} %bitcast.11, f32[4,3,48]{2,1,0:T(4,128)} %bitcast.12, ...), custom_call_target="tpu_custom_call" | custom-call | flops 24999999488 | tf_op jit(solution)/shard_map/pallas_call | solution.py:417
  498.1 1.4 multiply_subtract_fusion.3
  499.5 1.3 multiply_subtract_fusion.2
  500.7 2.4 multiply_subtract_fusion.1
  503.1 1.2 copy-done.9
  505.3 2.6 shard_map.354
  508.0 1.7 copy-done.3
  509.7 5.2 shard_map.355
  514.9 1.4 copy.48
  (87 shorter events, 8.5 us)
Async XLA Ops:
  7.2 3.4 copy-start.28
  7.2 3.4 copy-start
  7.2 3.4 copy-start.11
  7.2 183.6 %all-gather.7.cloned.1.call-start = ((), (), s32[]{:S(2)}) async-start(), calls=%async_computation.5 | async-start | bytes 2211840 | tf_op jit(solution)/shard_map/all_gather | solution.py:1611
  10.5 186.7 %all-gather.5.cloned.1.call-start = ((), (), s32[]{:S(2)}) async-start(), calls=%async_computation.4 | async-start | bytes 6881280 | tf_op jit(solution)/shard_map/all_gather | solution.py:1611
  94.4 228.3 %reduce-scatter.3.cloned.1.call-start = ((), (), s32[]{:S(2)}) async-start(), calls=%async_computation.2 | async-start | bytes 3317760 | tf_op jit(solution)/shard_map/reduce_scatter | solution.py:1637
  256.7 211.9 %reduce-scatter.5.cloned.1.call-start = ((), (), s32[]{:S(2)}) async-start(), calls=%async_computation.3 | async-start | bytes 6881280 | tf_op jit(solution)/shard_map/reduce_scatter | solution.py:1637
  322.8 85.4 %copy-start.14 = (bf16[2,192,1536]{2,1,0:T(8,128)(2,1)S(1)}, bf16[2,192,1536]{2,1,0:T(8,128)(2,1)}, u32[]{:S(2)}) copy-start(bf16[2,192,1536]{2,1,0:T(8,128)(2,1)} %tokens_in.1) | copy-start | bytes 3538948
  409.7 51.0 %copy-start.32 = (f32[3,192]{1,0:T(4,128)S(1)}, f32[3,192]{1,0:T(4,128)}, u32[]{:S(2)}) copy-start(f32[3,192]{1,0:T(4,128)} %get-tuple-element.93) | copy-start | bytes 6916
  409.7 51.7 %copy-start.27 = (f32[8,1536]{1,0:T(8,128)S(1)}, f32[8,1536]{1,0:T(8,128)}, u32[]{:S(2)}) copy-start(f32[8,1536]{1,0:T(8,128)} %get-tuple-element.92) | copy-start | bytes 147460
  460.6 5.5 %copy-start.16 = (bf16[8,48,576]{2,1,0:T(8,128)(2,1)}, bf16[8,48,576]{2,1,0:T(8,128)(2,1)S(1)}, u32[]{:S(2)}) copy-start(bf16[8,48,576]{2,1,0:T(8,128)(2,1)S(1)} %get-tuple-element.87.ins) | copy-start | bytes 1327108
  462.3 3.9 copy-start.20
  462.3 3.9 copy-start.23
  462.3 3.9 copy-start.24
  462.3 3.9 copy-start.26
  468.5 29.5 %copy-start.31 = (f32[2,48]{1,0:T(2,128)S(1)}, f32[2,48]{1,0:T(2,128)}, u32[]{:S(2)}) copy-start(f32[2,48]{1,0:T(2,128)} %param.22) | copy-start | bytes 1156
  468.6 30.9 %copy-start.29 = (f32[3,48]{1,0:T(4,128)S(1)}, f32[3,48]{1,0:T(4,128)}, u32[]{:S(2)}) copy-start(f32[3,48]{1,0:T(4,128)} %param.24) | copy-start | bytes 1732
  468.6 30.9 %copy-start.33 = (f32[3,48]{1,0:T(4,128)S(1)}, f32[3,48]{1,0:T(4,128)}, u32[]{:S(2)}) copy-start(f32[3,48]{1,0:T(4,128)} %param.30) | copy-start | bytes 1732
  468.6 30.9 %copy-start.34 = (f32[3,48]{1,0:T(4,128)S(1)}, f32[3,48]{1,0:T(4,128)}, u32[]{:S(2)}) copy-start(f32[3,48]{1,0:T(4,128)} %param.36) | copy-start | bytes 1732
  468.6 34.5 %copy-start.8 = (f32[48,4608]{1,0:T(8,128)S(1)}, f32[48,4608]{1,0:T(8,128)}, u32[]{:S(2)}) copy-start(f32[48,4608]{1,0:T(8,128)} %first.2) | copy-start | bytes 2654212
  468.6 39.4 %copy-start.2 = (f32[2,48,6912]{2,1,0:T(8,128)S(1)}, f32[2,48,6912]{2,1,0:T(8,128)}, u32[]{:S(2)}) copy-start(f32[2,48,6912]{2,1,0:T(8,128)} %first.3) | copy-start | bytes 7962628
  498.1 5.0 copy-start.7
  500.7 7.2 %copy-start.4 = (bf16[8,2,48,864]{3,2,1,0:T(8,128)(2,1)S(1)}, bf16[8,2,48,864]{3,2,1,0:T(8,128)(2,1)}, u32[]{:S(2)}) copy-start(bf16[8,2,48,864]{3,2,1,0:T(8,128)(2,1)} %get-tuple-element.99.got) | copy-start | bytes 3981316
  509.7 5.2 copy-start.22
  (15 other events, 22.3 us)
Sparse Core Ops, SparseCore 0:
  10.6 54.0 all-gather.6
  94.5 102.6 all-gather.4
  256.8 52.8 reduce-scatter.2
  322.9 109.6 reduce-scatter.4

commit v5 on v4

--- a/solution.py
+++ b/solution.py
@@ -1610,7 +1610,7 @@
     def along_z(value):
         return lax.all_gather(value, "z", axis=0, tiled=False)
 
-    most = width // 3 * 2
+    most = width // 2
     down_low = down_proj.astype(BF16)
     down_most = along_z(down_low[:, :most]).reshape(part_f, most)
     small = jnp.concatenate([norm_gains, conv_taps], axis=0)

time: 527 us -> 522 us (level)
  Pallas kernels: 471 us -> 465 us
    pallas_call x1, Pallas kernels: 77.6 us -> 70.5 us  [early(): pl.pallas_call(functools.partial(early_kernel, planes), out_shape=[jax.Sh...]
    unnamed x72 -> x68, local copies, waits for them, and re-layouts: 14.7 us -> 15.5 us
where the time goes in v5:
time: 522 us; the launch traced here: 519 us
  Pallas kernels  465 us (89%)
  local copies, waits for them, and re-layouts  18.5 us (4%)
  between operations  14.3 us (3%)
  other arithmetic  12.8 us (2%)
  waiting for transfers between devices  8.16 us (2%)
    pallas_call x1, Pallas kernels, mixer_forward(): pl.pallas_call(functools.partial(mixer_kernel, planes), out_shape=[jax.Sh...  93.9 us
    pallas_call x1, Pallas kernels, branch_forward(): pl.pallas_call(functools.partial(branch_kernel, planes), out_shape=[jax.S...  85 us
    pallas_call x1, Pallas kernels, early(): pl.pallas_call(functools.partial(early_kernel, planes), out_shape=[jax.Sh...  70.5 us
    pallas_call x1, Pallas kernels, ffn_back(): pl.pallas_call(functools.partial(ffn_back_kernel, planes), out_shape=[jax...  66 us
    pallas_call x1, Pallas kernels, ffn(): pl.pallas_call(functools.partial(ffn_kernel, planes), out_shape=[wide, wi...  62.2 us
    pallas_call x1, Pallas kernels, last(): pl.pallas_call(functools.partial(last_kernel, planes), out_shape=[jax.Sha...  52 us
    pallas_call x1, Pallas kernels, finish(): pl.pallas_call(functools.partial(finish_kernel, planes), out_shape=[jax.S...  27.2 us
    unnamed x68, local copies, waits for them, and re-layouts  15.5 us
  transfers between devices with their start and end apart: 4, of which 1 were waited for; matrix products, arithmetic and copies ran while one was open for 2% of the time, Pallas kernels for 71%

profile of v5, /device:TPU:1, one launch (start us, length us, event | category | flops | bytes accessed | tf_op | source)
XLA Modules:
  0.0 518.6 jit_solution(10359893958619766597)
XLA Ops:
  7.2 1.5 convert_element_type.9
  11.3 1.3 copy-done.12
  12.6 70.5 %shard_map.347 = (bf16[8,2,192,1536]{3,2,1,0:T(8,128)(2,1)}, bf16[8,2,48,864]{3,2,1,0:T(8,128)(2,1)S(1)}, bf16[4,8,48,576]{3,2,1,0:T(8,128)(2,1)S(1)}, bf16[4,48...) custom-call(f32[5,48]{1,0:T(8,128)S(1)} %pad_maximum_fusion.small, ...), custom_call_target="tpu_custom_call" | custom-call | flops 70000001024 | tf_op jit(solution)/shard_map/pallas_call | solution.py:340
  83.1 1.1 copy-done.5
  84.2 1.3 copy-done.16
  87.5 93.9 %shard_map.348 = (f32[2,192,1536]{2,1,0:T(8,128)}, bf16[8,2,192,1536]{3,2,1,0:T(8,128)(2,1)}, bf16[8,2,192,1536]{3,2,1,0:T(8,128)(2,1)}, f32[8,2,192,576]{3,2,1,...) custom-call(bf16[8,2,192,1536]{3,2,1,0:T(8,128)(2,1)} %get-tuple-ele, ...), custom_call_target="tpu_custom_call" | custom-call | flops 95000002560 | tf_op jit(solution)/shard_map/pallas_call | solution.py:1229
  181.4 8.1 %all-gather.5.cloned.1.call-done = bf16[32,2,48,864]{3,2,1,0:T(8,128)(2,1)} async-done(((bf16[8,2,48,864]{3,2,1,0:T(8,128)(2,1)}), bf16[32,2,48,864]{3,2,1,0:T(8,128)(2,1)}) %all-gather.5.cloned.1.call-update) | async-done | bytes 5308432 | tf_op jit(solution)/shard_map/all_gather | solution.py:1611
  189.5 62.2 %shard_map.349 = (bf16[8,2,192,864]{3,2,1,0:T(8,128)(2,1)}, bf16[8,2,192,864]{3,2,1,0:T(8,128)(2,1)}, bf16[8,2,192,864]{3,2,1,0:T(8,128)(2,1)}, bf16[4,216,1536]{2,1,0:T(8,128)(2,1)}, bf16[864,1536]{1,0:T(8,128)(2,1)}) custom-call(bf16[2,192,1536]{2,1,0:T(8,128)(2,1)} %cot_in.1, bf16[8,2,192,1536]{3,2,1,0:T(8,128)(2,1)} %get-tuple-element.69.normed, ...), custom_call_target="tpu_custom_call" | custom-call | flops 54999998464 | tf_op jit(solution)/shard_map/pallas_call | solution.py:622
  251.8 66.0 %shard_map.350 = (bf16[4,8,2,48,864]{4,3,2,1,0:T(8,128)(2,1)}, f32[2,192,1536]{2,1,0:T(8,128)}, bf16[2,192,1536]{2,1,0:T(8,128)(2,1)}, f32[8,1536]{1,0:T(8,128)}) custom-call(bf16[8,2,192,864]{3,2,1,0:T(8,128)(2,1)} %get-tuple-element.73.dgate_in, bf16[8,2,192,864]{3,2,1,0:T(8,128)(2,1)} %get-tuple-element.74.dup_in, bf16[4,8,2,48,864]{4,3,2,1,0:T(8,128)(2,1)} %bitcast.14, ...), custom_call_target="tpu_custom_call" | custom-call | flops 60000002048 | tf_op jit(solution)/shard_map/pallas_call | solution.py:995
  317.8 85.0 %shard_map.351 = (f32[2,192,1536]{2,1,0:T(8,128)}, bf16[8,2,192,1536]{3,2,1,0:T(8,128)(2,1)}, bf16[8,2,192,576]{3,2,1,0:T(8,128)(2,1)}, bf16[4,8,48,576]{3,2,1,0...) custom-call(bf16[8,2,192,864]{3,2,1,0:T(8,128)(2,1)} %get-tuple-element.71.active_in, ...), custom_call_target="tpu_custom_call" | custom-call | flops 89999998976 | tf_op jit(solution)/shard_map/pallas_call | solution.py:1465
  402.8 1.3 copy-done.13
  404.1 1.5 copy-done.14
  405.6 52.0 %shard_map.352 = (f32[2,192,1536]{2,1,0:T(8,128)}, f32[8,1536]{1,0:T(8,128)S(1)}, bf16[8,48,576]{2,1,0:T(8,128)(2,1)S(1)}) custom-call(bf16[8,2,192,576]{3,2,1,0:T(8,128)(2,1)} %get-tuple-element.82.left_in, bf16[1536,576]{1,0:T(8,128)(2,1)S(1)} %copy-done.14, bf16[2,192,1536]{2,1,0:T(8,128)(2,1)S(1)} %copy-done.13, ...), custom_call_target="tpu_custom_call" | custom-call | flops 49999998976 | tf_op jit(solution)/shard_map/pallas_call | solution.py:875
  459.3 3.8 add_convert_fusion
  463.2 2.3 multiply_subtract_fusion
  465.6 27.2 %shard_map.353 = (bf16[8,48,576]{2,1,0:T(8,128)(2,1)}, bf16[8,2,48,864]{3,2,1,0:T(8,128)(2,1)}, f32[5,48]{1,0:T(8,128)}, f32[48,1536]{1,0:T(8,128)}) custom-call(bf16[8,48,576]{2,1,0:T(8,128)(2,1)} %copy-done.15, bf16[8,2,48,864]{3,2,1,0:T(8,128)(2,1)} %bitcast.15, f32[8,4,2,48]{3,2,1,0:T(2,128)} %bitcast.11, f32[4,3,48]{2,1,0:T(4,128)} %bitcast.12, ...), custom_call_target="tpu_custom_call" | custom-call | flops 24999999488 | tf_op jit(solution)/shard_map/pallas_call | solution.py:417
  492.9 1.4 multiply_subtract_fusion.3
  494.3 1.3 multiply_subtract_fusion.2
  495.5 2.4 multiply_subtract_fusion.1
  497.9 1.2 copy-done.8
  500.1 2.6 shard_map.354
  502.8 1.7 copy-done.3
  504.5 5.2 %shard_map.355 = (f32[2,48,6912]{2,1,0:T(8,128)}, f32[2,48,6912]{2,1,0:T(8,128)}, f32[2,48,6912]{2,1,0:T(8,128)}) custom-call(bf16[8,2,48,864]{3,2,1,0:T(8,128)(2,1)S(1)} %copy-done.4, f32[2,48,6912]{2,1,0:T(8,128)S(1)} %copy-done.1, f32[2,48,6912]{2,1,0:T(8,128)S(1)} %copy-done.2, f32[2,48,6912]{2,1,0:T(8,128)S(1)} %copy-done.3), custom_call_target="tpu_custom_call" | custom-call | flops 31850496 | bytes 18579456 | tf_op jit(solution)/shard_map/pallas_call | solution.py:1533
  509.7 1.4 copy.48
  (82 shorter events, 8.2 us)
Async XLA Ops:
  7.2 174.2 %all-gather.7.cloned.1.call-start = ((), (), s32[]{:S(2)}) async-start(), calls=%async_computation.5 | async-start | bytes 1658880 | tf_op jit(solution)/shard_map/all_gather | solution.py:1611
  7.2 2.6 copy-start
  8.8 1.6 copy-start.6
  9.7 179.8 %all-gather.5.cloned.1.call-start = ((), (), s32[]{:S(2)}) async-start(), calls=%async_computation.4 | async-start | bytes 6881280 | tf_op jit(solution)/shard_map/all_gather | solution.py:1611
  86.9 230.9 %reduce-scatter.3.cloned.1.call-start = ((), (), s32[]{:S(2)}) async-start(), calls=%async_computation.2 | async-start | bytes 3317760 | tf_op jit(solution)/shard_map/reduce_scatter | solution.py:1637
  251.7 213.9 %reduce-scatter.5.cloned.1.call-start = ((), (), s32[]{:S(2)}) async-start(), calls=%async_computation.3 | async-start | bytes 6881280 | tf_op jit(solution)/shard_map/reduce_scatter | solution.py:1637
  404.1 1.5 copy-start.14
  405.6 52.1 %copy-start.30 = (f32[3,192]{1,0:T(4,128)S(1)}, f32[3,192]{1,0:T(4,128)}, u32[]{:S(2)}) copy-start(f32[3,192]{1,0:T(4,128)} %get-tuple-element.93) | copy-start | bytes 6916
  405.6 52.8 %copy-start.25 = (f32[8,1536]{1,0:T(8,128)S(1)}, f32[8,1536]{1,0:T(8,128)}, u32[]{:S(2)}) copy-start(f32[8,1536]{1,0:T(8,128)} %get-tuple-element.92) | copy-start | bytes 147460
  457.7 5.5 %copy-start.15 = (bf16[8,48,576]{2,1,0:T(8,128)(2,1)}, bf16[8,48,576]{2,1,0:T(8,128)(2,1)S(1)}, u32[]{:S(2)}) copy-start(bf16[8,48,576]{2,1,0:T(8,128)(2,1)S(1)} %get-tuple-element.87.ins) | copy-start | bytes 1327108
  459.3 3.9 copy-start.19
  459.3 3.9 copy-start.21
  459.3 3.9 copy-start.22
  459.3 3.9 copy-start.24
  465.6 27.3 %copy-start.29 = (f32[2,48]{1,0:T(2,128)S(1)}, f32[2,48]{1,0:T(2,128)}, u32[]{:S(2)}) copy-start(f32[2,48]{1,0:T(2,128)} %param.22) | copy-start | bytes 1156
  465.6 28.7 %copy-start.27 = (f32[3,48]{1,0:T(4,128)S(1)}, f32[3,48]{1,0:T(4,128)}, u32[]{:S(2)}) copy-start(f32[3,48]{1,0:T(4,128)} %param.24) | copy-start | bytes 1732
  465.6 28.7 %copy-start.31 = (f32[3,48]{1,0:T(4,128)S(1)}, f32[3,48]{1,0:T(4,128)}, u32[]{:S(2)}) copy-start(f32[3,48]{1,0:T(4,128)} %param.30) | copy-start | bytes 1732
  465.6 28.7 %copy-start.32 = (f32[3,48]{1,0:T(4,128)S(1)}, f32[3,48]{1,0:T(4,128)}, u32[]{:S(2)}) copy-start(f32[3,48]{1,0:T(4,128)} %param.36) | copy-start | bytes 1732
  465.6 37.1 %copy-start.2 = (f32[2,48,6912]{2,1,0:T(8,128)S(1)}, f32[2,48,6912]{2,1,0:T(8,128)}, u32[]{:S(2)}) copy-start(f32[2,48,6912]{2,1,0:T(8,128)} %first.3) | copy-start | bytes 7962628
  492.9 5.1 copy-start.7
  495.5 7.2 %copy-start.4 = (bf16[8,2,48,864]{3,2,1,0:T(8,128)(2,1)S(1)}, bf16[8,2,48,864]{3,2,1,0:T(8,128)(2,1)}, u32[]{:S(2)}) copy-start(bf16[8,2,48,864]{3,2,1,0:T(8,128)(2,1)} %get-tuple-element.99.got) | copy-start | bytes 3981316
  500.1 2.6 copy-start.1
  502.7 1.8 copy-start.3
  504.5 5.2 %copy-start.20 = (f32[2,192,1536]{2,1,0:T(8,128)S(1)}, f32[2,192,1536]{2,1,0:T(8,128)}, u32[]{:S(2)}) copy-start(f32[2,192,1536]{2,1,0:T(8,128)} %get-tuple-element.142) | copy-start | bytes 7077892
  (13 other events, 13.5 us)
Sparse Core Ops, SparseCore 0:
  10.2 43.1 all-gather.6
  87.0 102.4 all-gather.4
  251.8 52.8 reduce-scatter.2
  317.9 103.1 reduce-scatter.4
